TPU v7x, 128 devices: a whole 4x4x4 slice. The times are simulated.
128 devices in a mesh: row: 8 (over x, core), col: 16 (over z, y).
Axes of the slice: x: 4, y: 4, z: 4, core: 2. Of those that a mesh axis runs over, the one named last changes fastest.
Arguments:
- features: bfloat16 [524288, 512], P(('row', 'col')), may hold values from -6 to 6
- w_first: bfloat16 [1024, 512], replicated, may hold values from -0.1875 to 0.1875
- w_second: bfloat16 [1024, 512], replicated, may hold values from -0.1875 to 0.1875
- send_rows: int32 [128, 8, 256], P(('row', 'col')), may hold values from 0 to 4095
- halo_count: int32 [128, 8], P(('row', 'col')), may hold values from 0 to 256, as said below
- hub_owner: int32 [8, 2048, 1], P('row'), may hold values from 0 to 15; in each aligned block of 2048 rows (0 to 2047, 2048 to 4095, ..., all dimensions but the last counted through in order) at most 384 rows name the same one
- hub_row: int32 [8, 2048], P('row'), may hold values from 0 to 4095
- local_cols: int32 [128, 32, 2], P(('row', 'col')), may hold values from 0 to 31
- local_tiles: bfloat16 [128, 32, 2, 128, 128], P(('row', 'col')), may hold values from 0 to 1, as said below
- remote_cols: int32 [128, 32, 2], P(('row', 'col')), may hold values from 0 to 31, as said below
- remote_tiles: bfloat16 [128, 32, 2, 128, 128], P(('row', 'col')), may hold values from 0 to 1
Outputs:
- embeddings: bfloat16 [524288, 512], P(('row', 'col'))
Inputs may be any that keep to these rules, and one draw needn't show every extreme that they name: `halo_count`: zero where p is d's own row index; some entry equals 256. `hub_owner`: in each row of partitions no owner holds more than 384 hubs, and some owner holds exactly 384. `remote_cols`: each partition's tiles name every block of its remote store at least once. The diagonal of local_tiles[d, b, 0] lies in 0.5 to 1.
All inputs are finite; a program needn't handle non-finite values.
Results may differ from a plain program's by a relative error of at most 0.005.
Values may be sent and summed in bfloat16 or wider, within the bound.
No kernel may reach another device: no remote copies, remote signals or barrier semaphores. Data moves between devices by JAX's collectives and lax.ppermute only.
A program may use at most 128 MiB of HBM per device.

v0:
```python
import jax
import jax.numpy as jnp
from jax import lax
from jax.sharding import PartitionSpec as P


def gather_hubs(current, slot_rows, positions):
    packed = current[slot_rows]
    gathered = lax.all_gather(packed, "col", axis=0, tiled=True)
    return gathered[positions]


def chooser_table(index, count):
    return (index[:, :, None] == jnp.arange(count, dtype=jnp.int32)[None, None, :]).astype(
        jnp.bfloat16
    )


def pick_blocks(chooser, blocks):
    return jnp.einsum("btc,cjf->btjf", chooser, blocks, preferred_element_type=jnp.bfloat16)


def on_device(
    features,
    w_first,
    w_second,
    send_rows,
    halo_count,
    hub_owner,
    hub_row,
    local_cols,
    local_tiles,
    remote_cols,
    remote_tiles,
):
    feat_width = features.shape[1]
    col_count = lax.axis_size("col")
    my_col = lax.axis_index("col")
    rows_sent = send_rows[0]
    halo_cap = rows_sent.shape[1]
    keep_mask = jnp.arange(halo_cap, dtype=jnp.int32)[None, :] < halo_count[0][:, None]
    owners = hub_owner[0, :, 0]
    places = hub_row[0]
    hub_total = owners.shape[0]
    hub_cap = 3 * hub_total // col_count
    onehot = (owners[:, None] == jnp.arange(col_count, dtype=jnp.int32)[None, :]).astype(jnp.int32)
    hub_ranks = jnp.sum(jnp.cumsum(onehot, axis=0) * onehot, axis=1) - 1
    positions = owners * hub_cap + hub_ranks
    mine_mask = owners == my_col
    target = jnp.where(mine_mask, hub_ranks, hub_cap)
    slot_rows = jnp.zeros((hub_cap + 1,), jnp.int32).at[target].set(places)[:hub_cap]
    local_vals = local_tiles[0]
    remote_vals = remote_tiles[0]
    tile_size = local_vals.shape[-1]
    block_count = local_vals.shape[0]
    remote_count = (halo_count.shape[1] * halo_cap + hub_total) // tile_size
    local_chooser = chooser_table(local_cols[0], block_count)
    remote_chooser = chooser_table(remote_cols[0], remote_count)
    local_weight = jnp.sum(local_vals, axis=(1, 3), dtype=jnp.float32)
    current = features
    denominator = local_weight
    for layer_index, weight in enumerate((w_first, w_second)):
        outgoing = jnp.where(keep_mask[:, :, None], current[rows_sent], jnp.zeros((), jnp.bfloat16))
        if layer_index == 0:
            halo_rows, halo_marks = (
                lax.all_to_all(outgoing, "row", split_axis=0, concat_axis=0, tiled=True),
                lax.all_to_all(
                    keep_mask.astype(jnp.bfloat16), "row", split_axis=0, concat_axis=0, tiled=True
                ),
            )
            mark_vals = jnp.concatenate(
                [halo_marks.reshape(-1), jnp.ones((hub_total,), jnp.bfloat16)]
            )
            mark_blocks = mark_vals.reshape(-1, tile_size)
            picked_marks = jnp.einsum(
                "btc,cj->btj", remote_chooser, mark_blocks, preferred_element_type=jnp.bfloat16
            )
            denominator = local_weight + jnp.einsum(
                "btij,btj->bi", remote_vals, picked_marks, preferred_element_type=jnp.float32
            )
        else:
            halo_rows = lax.all_to_all(outgoing, "row", split_axis=0, concat_axis=0, tiled=True)
        hub_feats = gather_hubs(current, slot_rows, positions)
        remote = jnp.concatenate([halo_rows.reshape(-1, feat_width), hub_feats], axis=0).reshape(
            -1, tile_size, feat_width
        )
        own_blocks = current.reshape(block_count, tile_size, feat_width)
        summed = jnp.einsum(
            "btij,btjf->bif",
            local_vals,
            pick_blocks(local_chooser, own_blocks),
            preferred_element_type=jnp.float32,
        )
        summed = summed + jnp.einsum(
            "btij,btjf->bif",
            remote_vals,
            pick_blocks(remote_chooser, remote),
            preferred_element_type=jnp.float32,
        )
        averaged = (summed / denominator[:, :, None]).astype(jnp.bfloat16).reshape(-1, feat_width)
        preact = jnp.dot(current, weight[:feat_width], preferred_element_type=jnp.float32)
        preact = preact + jnp.dot(averaged, weight[feat_width:], preferred_element_type=jnp.float32)
        activated = jnp.maximum(preact, 0.0)
        current = (
            activated * lax.rsqrt(jnp.mean(activated * activated, axis=-1, keepdims=True) + 1e-05)
        ).astype(jnp.bfloat16)
    return current


def solution(mesh):
    in_specs = (
        P(("row", "col"), None),
        P(),
        P(),
        P(("row", "col"), None, None),
        P(("row", "col"), None),
        P("row", None, None),
        P("row", None),
        P(("row", "col"), None, None),
        P(("row", "col"), None, None, None, None),
        P(("row", "col"), None, None),
        P(("row", "col"), None, None, None, None),
    )
    out_specs = P(("row", "col"), None)
    return jax.shard_map(
        on_device, mesh=mesh, in_specs=in_specs, out_specs=out_specs, check_vma=False
    )
```

profile of v0, /device:TPU:6, one launch (start us, length us, event | category | flops | bytes accessed | tf_op | source)
XLA Modules:
  0.0 280.3 jit_solution(6219670113621919360)
XLA Ops:
  6.6 0.9 fusion.46
  7.4 4.5 %reduce-window.6 = s32[16,16,128]{2,1,0:T(8,128)S(1)} reduce-window(s32[16,16,128]{2,1,0:T(8,128)S(1)} %fusion.46, s32[]{:T(128)} %constant.12.clone.1), window={size=1x1x128 pad=0_0x0_0x127_0}, to_apply=%region_0.0 | reduce-window | flops 4161536 | bytes 262148 | tf_op jit(solution)/shard_map/reduce-window
  12.0 0.4 slice_reduce_fusion
  12.4 0.2 reduce-window.9
  12.6 0.1 broadcast_add_fusion
  12.7 0.8 fusion.45
  13.4 0.7 compare_select_fusion
  14.2 8.2 %scatter_custom_fusion = s32[385]{0:T(512)S(1)} fusion(s32[2048]{0:T(1024)S(1)} %bitcast.155, s32[2048]{0:T(1024)} %bitcast.159, s32[]{:T(128)} %constant.12.clone.1), kind=kCustom, calls=%fused_computation.92 | custom fusion | bytes 2052 | tf_op jit(solution)/shard_map/scatter | solution.py:51
  22.4 5.3 %gather_fusion.1 = bf16[384,512]{1,0:T(8,128)(2,1)} fusion(bf16[4096,512]{1,0:T(8,128)(2,1)} %param.11, s32[1024]{0:T(1024)S(1)} %pad_clamp_fusion), kind=kCustom, calls=%fused_computation.1 | custom fusion | bytes 787968 | tf_op jit(solution)/shard_map/gather | solution.py:8
  27.7 0.0 all-gather.5.cloned.1.call-update
  27.8 0.1 compare_convert_fusion
  27.9 0.5 broadcast.229
  28.4 0.7 reduce.3
  29.0 0.6 reshape.312
  29.6 4.8 %all-to-all-start.1 = ((bf16[8,2,128]{2,1,0:T(2,128)(2,1)}), bf16[8,2,128]{2,1,0:T(2,128)(2,1)S(1)}, u32[]{:S(2)}, u32[]{:S(2)}) async-start(bf16[8,2,128]{2,1,0:T(2,128)(2,1)} %reshape.312), calls=%async_computation.1 | async-start | bytes 8192 | tf_op jit(solution)/shard_map/all_to_all | solution.py:67
  34.5 12.0 %gather_fusion = bf16[2048,512]{1,0:T(8,128)(2,1)} fusion(bf16[4096,512]{1,0:T(8,128)(2,1)} %param.11, s32[2048]{0:T(1024)S(1)} %broadcast_clamp_fusion.1), kind=kCustom, calls=%fused_computation | custom fusion | bytes 4202496 | tf_op jit(solution)/shard_map/gather | solution.py:63
  46.4 0.1 iota_compare_fusion.5
  46.5 2.8 %broadcast_select_fusion.1 = bf16[8,256,512]{2,1,0:T(8,128)(2,1)} fusion(bf16[8,256,512]{2,1,0:T(8,128)(2,1)} %bitcast.140, pred[8,256]{1,0:T(8,128)(4,1)S(1)} %iota_compare_fusion.5), kind=kLoop, calls=%fused_computation.49 | loop fusion | flops 1048576 | bytes 4196352 | tf_op jit(solution)/shard_map/jit(_where)/select_n | solution.py:63
  49.3 4.9 %all-to-all-start = ((bf16[8,256,512]{2,1,0:T(8,128)(2,1)}), bf16[8,256,512]{2,1,0:T(8,128)(2,1)}, u32[]{:S(2)}, u32[]{:S(2)}) async-start(bf16[8,256,512]{2,1,0:T(8,128)(2,1)} %broadcast_select_fusion.1), calls=%async_computation | async-start | bytes 4194304 | tf_op jit(solution)/shard_map/all_to_all | solution.py:66
  54.3 0.2 all-gather.7.cloned.1.call-start
  54.5 2.2 convert_reduce_fusion
  56.7 8.8 %fusion.18 = bf16[32,2,128,512]{3,0,2,1:T(8,128)(2,1)} fusion(bf16[32,128,512]{2,1,0:T(8,128)(2,1)} %bitcast.130, s32[32,2]{0,1:T(2,128)S(1)} %bitcast.150), kind=kOutput, calls=%fused_computation.35 | convolution fusion | flops 268437504 | bytes 12583168 | tf_op jit(solution)/shard_map/btc,cjf->btjf/dot_general | solution.py:20
  65.5 5.7 %fusion.42 = f32[4096,512]{1,0:T(8,128)} fusion(bf16[4096,512]{1,0:T(8,128)(2,1)S(1)} %copy-done.2, bf16[1024,512]{1,0:T(8,128)(2,1)S(1)} %copy-done.3), kind=kOutput, calls=%fused_computation.55 | convolution fusion | flops 2147483648 | bytes 13107200 | tf_op jit(solution)/shard_map/dot_general | solution.py:101
  71.3 0.2 convolution_bitcast_fusion
  71.5 0.6 fusion.25
  72.1 19.5 %all-gather.5.cloned.1.call-done = bf16[6144,512]{1,0:T(8,128)(2,1)} async-done(((bf16[384,512]{1,0:T(8,128)(2,1)}), bf16[6144,512]{1,0:T(8,128)(2,1)}) %all-gather.5.cloned.1.call-update) | async-done | bytes 6291472 | tf_op jit(solution)/shard_map/all_gather | solution.py:9
  91.6 13.0 %gather_fusion.2 = bf16[2048,512]{1,0:T(8,128)(2,1)} fusion(bf16[6144,512]{1,0:T(8,128)(2,1)} %all-gather.5.cloned.1.call-done, s32[2048]{0:T(1024)S(1)} %broadcast_clamp_fusion), kind=kCustom, calls=%fused_computation.2 | custom fusion | bytes 4202496 | tf_op jit(solution)/shard_map/gather | solution.py:10
  104.7 2.5 pad_maximum_fusion
  107.2 3.3 %fusion.16 = bf16[32,2,128,512]{3,0,2,1:T(8,128)(2,1)S(1)} fusion(bf16[32,128,512]{2,1,0:T(8,128)(2,1)S(1)} %bitcast.135, s32[32,2]{0,1:T(2,128)S(1)} %bitcast.153), kind=kOutput, calls=%fused_computation.33 | convolution fusion | flops 268437504 | bytes 12583168 | tf_op jit(solution)/shard_map/btc,cjf->btjf/dot_general | solution.py:20
  110.5 12.9 %fusion.8 = f32[32,512,128,1]{1,2,3,0:T(8,128)} fusion(bf16[32,2,128,512]{3,0,2,1:T(8,128)(2,1)S(1)} %fusion.16, bf16[1,32,2,128,128]{4,3,2,1,0:T(8,128)(2,1)S(1)} %copy-done), kind=kOutput, calls=%fused_computation.17 | convolution fusion | flops 1073741824 | bytes 18874368 | tf_op jit(solution)/shard_map/btij,btjf->bif/dot_general | solution.py:94
  123.4 17.9 %fusion.3 = bf16[32,512,128]{1,2,0:T(8,128)(2,1)} fusion(f32[32,512,128,1]{1,2,3,0:T(8,128)} %fusion.8, f32[32,128]{1,0:T(8,128)S(1)} %add.104, bf16[32,2,128,512]{3,0,2,1:T(8,128)(2,1)} %fusion.18, bf16[1,32,2,128,128]{4,3,2,1,0:T(8,128)(2,1)} %param.19), kind=kOutput, calls=%fused_computation.12 | convolution fusion | flops 1080033280 | bytes 23085056 | tf_op jit(solution)/shard_map/btij,btjf->bif/dot_general | solution.py:88
  141.3 5.6 %multiply_reduce_fusion.1 = (f32[4096]{0:T(1024)S(1)}, f32[4096,512]{1,0:T(8,128)S(1)}) fusion(f32[4096,512]{1,0:T(8,128)S(1)} %bitcast.132, bf16[4096,512]{1,0:T(8,128)(2,1)} %bitcast.138, bf16[1024,512]{1,0:T(8,128)(2,1)} %param.12), kind=kOutput, calls=%fused_computation.25 | convolution fusion | flops 2155868160 | bytes 21512192 | tf_op jit(solution)/shard_map/dot_general | solution.py:102
  147.0 2.4 multiply_convert_fusion.1
  149.4 5.3 %gather_fusion.4 = bf16[384,512]{1,0:T(8,128)(2,1)} fusion(bf16[4096,512]{1,0:T(8,128)(2,1)} %multiply_convert_fusion.1, s32[1024]{0:T(1024)S(1)} %pad_clamp_fusion), kind=kCustom, calls=%fused_computation.4 | custom fusion | bytes 787968 | tf_op jit(solution)/shard_map/gather | solution.py:8
  154.7 0.0 all-gather.7.cloned.1.call-update
  154.7 11.9 %gather_fusion.3 = bf16[2048,512]{1,0:T(8,128)(2,1)} fusion(bf16[4096,512]{1,0:T(8,128)(2,1)} %multiply_convert_fusion.1, s32[2048]{0:T(1024)S(1)} %broadcast_clamp_fusion.1), kind=kCustom, calls=%fused_computation.3 | custom fusion | bytes 4202496 | tf_op jit(solution)/shard_map/gather | solution.py:63
  166.6 2.8 broadcast_select_fusion
  169.4 4.8 %all-to-all-start.2 = ((bf16[8,256,512]{2,1,0:T(8,128)(2,1)}), bf16[8,256,512]{2,1,0:T(8,128)(2,1)}, u32[]{:S(2)}, u32[]{:S(2)}) async-start(bf16[8,256,512]{2,1,0:T(8,128)(2,1)} %broadcast_select_fusion), calls=%async_computation.2 | async-start | bytes 4194304 | tf_op jit(solution)/shard_map/all_to_all | solution.py:82
  174.3 8.9 %fusion.14 = bf16[32,2,128,512]{3,0,2,1:T(8,128)(2,1)} fusion(bf16[32,128,512]{2,1,0:T(8,128)(2,1)} %bitcast.129, s32[32,2]{0,1:T(2,128)S(1)} %bitcast.151), kind=kOutput, calls=%fused_computation.31 | convolution fusion | flops 268437504 | bytes 12583168 | tf_op jit(solution)/shard_map/btc,cjf->btjf/dot_general | solution.py:20
  183.1 5.7 %fusion.39 = f32[4096,512]{1,0:T(8,128)} fusion(bf16[4096,512]{1,0:T(8,128)(2,1)S(1)} %copy-done.1, bf16[1024,512]{1,0:T(8,128)(2,1)S(1)} %copy-done.4), kind=kOutput, calls=%fused_computation.52 | convolution fusion | flops 2147483648 | bytes 13107200 | tf_op jit(solution)/shard_map/dot_general | solution.py:101
  188.9 27.0 %all-gather.7.cloned.1.call-done = bf16[6144,512]{1,0:T(8,128)(2,1)} async-done(((bf16[384,512]{1,0:T(8,128)(2,1)}), bf16[6144,512]{1,0:T(8,128)(2,1)}) %all-gather.7.cloned.1.call-update) | async-done | bytes 6291472 | tf_op jit(solution)/shard_map/all_gather | solution.py:9
  215.8 13.2 %gather_fusion.5 = bf16[2048,512]{1,0:T(8,128)(2,1)} fusion(bf16[6144,512]{1,0:T(8,128)(2,1)} %all-gather.7.cloned.1.call-done, s32[2048]{0:T(1024)S(1)} %broadcast_clamp_fusion), kind=kCustom, calls=%fused_computation.5 | custom fusion | bytes 4202496 | tf_op jit(solution)/shard_map/gather | solution.py:10
  229.1 2.5 pad_maximum_fusion.1
  231.6 3.3 %fusion.12 = bf16[32,2,128,512]{3,0,2,1:T(8,128)(2,1)S(1)} fusion(bf16[32,128,512]{2,1,0:T(8,128)(2,1)S(1)} %bitcast.136, s32[32,2]{0,1:T(2,128)S(1)} %bitcast.154), kind=kOutput, calls=%fused_computation.29 | convolution fusion | flops 268437504 | bytes 12583168 | tf_op jit(solution)/shard_map/btc,cjf->btjf/dot_general | solution.py:20
  234.9 12.7 %fusion.4 = f32[32,512,128,1]{1,2,3,0:T(8,128)} fusion(bf16[32,2,128,512]{3,0,2,1:T(8,128)(2,1)S(1)} %fusion.12, bf16[1,32,2,128,128]{4,3,2,1,0:T(8,128)(2,1)S(1)} %copy-done), kind=kOutput, calls=%fused_computation.13 | convolution fusion | flops 1073741824 | bytes 18874368 | tf_op jit(solution)/shard_map/btij,btjf->bif/dot_general | solution.py:94
  247.6 17.9 %fusion.1 = bf16[32,512,128]{1,2,0:T(8,128)(2,1)} fusion(f32[32,512,128,1]{1,2,3,0:T(8,128)} %fusion.4, f32[32,128]{1,0:T(8,128)S(1)} %add.104, bf16[32,2,128,512]{3,0,2,1:T(8,128)(2,1)} %fusion.14, bf16[1,32,2,128,128]{4,3,2,1,0:T(8,128)(2,1)} %param.19), kind=kOutput, calls=%fused_computation.9 | convolution fusion | flops 1080033280 | bytes 23085056 | tf_op jit(solution)/shard_map/btij,btjf->bif/dot_general | solution.py:88
  265.5 5.4 %multiply_reduce_fusion = (f32[4096]{0:T(1024)S(1)}, f32[4096,512]{1,0:T(8,128)S(1)}) fusion(f32[4096,512]{1,0:T(8,128)S(1)} %bitcast.134, bf16[4096,512]{1,0:T(8,128)(2,1)} %bitcast.137, bf16[1024,512]{1,0:T(8,128)(2,1)} %param.13), kind=kOutput, calls=%fused_computation.22 | convolution fusion | flops 2155868160 | bytes 21512192 | tf_op jit(solution)/shard_map/dot_general | solution.py:102
  270.9 2.4 multiply_convert_fusion
  (45 shorter events, 0.2 us)
Async XLA Ops:
  6.5 64.9 %copy-start = (bf16[1,32,2,128,128]{4,3,2,1,0:T(8,128)(2,1)S(1)}, bf16[1,32,2,128,128]{4,3,2,1,0:T(8,128)(2,1)}, u32[]{:S(2)}) copy-start(bf16[1,32,2,128,128]{4,3,2,1,0:T(8,128)(2,1)} %param.21) | copy-start | bytes 6291460
  6.5 21.2 %copy-start.8 = (s32[1,8]{1,0:T(1,128)S(1)}, s32[1,8]{1,0:T(1,128)}, u32[]{:S(2)}) copy-start(s32[1,8]{1,0:T(1,128)} %param.15) | copy-start | bytes 100
  6.5 27.9 %copy-start.7 = (s32[1,8,256]{2,1,0:T(8,128)S(1)}, s32[1,8,256]{2,1,0:T(8,128)}, u32[]{:S(2)}) copy-start(s32[1,8,256]{2,1,0:T(8,128)} %param.14) | copy-start | bytes 24580
  6.5 85.1 %all-gather.5.cloned.1.call-start = ((), (), s32[]{:S(2)}) async-start(), calls=%async_computation.3 | async-start | bytes 6684672 | tf_op jit(solution)/shard_map/all_gather | solution.py:9
  29.6 19.7 %all-to-all-start.1 = ((bf16[8,2,128]{2,1,0:T(2,128)(2,1)}), bf16[8,2,128]{2,1,0:T(2,128)(2,1)S(1)}, u32[]{:S(2)}, u32[]{:S(2)}) async-start(bf16[8,2,128]{2,1,0:T(2,128)(2,1)} %reshape.312), calls=%async_computation.1 | async-start | bytes 8192 | tf_op jit(solution)/shard_map/all_to_all | solution.py:67
  49.3 7.3 %copy-start.5 = (s32[1,32,2]{1,2,0:T(2,128)S(1)}, s32[1,32,2]{1,2,0:T(2,128)}, u32[]{:S(2)}) copy-start(s32[1,32,2]{1,2,0:T(2,128)} %param.18) | copy-start | bytes 772
  49.3 55.3 %all-to-all-start = ((bf16[8,256,512]{2,1,0:T(8,128)(2,1)}), bf16[8,256,512]{2,1,0:T(8,128)(2,1)}, u32[]{:S(2)}, u32[]{:S(2)}) async-start(bf16[8,256,512]{2,1,0:T(8,128)(2,1)} %broadcast_select_fusion.1), calls=%async_computation | async-start | bytes 4194304 | tf_op jit(solution)/shard_map/all_to_all | solution.py:66
  54.3 161.6 %all-gather.7.cloned.1.call-start = ((), (), s32[]{:S(2)}) async-start(), calls=%async_computation.4 | async-start | bytes 6684672 | tf_op jit(solution)/shard_map/all_gather | solution.py:9
  56.7 8.8 %copy-start.2 = (bf16[4096,512]{1,0:T(8,128)(2,1)S(1)}, bf16[4096,512]{1,0:T(8,128)(2,1)}, u32[]{:S(2)}) copy-start(bf16[4096,512]{1,0:T(8,128)(2,1)} %param.11) | copy-start | bytes 12582916
  56.7 8.8 %copy-start.3 = (bf16[1024,512]{1,0:T(8,128)(2,1)S(1)}, bf16[1024,512]{1,0:T(8,128)(2,1)}, u32[]{:S(2)}) copy-start(bf16[1024,512]{1,0:T(8,128)(2,1)} %param.12) | copy-start | bytes 3145732
  65.5 5.7 %copy-start.6 = (s32[1,32,2]{1,2,0:T(2,128)S(1)}, s32[1,32,2]{1,2,0:T(2,128)}, u32[]{:S(2)}) copy-start(s32[1,32,2]{1,2,0:T(2,128)} %param.20) | copy-start | bytes 772
  110.5 30.9 %slice-start = ((s8[8388608]{0:T(1024)(128)(4,1)}), s8[4194304]{0:T(1024)(128)(4,1)S(1)}, s32[]{:S(2)}) async-start(s8[8388608]{0:T(1024)(128)(4,1)} %bitcast.131), calls=%async_computation.5 | async-start | bytes 8388608
  123.4 17.9 %slice-start.1 = ((s8[8388608]{0:T(1024)(128)(4,1)}), s8[4194304]{0:T(1024)(128)(4,1)S(1)}, s32[]{:S(2)}) async-start(s8[8388608]{0:T(1024)(128)(4,1)} %bitcast.131), calls=%async_computation.6 | async-start | bytes 8388608
  169.4 59.7 %all-to-all-start.2 = ((bf16[8,256,512]{2,1,0:T(8,128)(2,1)}), bf16[8,256,512]{2,1,0:T(8,128)(2,1)}, u32[]{:S(2)}, u32[]{:S(2)}) async-start(bf16[8,256,512]{2,1,0:T(8,128)(2,1)} %broadcast_select_fusion), calls=%async_computation.2 | async-start | bytes 4194304 | tf_op jit(solution)/shard_map/all_to_all | solution.py:82
  174.2 8.9 %copy-start.1 = (bf16[4096,512]{1,0:T(8,128)(2,1)S(1)}, bf16[4096,512]{1,0:T(8,128)(2,1)}, u32[]{:S(2)}) copy-start(bf16[4096,512]{1,0:T(8,128)(2,1)} %multiply_convert_fusion.1) | copy-start | bytes 12582916
  174.2 8.9 %copy-start.4 = (bf16[1024,512]{1,0:T(8,128)(2,1)S(1)}, bf16[1024,512]{1,0:T(8,128)(2,1)}, u32[]{:S(2)}) copy-start(bf16[1024,512]{1,0:T(8,128)(2,1)} %param.13) | copy-start | bytes 3145732
  234.9 30.7 %slice-start.2 = ((s8[8388608]{0:T(1024)(128)(4,1)}), s8[4194304]{0:T(1024)(128)(4,1)S(1)}, s32[]{:S(2)}) async-start(s8[8388608]{0:T(1024)(128)(4,1)} %bitcast.133), calls=%async_computation.7 | async-start | bytes 8388608
  247.6 17.9 %slice-start.3 = ((s8[8388608]{0:T(1024)(128)(4,1)}), s8[4194304]{0:T(1024)(128)(4,1)S(1)}, s32[]{:S(2)}) async-start(s8[8388608]{0:T(1024)(128)(4,1)} %bitcast.133), calls=%async_computation.8 | async-start | bytes 8388608
Sparse Core Ops, SparseCore 0:
  27.9 63.7 all-gather.4
  154.8 60.9 all-gather.6
where the time goes:
time: 286 us; the launch traced here: 280 us
  matrix products  109 us (38%)
  local copies, waits for them, and re-layouts  70.7 us (25%)
  waiting for transfers between devices  46.5 us (16%)
  other arithmetic  25.6 us (9%)
  starting transfers between devices  14.7 us (5%)
  between operations  13.8 us (5%)
    all_gather x2, waiting for transfers between devices, gather_hubs(): gathered = lax.all_gather(packed, 'col', axis=0, tiled=True)  46.5 us
    dot_general x2, matrix products, on_device(): jnp.einsum('btij,btjf->bif', local_vals, pick_blocks(local_chooser, own_b...  35.9 us
    gather x2, local copies, waits for them, and re-layouts, gather_hubs(): return gathered[positions]  26.3 us
    dot_general x2, matrix products, on_device(): jnp.einsum('btij,btjf->bif', remote_vals, pick_blocks(remote_chooser, rem...  25.6 us
    dot_general x4, matrix products, pick_blocks(): jnp.einsum('btc,cjf->btjf', chooser, blocks, preferred_element_type=jnp.b...  24.2 us
    gather x2, local copies, waits for them, and re-layouts, on_device(): current[rows_sent]  23.9 us
    dot_general x2, matrix products, on_device(): jnp.dot(current, weight[:feat_width], preferred_element_type=jnp.float32)  11.4 us
    dot_general x2, matrix products, on_device(): jnp.dot(averaged, weight[feat_width:], preferred_element_type=jnp.float32)  11 us
  transfers between devices with their start and end apart: 5, of which 2 were waited for; matrix products, arithmetic and copies ran while one was open for 32% of the time, Pallas kernels for 0%

commit v1 on v0

v1 whole, which is shorter than its diff:
```python
import functools

import jax
import jax.numpy as jnp
from jax import lax
from jax.experimental import pallas as pl
from jax.experimental.pallas import tpu as pltpu
from jax.sharding import PartitionSpec as P

F32 = jnp.float32
BF16 = jnp.bfloat16
I32 = jnp.int32
VMEM_LIMIT = 58 * 1024 * 1024
TB = 128
ROWS = 8
COLS = 16
SIDE = 4
HALO = 256
NOTE = 16
HUBS = 2048
HUB_CAP = 384
TALL = 512


def params():
    return pltpu.CompilerParams(vmem_limit_bytes=VMEM_LIMIT)


def cost():
    return pl.CostEstimate(flops=1000, bytes_accessed=1000, transcendentals=0)


def vmem():
    return pl.BlockSpec(memory_space=pltpu.VMEM)


def smem():
    return pl.BlockSpec(memory_space=pltpu.SMEM)


def hbm():
    return pl.BlockSpec(memory_space=pl.ANY)


def whole(*shape):
    return pl.BlockSpec(shape, lambda i: (0,) * len(shape))


def band(tall, *rest):
    return pl.BlockSpec((tall, *rest), lambda i: (i,) + (0,) * len(rest))


def shape(dtype, *dims):
    return jax.ShapeDtypeStruct(dims, dtype)


def iota(dims, dim):
    return lax.broadcasted_iota(I32, dims, dim)


def widen(rows, wide, first):
    lanes = rows.shape[1] // TB
    for j in range(lanes):
        wide[pl.ds(first * lanes + j, rows.shape[0], stride=lanes), :] = rows[:, j * TB : (j + 1) * TB]


def move_row(source, row, target, slot):
    lanes = 4
    target[pl.ds(pl.multiple_of(slot * lanes, lanes), lanes), :] = source[
        pl.ds(pl.multiple_of(row * lanes, lanes), lanes), :
    ]


def write_index(my_col, owner, rows, send_ref, pos_ref):
    chunks = HUBS // TB
    owner_id = iota((COLS, TB), 0)
    masks = [jnp.where(owner[:, c * TB : (c + 1) * TB] == owner_id, 1.0, 0.0) for c in range(chunks)]
    earlier = jnp.where(iota((TB, TB), 0) < iota((TB, TB), 1), 1.0, 0.0).astype(BF16)
    inside = jnp.dot(jnp.concatenate(masks, axis=0).astype(BF16), earlier, preferred_element_type=F32)
    running = jnp.zeros((COLS, 1), F32)
    ranks = []
    for c in range(chunks):
        rank = inside[c * COLS : (c + 1) * COLS, :] + running
        ranks.append(jnp.sum(masks[c] * rank, axis=0, keepdims=True))
        running = running + jnp.sum(masks[c], axis=1, keepdims=True)
    rank = jnp.concatenate(ranks, axis=0).astype(I32)
    who = jnp.concatenate([owner[:, c * TB : (c + 1) * TB] for c in range(chunks)], axis=0)
    local = jnp.concatenate([rows[:, c * TB : (c + 1) * TB] for c in range(chunks)], axis=0).astype(F32)
    slot = jnp.where(who == my_col, rank, -1)
    for k in range(HUB_CAP // TB):
        wanted = iota((TB, TB), 0) + k * TB
        total = jnp.zeros((TB, TB), F32)
        for c in range(chunks):
            total = total + jnp.where(slot[c : c + 1, :] == wanted, local[c : c + 1, :], 0.0)
        send_ref[k * TB : (k + 1) * TB, :] = jnp.sum(total, axis=1, keepdims=True).astype(I32)
    pos_ref[0:chunks, :] = who * HUB_CAP + rank
    held = jnp.concatenate([jnp.broadcast_to(running, (COLS, TB)), jnp.zeros((TB - COLS, TB), F32)], axis=0)
    pos_ref[chunks : chunks + 8, :] = held.T[0:8, :].astype(I32)


def add_picked(step, send_ref, rows, total):
    wanted = send_ref[...] - step * TALL
    chosen = jnp.where(wanted == iota((HUB_CAP, TALL), 1), 1.0, 0.0).astype(BF16)
    part = jnp.dot(chosen, rows, preferred_element_type=F32)

    @pl.when(step == 0)
    def _():
        total[...] = part

    @pl.when(step > 0)
    def _():
        total[...] = total[...] + part


def hub_kernel(place_ref, owner_ref, row_ref, table_ref, out_ref, send_ref, pos_ref, total):
    step = pl.program_id(0)

    @pl.when(step == 0)
    def _():
        write_index(place_ref[1], owner_ref[...], row_ref[...], send_ref, pos_ref)

    add_picked(step, send_ref, table_ref[...], total)

    @pl.when(step == pl.num_programs(0) - 1)
    def _():
        out_ref[...] = total[...].astype(BF16)


def hub_start(place, owner, rows, table):
    nodes, width = table.shape
    listed = HUBS // TB + 8
    return pl.pallas_call(
        hub_kernel,
        grid=(nodes // TALL,),
        in_specs=[smem(), whole(1, HUBS), whole(1, HUBS), band(TALL, width)],
        out_specs=[whole(HUB_CAP, width), whole(HUB_CAP, 1), whole(listed, TB)],
        out_shape=[shape(BF16, HUB_CAP, width), shape(I32, HUB_CAP, 1), shape(I32, listed, TB)],
        scratch_shapes=[pltpu.VMEM((HUB_CAP, width), F32)],
        compiler_params=params(),
        cost_estimate=cost(),
        name="hub_start",
    )(place, owner, rows, table)


def write_halos(noted, rows_ref, count_ref, wide, picked, out):
    lanes = 4
    unroll = 16
    height = HALO + (NOTE if noted else 0)
    for peer in range(ROWS):
        count = count_ref[peer]

        @pl.loop(0, (count + unroll - 1) // unroll)
        def _(group):
            for u in range(unroll):
                slot = group * unroll + u
                move_row(wide, rows_ref[peer * HALO + slot], picked, slot)

        for half in range(HALO // TB):
            live = iota((TB, TB), 0) + half * TB < count
            top = peer * height + half * TB
            for j in range(lanes):
                part = picked[pl.ds(half * TB * lanes + j, TB, stride=lanes), :]
                out[top : top + TB, j * TB : (j + 1) * TB] = jnp.where(live, part, 0.0).astype(BF16)
        if noted:
            top = peer * height + HALO
            out[top : top + NOTE, :] = jnp.full((NOTE, lanes * TB), count, I32).astype(F32).astype(BF16)


def halo_kernel(noted, rows_ref, count_ref, table_ref, out_ref, wide, picked):
    step = pl.program_id(0)
    widen(table_ref[...].astype(F32), wide, step * TALL)

    @pl.when(step == pl.num_programs(0) - 1)
    def _():
        write_halos(noted, rows_ref, count_ref, wide, picked, out_ref)


def halo_start(noted, rows, count, table):
    nodes, width = table.shape
    height = ROWS * (HALO + (NOTE if noted else 0))
    return pl.pallas_call(
        functools.partial(halo_kernel, noted),
        grid=(nodes // TALL,),
        in_specs=[smem(), smem(), band(TALL, width)],
        out_specs=whole(height, width),
        out_shape=shape(BF16, height, width),
        scratch_shapes=[pltpu.VMEM((nodes * width // TB, TB), F32), pltpu.VMEM((HALO * width // TB, TB), F32)],
        compiler_params=params(),
        cost_estimate=cost(),
        name="halo_start",
    )(rows, count, table)


def near_kernel(
    weighed, place_ref, cols_ref, far_ref, table_ref, halo_ref, tiles_ref, far_tiles_ref, weight_ref, *rest
):
    if weighed:
        near_ref, inverse_ref, averaged = rest
    else:
        inverse_ref, near_ref, averaged = rest
    step = pl.program_id(0)
    group = tiles_ref.shape[0]
    width = table_ref.shape[1]
    my_row = place_ref[0]
    height = halo_ref.shape[0] // ROWS
    for b in range(group):
        at = (step * group + b) * 2
        rights = []
        for t in range(2):
            rights.append(table_ref[pl.ds(pl.multiple_of(cols_ref[at + t] * TB, TB), TB), :])
        blocks = [far_ref[at + t] for t in range(2)]
        for block in blocks:
            top = jnp.where(
                block < 2 * ROWS, lax.div(block, 2) * height + lax.rem(block, 2) * TB, my_row * height
            )
            rights.append(halo_ref[pl.ds(pl.multiple_of(top, 16), TB), :])
        left = jnp.concatenate([tiles_ref[b, 0], tiles_ref[b, 1], far_tiles_ref[b, 0], far_tiles_ref[b, 1]], axis=1)
        total = jnp.dot(left, jnp.concatenate(rights, axis=0), preferred_element_type=F32)
        if weighed:
            mass = tiles_ref[b, 0].astype(F32) + tiles_ref[b, 1].astype(F32)
            for t in range(2):
                top = pl.multiple_of(lax.rem(lax.div(blocks[t], 2), ROWS) * height + HALO, 16)
                noted = halo_ref[pl.ds(top, NOTE), 0:TB].astype(F32)[0:1, :]
                is_hub = jnp.where(blocks[t] < 2 * ROWS, 0.0, 1024.0)
                slots = (iota((1, TB), 1) + lax.rem(blocks[t], 2) * TB).astype(F32)
                mass = mass + jnp.where(slots < noted + is_hub, far_tiles_ref[b, t].astype(F32), 0.0)
            inverse = 1.0 / jnp.sum(mass, axis=1, keepdims=True)
            inverse_ref[b * TB : (b + 1) * TB, :] = inverse
        else:
            inverse = inverse_ref[b * TB : (b + 1) * TB, :]
        averaged[b * TB : (b + 1) * TB, :] = (total * inverse).astype(BF16)
    own = table_ref[pl.ds(pl.multiple_of(step * TALL, TALL), TALL), :]
    near_ref[...] = jnp.dot(own, weight_ref[0:width, :], preferred_element_type=F32) + jnp.dot(
        averaged[...], weight_ref[width : 2 * width, :], preferred_element_type=F32
    )


def near_part(weighed, place, cols, far_cols, table, halos, tiles, far_tiles, weight, inverse=None):
    nodes, width = table.shape
    group = TALL // TB
    in_specs = [
        smem(),
        smem(),
        smem(),
        whole(nodes, width),
        whole(*halos.shape),
        band(group, 2, TB, TB),
        band(group, 2, TB, TB),
        whole(*weight.shape),
    ]
    args = [place, cols, far_cols, table, halos, tiles, far_tiles, weight]
    out_specs = [band(TALL, width)]
    out_shape = [shape(F32, nodes, width)]
    if weighed:
        out_specs.append(band(TALL, 1))
        out_shape.append(shape(F32, nodes, 1))
    else:
        in_specs.append(band(TALL, 1))
        args.append(inverse)
    return pl.pallas_call(
        functools.partial(near_kernel, weighed),
        grid=(nodes // TALL,),
        in_specs=in_specs,
        out_specs=out_specs,
        out_shape=out_shape,
        scratch_shapes=[pltpu.VMEM((TALL, width), BF16)],
        compiler_params=params(),
        cost_estimate=cost(),
        name="near_part",
    )(*args)


def tail_kernel(last, *refs):
    cols_ref, pos_ref, hubs_ref, tiles_ref, near_ref, weight_ref, inverse_ref = refs[:7]
    rest = refs[7:]
    if last:
        out_ref, held, wide, placed, store, averaged, sem = rest
    else:
        send_ref, out_ref, picked_ref, held, wide, placed, store, averaged, sem, total = rest
    step = pl.program_id(0)
    group = tiles_ref.shape[0]
    lanes = 4

    @pl.when(step == 0)
    def _():
        copies = []
        for owner in range(COLS):
            span = pl.ds(owner * HUB_CAP, HUB_CAP)
            copies.append(pltpu.make_async_copy(hubs_ref.at[span], held.at[span], sem.at[owner]))
        for copy in copies:
            copy.start()
        store[HUBS : HUBS + TB, :] = jnp.zeros((TB, lanes * TB), BF16)
        for owner in range(COLS):
            copies[owner].wait()
            chunk = 32

            @pl.loop(0, (pos_ref[HUBS + owner] + chunk - 1) // chunk)
            def _(n):
                top = pl.multiple_of(owner * HUB_CAP + n * chunk, chunk)
                widen(held[pl.ds(top, chunk), :].astype(F32), wide, top)

        unroll = 16

        @pl.loop(0, HUBS // unroll)
        def _(n):
            for u in range(unroll):
                slot = n * unroll + u
                move_row(wide, pos_ref[slot], placed, slot)

        for j in range(lanes):
            store[0:HUBS, j * TB : (j + 1) * TB] = placed[pl.ds(j, HUBS, stride=lanes), :].astype(BF16)

    for b in range(group):
        rights = []
        for t in range(2):
            block = cols_ref[(step * group + b) * 2 + t]
            top = jnp.where(block < 2 * ROWS, HUBS, (block - 2 * ROWS) * TB)
            rights.append(store[pl.ds(pl.multiple_of(top, TB), TB), :])
        left = jnp.concatenate([tiles_ref[b, 0], tiles_ref[b, 1]], axis=1)
        far = jnp.dot(left, jnp.concatenate(rights, axis=0), preferred_element_type=F32)
        averaged[b * TB : (b + 1) * TB, :] = (far * inverse_ref[b * TB : (b + 1) * TB, :]).astype(BF16)
    preact = near_ref[...] + jnp.dot(averaged[...], weight_ref[...], preferred_element_type=F32)
    active = jnp.maximum(preact, 0.0)
    scale = lax.rsqrt(jnp.mean(active * active, axis=1, keepdims=True) + 1e-05)
    result = (active * scale).astype(BF16)
    out_ref[...] = result
    if not last:
        add_picked(step, send_ref, result, total)

        @pl.when(step == pl.num_programs(0) - 1)
        def _():
            picked_ref[...] = total[...].astype(BF16)


def tail_part(last, cols, pos, hubs, tiles, near, weight, inverse, send=None):
    nodes, width = near.shape
    group = TALL // TB
    lanes = width // TB
    in_specs = [
        smem(),
        smem(),
        hbm(),
        band(group, 2, TB, TB),
        band(TALL, width),
        whole(width, width),
        band(TALL, 1),
    ]
    args = [cols, pos, hubs, tiles, near, weight, inverse]
    out_specs = [band(TALL, width)]
    out_shape = [shape(BF16, nodes, width)]
    scratch = [
        pltpu.VMEM(hubs.shape, BF16),
        pltpu.VMEM((hubs.shape[0] * lanes, TB), F32),
        pltpu.VMEM((HUBS * lanes, TB), F32),
        pltpu.VMEM((HUBS + TB, width), BF16),
        pltpu.VMEM((TALL, width), BF16),
        pltpu.SemaphoreType.DMA((COLS,)),
    ]
    if not last:
        in_specs.append(whole(HUB_CAP, 1))
        args.append(send)
        out_specs.append(whole(HUB_CAP, width))
        out_shape.append(shape(BF16, HUB_CAP, width))
        scratch.append(pltpu.VMEM((HUB_CAP, width), F32))
    return pl.pallas_call(
        functools.partial(tail_kernel, last),
        grid=(nodes // TALL,),
        in_specs=in_specs,
        out_specs=out_specs,
        out_shape=out_shape,
        scratch_shapes=scratch,
        compiler_params=params(),
        cost_estimate=cost(),
        name="tail_part",
    )(*args)


def send_halos(outgoing):
    width = outgoing.shape[1]
    blocks = outgoing.reshape(ROWS, -1, width)
    return lax.all_to_all(blocks, "row", 0, 0, tiled=True).reshape(-1, width)


def on_device(
    features,
    w_first,
    w_second,
    send_rows,
    halo_count,
    hub_owner,
    hub_row,
    local_cols,
    local_tiles,
    remote_cols,
    remote_tiles,
):
    width = features.shape[1]
    place = jnp.stack([lax.axis_index("row"), lax.axis_index("col")]).astype(I32)
    rows = send_rows.reshape(-1)
    count = halo_count.reshape(-1)
    cols = local_cols.reshape(-1)
    far_cols = remote_cols.reshape(-1)
    tiles, far_tiles = local_tiles[0], remote_tiles[0]
    picked, send, pos = hub_start(place, hub_owner.reshape(1, -1), hub_row, features)
    pos = pos.reshape(-1)
    gathered = lax.all_gather(picked, "col", axis=0, tiled=True)
    halos = send_halos(halo_start(True, rows, count, features))
    near, inverse = near_part(True, place, cols, far_cols, features, halos, tiles, far_tiles, w_first)
    middle, picked = tail_part(
        False, far_cols, pos, gathered, far_tiles, near, w_first[width:], inverse, send
    )
    gathered = lax.all_gather(picked, "col", axis=0, tiled=True)
    halos = send_halos(halo_start(False, rows, count, middle))
    near = near_part(False, place, cols, far_cols, middle, halos, tiles, far_tiles, w_second, inverse)[0]
    return tail_part(True, far_cols, pos, gathered, far_tiles, near, w_second[width:], inverse)[0]


def solution(mesh):
    in_specs = (
        P(("row", "col"), None),
        P(),
        P(),
        P(("row", "col"), None, None),
        P(("row", "col"), None),
        P("row", None, None),
        P("row", None),
        P(("row", "col"), None, None),
        P(("row", "col"), None, None, None, None),
        P(("row", "col"), None, None),
        P(("row", "col"), None, None, None, None),
    )
    out_specs = P(("row", "col"), None)
    return jax.shard_map(on_device, mesh=mesh, in_specs=in_specs, out_specs=out_specs, check_vma=False)
```

time: 286 us -> 187 us (0.65); the launches traced: 280 us -> 184 us
  matrix products: 109 us -> 0 us
  Pallas kernels: 0 us -> 90.7 us
  local copies, waits for them, and re-layouts: 70.7 us -> 6.49 us
  other arithmetic: 25.6 us -> 0.65 us
  waiting for transfers between devices: 46.5 us -> 63.3 us
  starting transfers between devices: 14.7 us -> 9.92 us
    dot_general x14 -> x0, matrix products: 109 us -> none  [the longest x2 35.9 us: on_device(): jnp.einsum('btij,btjf->bif', local_vals, pick_blocks(local_chooser, own_b...]
    pallas_call x0 -> x7, Pallas kernels: none -> 90.7 us  [the longest x2 37.1 us: tail_part(): pl.pallas_call(functools.partial(tail_kernel, last), grid=(nodes // TALL,...]
    gather x6 -> x0, local copies, waits for them, and re-layouts: 60.8 us -> none  [the longest x2 26.3 us: gather_hubs(): return gathered[positions]]
    all_to_all x3 -> x2, waiting for transfers between devices: 0.01 us -> 48.5 us  [send_halos(): return lax.all_to_all(blocks, 'row', 0, 0, tiled=True).reshape(-1, width)]
    all_gather x2, waiting for transfers between devices: 46.5 us -> 14.8 us  [on_device(): gathered = lax.all_gather(picked, 'col', axis=0, tiled=True)]
    scatter x1 -> x0, local copies, waits for them, and re-layouts: 8.2 us -> none  [on_device(): jnp.zeros((hub_cap + 1,), jnp.int32).at[target].set(places)[:hub_cap]]
    convert_element_type x5 -> x0, other arithmetic: 6.35 us -> none  [the longest x2 4.75 us: on_device(): current = (activated * lax.rsqrt(jnp.mean(activated * activated, axis=-1,...]
    select_n x4 -> x0, other arithmetic: 6.33 us -> none  [the longest x2 5.6 us: on_device(): jnp.where(keep_mask[:, :, None], current[rows_sent], jnp.zeros((), jnp.bf...]
  transfers between devices with their start and end apart: 5 -> 4, of which waited for: 2 -> 4; matrix products, arithmetic and copies ran while one was open for 32% -> 2% of each run, Pallas kernels for 0% -> 25%
where the time goes in v1:
time: 187 us; the launch traced here: 184 us
  Pallas kernels  90.7 us (49%)
  waiting for transfers between devices  63.3 us (34%)
  between operations  13.5 us (7%)
  starting transfers between devices  9.92 us (5%)
  local copies, waits for them, and re-layouts  6.49 us (3%)
    all_to_all x2, waiting for transfers between devices, send_halos(): return lax.all_to_all(blocks, 'row', 0, 0, tiled=True).reshape(-1, width)  48.5 us
    pallas_call x2, Pallas kernels, tail_part(): pl.pallas_call(functools.partial(tail_kernel, last), grid=(nodes // TALL,...  37.1 us
    pallas_call x2, Pallas kernels, near_part(): pl.pallas_call(functools.partial(near_kernel, weighed), grid=(nodes // TA...  28.4 us
    pallas_call x2, Pallas kernels, halo_start(): pl.pallas_call(functools.partial(halo_kernel, noted), grid=(nodes // TALL...  16.9 us
    all_gather x2, waiting for transfers between devices, on_device(): gathered = lax.all_gather(picked, 'col', axis=0, tiled=True)  14.8 us
    all_to_all x2, starting transfers between devices, send_halos(): return lax.all_to_all(blocks, 'row', 0, 0, tiled=True).reshape(-1, width)  9.91 us
    pallas_call x1, Pallas kernels, hub_start(): pl.pallas_call(hub_kernel, grid=(nodes // TALL,), in_specs=[smem(), whole...  8.3 us
  transfers between devices with their start and end apart: 4, of which 4 were waited for; matrix products, arithmetic and copies ran while one was open for 2% of the time, Pallas kernels for 25%

profile of v1, /device:TPU:6, one launch (start us, length us, event | category | flops | bytes accessed | tf_op | source)
XLA Modules:
  0.0 184.5 jit_solution(8081012982879447118)
XLA Ops:
  6.5 0.0 copy-start.4
  6.5 0.0 all-gather.3.cloned.1.call-start
  6.5 0.7 pad_add_fusion.place_ref
  7.2 8.3 %hub_start.1 = (bf16[384,512]{1,0:T(8,128)(2,1)}, s32[384,1]{1,0:T(8,128)}, s32[24,128]{1,0:T(8,128)}) custom-call(s32[2]{0:T(128)} %pad_add_fusion.place_ref, s32[1,2048]{1,0:T(1,128)} %bitcast.27, s32[1,2048]{1,0:T(1,128)} %row_ref.1, bf16[4096,512]{1,0:T(8,128)(2,1)} %table_ref.5), custom_call_target="tpu_custom_call" | custom-call | flops 1000 | bytes 1000 | tf_op jit(solution)/shard_map/hub_start/pallas_call | solution.py:132
  15.5 0.0 all-gather.3.cloned.1.call-update
  15.5 0.0 copy-done.4
  15.5 0.6 copy.16
  16.1 0.0 copy-start.5
  16.1 0.0 copy-start.6
  16.1 0.0 copy-start.2
  16.1 8.4 %halo_start.2 = bf16[2176,512]{1,0:T(8,128)(2,1)} custom-call(s32[2048]{0:T(1024)} %bitcast.23, s32[8]{0:T(128)} %bitcast.29, bf16[4096,512]{1,0:T(8,128)(2,1)} %table_ref.5), custom_call_target="tpu_custom_call" | custom-call | flops 1000 | bytes 1000 | tf_op jit(solution)/shard_map/halo_start/pallas_call | solution.py:181
  24.6 4.9 %all-to-all-start = ((bf16[8,272,512]{2,1,0:T(8,128)(2,1)}), bf16[8,272,512]{2,1,0:T(8,128)(2,1)S(1)}, u32[]{:S(2)}, u32[]{:S(2)}) async-start(bf16[8,272,512]{2,1,0:T(8,128)(2,1)} %bitcast.17), calls=%async_computation | async-start | bytes 4456448 | tf_op jit(solution)/shard_map/all_to_all | solution.py:381
  29.5 0.0 all-gather.5.cloned.1.call-start
  29.5 0.0 copy-done.5
  29.5 0.1 copy.14
  29.6 0.7 reshape.30.far_ref.refs_0_
  30.3 0.0 copy-done.6
  30.3 0.1 copy.15
  30.4 0.6 reshape.33.cols_ref
  31.0 0.0 copy-done.2
  31.0 0.8 slice.6.refs_5_
  31.9 24.2 %all-to-all-done = bf16[8,272,512]{2,1,0:T(8,128)(2,1)S(1)} async-done(((bf16[8,272,512]{2,1,0:T(8,128)(2,1)}), bf16[8,272,512]{2,1,0:T(8,128)(2,1)S(1)}, u32[]{:S(2)}, u32[]{:S(2)}) %all-to-all-start) | async-done | bytes 2228256 | tf_op jit(solution)/shard_map/all_to_all | solution.py:381
  56.1 0.0 copy-start
  56.1 1.4 copy-done
  57.4 13.9 %near_part.2 = (f32[4096,512]{1,0:T(8,128)}, f32[4096,1]{1,0:T(8,128)}) custom-call(s32[2]{0:T(128)} %pad_add_fusion.place_ref, s32[64]{0:T(128)} %reshape.33.cols_ref, s32[64]{0:T(128)} %reshape.30.far_ref.refs_0_, bf16[4096,512]{1,0:T(8,128)(2,1)} %table_ref.5, bf16[2176,512]{1,0:T(8,128)(2,1)} %bitcast.18, bf16[32,2,128,128]{3,2,1,0:T(8,128)(2,1)} %bitcast.20, ...), custom_call_target="tpu_custom_call" | custom-call | flops 1000 | bytes 1000 | tf_op jit(solution)/shard_map/near_part/pallas_call | solution.py:260
  71.3 8.1 %all-gather.3.cloned.1.call-done.refs_2_ = bf16[6144,512]{1,0:T(8,128)(2,1)} async-done(((bf16[384,512]{1,0:T(8,128)(2,1)}), bf16[6144,512]{1,0:T(8,128)(2,1)}) %all-gather.3.cloned.1.call-update) | async-done | bytes 6291472 | tf_op jit(solution)/shard_map/all_gather | solution.py:406
  79.4 19.5 %tail_part.2 = (bf16[4096,512]{1,0:T(8,128)(2,1)}, bf16[384,512]{1,0:T(8,128)(2,1)}) custom-call(s32[64]{0:T(128)} %reshape.30.far_ref.refs_0_, s32[3072]{0:T(1024)} %bitcast.25, bf16[6144,512]{1,0:T(8,128)(2,1)} %all-gather.3.cloned.1.call-done.refs_2_, bf16[32,2,128,128]{3,2,1,0:T(8,128)(2,1)} %bitcast.14, f32[4096,512]{1,0:T(8,128)} %get-tuple-element.14.refs_4_, ...), custom_call_target="tpu_custom_call" | custom-call | flops 1000 | bytes 1000 | tf_op jit(solution)/shard_map/tail_part/pallas_call | solution.py:365
  98.9 0.0 all-gather.5.cloned.1.call-update
  98.9 0.0 copy-start.3
  98.9 8.4 %halo_start.3 = bf16[2048,512]{1,0:T(8,128)(2,1)} custom-call(s32[2048]{0:T(1024)} %bitcast.24, s32[8]{0:T(128)} %bitcast.30, bf16[4096,512]{1,0:T(8,128)(2,1)} %get-tuple-element.18.table_ref), custom_call_target="tpu_custom_call" | custom-call | flops 1000 | bytes 1000 | tf_op jit(solution)/shard_map/halo_start/pallas_call | solution.py:181
  107.4 5.0 %all-to-all-start.1 = ((bf16[8,256,512]{2,1,0:T(8,128)(2,1)}), bf16[8,256,512]{2,1,0:T(8,128)(2,1)S(1)}, u32[]{:S(2)}, u32[]{:S(2)}) async-start(bf16[8,256,512]{2,1,0:T(8,128)(2,1)} %bitcast.22), calls=%async_computation.1 | async-start | bytes 4194304 | tf_op jit(solution)/shard_map/all_to_all | solution.py:381
  112.3 0.0 copy-done.3
  112.3 0.8 slice.7.refs_5_
  113.2 24.3 %all-to-all-done.1 = bf16[8,256,512]{2,1,0:T(8,128)(2,1)S(1)} async-done(((bf16[8,256,512]{2,1,0:T(8,128)(2,1)}), bf16[8,256,512]{2,1,0:T(8,128)(2,1)S(1)}, u32[]{:S(2)}, u32[]{:S(2)}) %all-to-all-start.1) | async-done | bytes 2097184 | tf_op jit(solution)/shard_map/all_to_all | solution.py:381
  137.5 0.0 copy-start.1
  137.5 1.3 copy-done.1
  138.8 14.6 %near_part.3.refs_4_ = f32[4096,512]{1,0:T(8,128)} custom-call(s32[2]{0:T(128)} %pad_add_fusion.place_ref, s32[64]{0:T(128)} %reshape.33.cols_ref, s32[64]{0:T(128)} %reshape.30.far_ref.refs_0_, bf16[4096,512]{1,0:T(8,128)(2,1)} %get-tuple-element.18.table_ref, bf16[2048,512]{1,0:T(8,128)(2,1)} %bitcast.19, bf16[32,2,128,128]{3,2,1,0:T(8,128)(2,1)} %bitcast.21, ...), custom_call_target="tpu_custom_call" | custom-call | flops 1000 | bytes 1000 | tf_op jit(solution)/shard_map/near_part/pallas_call | solution.py:260
  153.4 6.7 %all-gather.5.cloned.1.call-done.refs_2_ = bf16[6144,512]{1,0:T(8,128)(2,1)} async-done(((bf16[384,512]{1,0:T(8,128)(2,1)}), bf16[6144,512]{1,0:T(8,128)(2,1)}) %all-gather.5.cloned.1.call-update) | async-done | bytes 6291472 | tf_op jit(solution)/shard_map/all_gather | solution.py:412
  160.1 17.6 %tail_part.3 = bf16[4096,512]{1,0:T(8,128)(2,1)} custom-call(s32[64]{0:T(128)} %reshape.30.far_ref.refs_0_, s32[3072]{0:T(1024)} %bitcast.26, bf16[6144,512]{1,0:T(8,128)(2,1)} %all-gather.5.cloned.1.call-done.refs_2_, bf16[32,2,128,128]{3,2,1,0:T(8,128)(2,1)} %bitcast.16, f32[4096,512]{1,0:T(8,128)} %near_part.3.refs_4_, bf16[512,512]{1,0:T(8,128)(2,1)} %slice.7.refs_5_, ...), custom_call_target="tpu_custom_call" | custom-call | flops 1000 | bytes 1000 | tf_op jit(solution)/shard_map/tail_part/pallas_call | solution.py:365
Async XLA Ops:
  6.5 9.0 %copy-start.4 = (s32[1,8,256]{2,1,0:T(8,128)S(1)}, s32[1,8,256]{2,1,0:T(8,128)}, u32[]{:S(2)}) copy-start(s32[1,8,256]{2,1,0:T(8,128)} %param.14) | copy-start | bytes 24580
  6.5 72.9 %all-gather.3.cloned.1.call-start = ((), (), s32[]{:S(2)}) async-start(), calls=%async_computation.2 | async-start | bytes 6684672 | tf_op jit(solution)/shard_map/all_gather | solution.py:406
  16.1 13.4 %copy-start.5 = (s32[1,32,2]{1,2,0:T(2,128)S(1)}, s32[1,32,2]{1,2,0:T(2,128)}, u32[]{:S(2)}) copy-start(s32[1,32,2]{1,2,0:T(2,128)} %param.20) | copy-start | bytes 772
  16.1 14.2 %copy-start.6 = (s32[1,32,2]{1,2,0:T(2,128)S(1)}, s32[1,32,2]{1,2,0:T(2,128)}, u32[]{:S(2)}) copy-start(s32[1,32,2]{1,2,0:T(2,128)} %param.18) | copy-start | bytes 772
  16.1 14.9 %copy-start.2 = (bf16[1024,512]{1,0:T(8,128)(2,1)S(1)}, bf16[1024,512]{1,0:T(8,128)(2,1)}, u32[]{:S(2)}) copy-start(bf16[1024,512]{1,0:T(8,128)(2,1)} %weight_ref.2) | copy-start | bytes 3145732
  24.6 31.5 %all-to-all-start = ((bf16[8,272,512]{2,1,0:T(8,128)(2,1)}), bf16[8,272,512]{2,1,0:T(8,128)(2,1)S(1)}, u32[]{:S(2)}, u32[]{:S(2)}) async-start(bf16[8,272,512]{2,1,0:T(8,128)(2,1)} %bitcast.17), calls=%async_computation | async-start | bytes 4456448 | tf_op jit(solution)/shard_map/all_to_all | solution.py:381
  29.5 130.6 %all-gather.5.cloned.1.call-start = ((), (), s32[]{:S(2)}) async-start(), calls=%async_computation.3 | async-start | bytes 6684672 | tf_op jit(solution)/shard_map/all_gather | solution.py:412
  56.1 1.4 copy-start
  98.9 13.4 %copy-start.3 = (bf16[1024,512]{1,0:T(8,128)(2,1)S(1)}, bf16[1024,512]{1,0:T(8,128)(2,1)}, u32[]{:S(2)}) copy-start(bf16[1024,512]{1,0:T(8,128)(2,1)} %weight_ref.3) | copy-start | bytes 3145732
  107.4 30.1 %all-to-all-start.1 = ((bf16[8,256,512]{2,1,0:T(8,128)(2,1)}), bf16[8,256,512]{2,1,0:T(8,128)(2,1)S(1)}, u32[]{:S(2)}, u32[]{:S(2)}) async-start(bf16[8,256,512]{2,1,0:T(8,128)(2,1)} %bitcast.22), calls=%async_computation.1 | async-start | bytes 4194304 | tf_op jit(solution)/shard_map/all_to_all | solution.py:381
  137.5 1.3 copy-start.1
Sparse Core Ops, SparseCore 0:
  15.6 63.7 all-gather.2
  99.1 60.9 all-gather.4

commit v2 on v0

v2 whole, which is shorter than its diff:
```python
import functools

import jax
import jax.numpy as jnp
from jax import lax
from jax.experimental import pallas as pl
from jax.experimental.pallas import tpu as pltpu
from jax.sharding import PartitionSpec as P

F32 = jnp.float32
BF16 = jnp.bfloat16
I32 = jnp.int32
MIB = 1024 * 1024
TB = 128
ROWS = 8
COLS = 16
SIDE = 4
HALO = 256
HUBS = 2048
PAIR = 24
SHARE = 128
HALF = 64
TALL = 1024


def params(mib):
    return pltpu.CompilerParams(vmem_limit_bytes=mib * MIB)


def cost():
    return pl.CostEstimate(flops=1000, bytes_accessed=1000, transcendentals=0)


def vmem():
    return pl.BlockSpec(memory_space=pltpu.VMEM)


def smem():
    return pl.BlockSpec(memory_space=pltpu.SMEM)


def hbm():
    return pl.BlockSpec(memory_space=pl.ANY)


def shape(dtype, *dims):
    return jax.ShapeDtypeStruct(dims, dtype)


def iota(dims, dim):
    return lax.broadcasted_iota(I32, dims, dim)


def widen(rows, wide, first):
    lanes = rows.shape[1] // TB
    for j in range(lanes):
        wide[pl.ds(first * lanes + j, rows.shape[0], stride=lanes), :] = rows[:, j * TB : (j + 1) * TB]


def move_row(source, row, target, slot):
    lanes = 4
    target[pl.ds(pl.multiple_of(slot * lanes, lanes), lanes), :] = source[
        pl.ds(pl.multiple_of(row * lanes, lanes), lanes), :
    ]


def write_index(my_col, owner, rows):
    my_z, my_y = my_col // SIDE, lax.rem(my_col, SIDE)
    chunks = HUBS // TB
    owner_id = iota((COLS, TB), 0)
    masks, below = [], jnp.zeros((COLS, TB), F32)
    for c in range(chunks):
        part = owner[:, c * TB : (c + 1) * TB]
        masks.append(jnp.where(part == owner_id, 1.0, 0.0))
        below = below + jnp.where(part < owner_id, 1.0, 0.0)
    offset = jnp.sum(below, axis=1, keepdims=True)
    earlier = jnp.where(iota((TB, TB), 0) < iota((TB, TB), 1), 1.0, 0.0).astype(BF16)
    inside = jnp.dot(jnp.concatenate(masks, axis=0).astype(BF16), earlier, preferred_element_type=F32)
    running = jnp.zeros((COLS, 1), F32)
    ranks, places = [], []
    for c in range(chunks):
        rank = inside[c * COLS : (c + 1) * COLS, :] + running
        ranks.append(jnp.sum(masks[c] * rank, axis=0, keepdims=True))
        places.append(jnp.sum(masks[c] * (rank + offset), axis=0, keepdims=True))
        running = running + jnp.sum(masks[c], axis=1, keepdims=True)
    rank = jnp.concatenate(ranks, axis=0).astype(I32)
    place = jnp.concatenate(places, axis=0).astype(I32)
    who = jnp.concatenate([owner[:, c * TB : (c + 1) * TB] for c in range(chunks)], axis=0)
    local = jnp.concatenate([rows[:, c * TB : (c + 1) * TB] for c in range(chunks)], axis=0).astype(F32)
    holder = lax.bitwise_and(place, COLS - 1)
    share = lax.shift_right_logical(place, 4)
    turn = lax.shift_right_logical(rank, 4)
    slot = jnp.where(who == my_col, holder * PAIR + turn, -1)
    kept = jnp.where(holder == my_col, share, -1)
    arrived = (who * PAIR + turn).astype(F32)

    def pick(keys, values, first):
        wanted = iota((TB, TB), 0) + first
        total = jnp.zeros((TB, TB), F32)
        for c in range(chunks):
            total = total + jnp.where(keys[c : c + 1, :] == wanted, values[c : c + 1, :], 0.0)
        return jnp.sum(total, axis=1, keepdims=True).astype(I32)

    send = jnp.concatenate([pick(slot, local, k * TB) for k in range(COLS * PAIR // TB)], axis=0)
    keep = pick(kept, arrived, 0)
    step_z = lax.bitwise_and(lax.shift_right_logical(holder, 2) - my_z + SIDE, SIDE - 1)
    step_y = lax.bitwise_and(lax.bitwise_and(holder, SIDE - 1) - my_y + SIDE, SIDE - 1)
    first = step_z * 256 + step_y * HALF + share
    second = HUBS // 2 + step_y * 256 + step_z * HALF + share - HALF
    return send, keep, jnp.where(share < HALF, first, second)


def choose(wanted, first, count, rows):
    chosen = jnp.where(wanted - first == iota((wanted.shape[0], count), 1), 1.0, 0.0).astype(BF16)
    return jnp.dot(chosen, rows, preferred_element_type=F32)


def load_table(table_ref, held, sem):
    chunk = held.shape[0] // SIDE
    copies = []
    for k in range(SIDE):
        span = pl.ds(k * chunk, chunk)
        copies.append(pltpu.make_async_copy(table_ref.at[span], held.at[span], sem.at[k]))
    for copy in copies:
        copy.start()
    return copies


def hub_kernel(col_ref, owner_ref, row_ref, table_ref, out_ref, send_ref, keep_ref, pos_ref, held, sem):
    copies = load_table(table_ref, held, sem)
    send, keep, pos = write_index(col_ref[0], owner_ref[...], row_ref[...])
    send_ref[...] = send
    keep_ref[...] = keep
    pos_ref[...] = pos
    chunk = held.shape[0] // SIDE
    total = jnp.zeros(out_ref.shape, F32)
    for k in range(SIDE):
        copies[k].wait()
        total = total + choose(send, k * chunk, chunk, held[k * chunk : (k + 1) * chunk, :])
    out_ref[...] = total.astype(BF16)


def hub_start(my_col, owner, rows, table):
    nodes, width = table.shape
    sent = COLS * PAIR
    return pl.pallas_call(
        hub_kernel,
        in_specs=[smem(), vmem(), vmem(), hbm()],
        out_specs=[vmem()] * 4,
        out_shape=[shape(BF16, sent, width), shape(I32, sent, 1), shape(I32, SHARE, 1), shape(I32, HUBS // TB, TB)],
        scratch_shapes=[pltpu.VMEM((nodes, width), BF16), pltpu.SemaphoreType.DMA((SIDE,))],
        compiler_params=params(60),
        cost_estimate=cost(),
        name="hub_start",
    )(my_col, owner, rows, table)


def keep_kernel(keep_ref, arrived_ref, first_ref, second_ref):
    kept = choose(keep_ref[...], 0, arrived_ref.shape[0], arrived_ref[...]).astype(BF16)
    first_ref[...] = kept[:HALF]
    second_ref[...] = kept[HALF:]


def hub_keep(keep_index, arrived):
    half = shape(BF16, HALF, arrived.shape[1])
    return pl.pallas_call(
        keep_kernel,
        in_specs=[vmem(), vmem()],
        out_specs=[vmem(), vmem()],
        out_shape=[half, half],
        compiler_params=params(60),
        cost_estimate=cost(),
        name="hub_keep",
    )(keep_index, arrived)


def halo_kernel(rows_ref, count_ref, table_ref, out_ref, held, wide, picked, staged, sem, out_sem):
    lanes = 4
    unroll = 32
    copies = load_table(table_ref, held, sem)
    chunk = held.shape[0] // SIDE
    for k in range(SIDE):
        copies[k].wait()

        @pl.loop(0, chunk // TB)
        def _(n):
            top = pl.multiple_of(k * chunk + n * TB, TB)
            widen(held[pl.ds(top, TB), :].astype(F32), wide, top)

    out = [
        pltpu.make_async_copy(
            staged.at[pl.ds(peer * HALO, HALO)], out_ref.at[pl.ds(peer * HALO, HALO)], out_sem.at[peer]
        )
        for peer in range(ROWS)
    ]
    for peer in range(ROWS):
        count = count_ref[0, peer]

        @pl.loop(0, (count + unroll - 1) // unroll)
        def _(group):
            for u in range(unroll):
                slot = group * unroll + u
                move_row(wide, rows_ref[peer, slot], picked, slot)

        for half in range(HALO // TB):
            live = iota((TB, TB), 0) + half * TB < count
            top = peer * HALO + half * TB
            for j in range(lanes):
                part = picked[pl.ds(half * TB * lanes + j, TB, stride=lanes), :]
                staged[top : top + TB, j * TB : (j + 1) * TB] = jnp.where(live, part, 0.0).astype(BF16)
        out[peer].start()
    for copy in out:
        copy.wait()


def halo_start(rows, count, table):
    nodes, width = table.shape
    lanes = width // TB
    return pl.pallas_call(
        halo_kernel,
        in_specs=[smem(), smem(), hbm()],
        out_specs=hbm(),
        out_shape=shape(BF16, ROWS * HALO, width),
        scratch_shapes=[
            pltpu.VMEM((nodes, width), BF16),
            pltpu.VMEM((nodes * lanes, TB), F32),
            pltpu.VMEM((HALO * lanes, TB), F32),
            pltpu.VMEM((ROWS * HALO, width), BF16),
            pltpu.SemaphoreType.DMA((SIDE,)),
            pltpu.SemaphoreType.DMA((ROWS,)),
        ],
        compiler_params=params(60),
        cost_estimate=cost(),
        name="halo_start",
    )(rows, count, table)


def start_chunks(pairs, sem):
    copies = [pltpu.make_async_copy(source, target, sem.at[k]) for k, (source, target) in enumerate(pairs)]
    for copy in copies:
        copy.start()
    return copies


def chunk_copies(source, target, sem):
    return [
        pltpu.make_async_copy(source.at[pl.ds(k * TALL, TALL)], target.at[pl.ds(k * TALL, TALL)], sem.at[k])
        for k in range(source.shape[0] // TALL)
    ]


def gather_blocks(table, cols_ref, block):
    tops = [pl.multiple_of(cols_ref[t, block] * TB, TB) for t in range(2)]
    return jnp.concatenate([table[pl.ds(top, TB), :] for top in tops], axis=0)


def tail_kernel(last, *refs):
    pieces = refs[:8]
    row_ref, count_ref, cols_ref, far_ref, pos_ref = refs[8:13]
    halo_ref, table_ref, tiles_ref, far_tiles_ref, weight_ref = refs[13:18]
    rest = refs[18:]
    if last:
        out_ref = rest[0]
        rest = rest[1:]
    else:
        send_ref, out_ref, picked_ref, total = rest[:3] + rest[-1:]
        rest = rest[3:-1]
    held, wide, placed, store, table, tiles, far_tiles, weight, joined, result, sem, out_sem = rest
    lanes = 4
    size = HUBS // 8
    width = store.shape[1]
    halo_rows = ROWS * HALO
    pairs = [(pieces[k], held.at[pl.ds(k * size, size)]) for k in range(8)]
    pairs.append((table_ref, table))
    pairs.append((weight_ref, weight))
    pairs.append((tiles_ref, tiles))
    pairs.append((halo_ref, store.at[pl.ds(0, halo_rows)]))
    pairs.append((far_tiles_ref, far_tiles))
    copies = start_chunks(pairs, sem)
    for k in range(8):
        copies[k].wait()
        widen(held[k * size : (k + 1) * size, :].astype(F32), wide, k * size)
    unroll = 64
    for k in range(HUBS // TB):

        @pl.loop(0, TB // unroll)
        def _(n):
            for u in range(unroll):
                slot = n * unroll + u
                move_row(wide, pos_ref[k, slot], placed, k * TB + slot)

    for j in range(lanes):
        store[halo_rows : halo_rows + HUBS, j * TB : (j + 1) * TB] = placed[pl.ds(j, HUBS, stride=lanes), :].astype(BF16)
    for copy in copies[8:]:
        copy.wait()
    out = chunk_copies(result, out_ref, out_sem)
    group = TALL // TB
    my_row = row_ref[0]
    for k in range(result.shape[0] // TALL):
        for b in range(group):
            block = k * group + b
            near, far = tiles[block], far_tiles[block]
            left = jnp.concatenate([near[0], near[1], far[0], far[1]], axis=1)
            right = jnp.concatenate([gather_blocks(table, cols_ref, block), gather_blocks(store, far_ref, block)], axis=0)
            total_rows = jnp.dot(left, right, preferred_element_type=F32)
            mass = near[0].astype(F32) + near[1].astype(F32)
            for t in range(2):
                col = far_ref[t, block]
                peer = lax.bitwise_and(lax.shift_right_logical(col, 1), ROWS - 1)
                count = count_ref[lax.bitwise_xor(peer, my_row), my_row]
                live = jnp.where(col < 2 * ROWS, count - lax.bitwise_and(col, 1) * TB, TB)
                mass = mass + jnp.where(iota((TB, TB), 1) < live, far[t].astype(F32), 0.0)
            inverse = 1.0 / jnp.sum(mass, axis=1, keepdims=True)
            joined[b * TB : (b + 1) * TB, width : 2 * width] = (total_rows * inverse).astype(BF16)
        span = slice(k * TALL, (k + 1) * TALL)
        joined[:, 0:width] = table[span, :]
        preact = jnp.dot(joined[...], weight[...], preferred_element_type=F32)
        active = jnp.maximum(preact, 0.0)
        scale = lax.rsqrt(jnp.mean(active * active, axis=1, keepdims=True) + 1e-05)
        rows = (active * scale).astype(BF16)
        result[span, :] = rows
        out[k].start()
        if not last:
            part = choose(send_ref[...], k * TALL, TALL, rows)
            if k == 0:
                total[...] = part
            else:
                total[...] = total[...] + part
    if not last:
        picked_ref[...] = total[...].astype(BF16)
    for copy in out:
        copy.wait()


def tail_part(last, hubs, row, count, cols, far_cols, pos, halos, table, tiles, far_tiles, weight, send=None):
    nodes, width = table.shape
    lanes = width // TB
    in_specs = [hbm()] * 8 + [smem()] * 5 + [hbm()] * 5
    args = [*hubs, row, count, cols, far_cols, pos, halos, table, tiles, far_tiles, weight]
    out_specs = [hbm()]
    out_shape = [shape(BF16, nodes, width)]
    scratch = [
        pltpu.VMEM((HUBS, width), BF16),
        pltpu.VMEM((HUBS * lanes, TB), F32),
        pltpu.VMEM((HUBS * lanes, TB), F32),
        pltpu.VMEM((ROWS * HALO + HUBS, width), BF16),
        pltpu.VMEM((nodes, width), BF16),
        pltpu.VMEM(tiles.shape, BF16),
        pltpu.VMEM(far_tiles.shape, BF16),
        pltpu.VMEM(weight.shape, BF16),
        pltpu.VMEM((TALL, 2 * width), BF16),
        pltpu.VMEM((nodes, width), BF16),
        pltpu.SemaphoreType.DMA((13,)),
        pltpu.SemaphoreType.DMA((nodes // TALL,)),
    ]
    if not last:
        sent = COLS * PAIR
        in_specs.append(vmem())
        args.append(send)
        out_specs.append(vmem())
        out_shape.append(shape(BF16, sent, width))
        scratch.append(pltpu.VMEM((sent, width), F32))
    return pl.pallas_call(
        functools.partial(tail_kernel, last),
        in_specs=in_specs,
        out_specs=out_specs,
        out_shape=out_shape,
        scratch_shapes=scratch,
        compiler_params=params(60),
        cost_estimate=cost(),
        name="tail_part",
    )(*args)


def fetch(array, dz, dy):
    pairs = [
        (((z + dz) % SIDE) * SIDE + (y + dy) % SIDE, z * SIDE + y) for z in range(SIDE) for y in range(SIDE)
    ]
    return lax.ppermute(array, "col", pairs)


def spread_hubs(first, second):
    order = (1, 3, 2)
    near_y = {k: fetch(first, 0, k) for k in order}
    near_z = {k: fetch(second, k, 0) for k in order}
    first_all = jnp.concatenate([first] + [near_y[k] for k in range(1, SIDE)], axis=0)
    second_all = jnp.concatenate([second] + [near_z[k] for k in range(1, SIDE)], axis=0)
    far_z = {k: fetch(first_all, k, 0) for k in order}
    far_y = {k: fetch(second_all, 0, k) for k in order}
    left = [first_all] + [far_z[k] for k in range(1, SIDE)]
    right = [second_all] + [far_y[k] for k in range(1, SIDE)]
    return left + right


def share_counts(count):
    table = count
    for bit in (1, 2, 4):
        pairs = [(i, i ^ bit) for i in range(ROWS)]
        table = jnp.concatenate([table, lax.ppermute(table, "row", pairs)], axis=0)
    return table


def exchange(picked, keep, outgoing):
    width = picked.shape[1]
    arrived = lax.all_to_all(picked.reshape(COLS, PAIR, width), "col", 0, 0, tiled=True)
    arrived, outgoing = lax.optimization_barrier((arrived.reshape(-1, width), outgoing))
    hubs = spread_hubs(*hub_keep(keep, arrived))
    halos = lax.all_to_all(outgoing.reshape(ROWS, HALO, width), "row", 0, 0, tiled=True)
    return hubs, halos.reshape(-1, width)


def on_device(
    features,
    w_first,
    w_second,
    send_rows,
    halo_count,
    hub_owner,
    hub_row,
    local_cols,
    local_tiles,
    remote_cols,
    remote_tiles,
):
    my_row = lax.axis_index("row").astype(I32).reshape(1)
    my_col = lax.axis_index("col").astype(I32).reshape(1)
    rows = send_rows[0]
    cols = local_cols[0].T
    far_cols = remote_cols[0].T
    tiles, far_tiles = local_tiles[0], remote_tiles[0]
    counts = share_counts(halo_count)
    picked, send, keep, pos = hub_start(my_col, hub_owner.reshape(1, -1), hub_row, features)
    outgoing, counts = lax.optimization_barrier((halo_start(rows, halo_count, features), counts))
    hubs, halos = exchange(picked, keep, outgoing)
    shared = (my_row, counts, cols, far_cols, pos)
    middle, picked = tail_part(False, hubs, *shared, halos, features, tiles, far_tiles, w_first, send)
    hubs, halos = exchange(picked, keep, halo_start(rows, halo_count, middle))
    return tail_part(True, hubs, *shared, halos, middle, tiles, far_tiles, w_second)[0]


def solution(mesh):
    in_specs = (
        P(("row", "col"), None),
        P(),
        P(),
        P(("row", "col"), None, None),
        P(("row", "col"), None),
        P("row", None, None),
        P("row", None),
        P(("row", "col"), None, None),
        P(("row", "col"), None, None, None, None),
        P(("row", "col"), None, None),
        P(("row", "col"), None, None, None, None),
    )
    out_specs = P(("row", "col"), None)
    return jax.shard_map(on_device, mesh=mesh, in_specs=in_specs, out_specs=out_specs, check_vma=False)
```

time: 286 us -> 182 us (0.64); the launches traced: 280 us -> 179 us
  matrix products: 109 us -> 0 us
  Pallas kernels: 0 us -> 70.3 us
  local copies, waits for them, and re-layouts: 70.7 us -> 8.31 us
  starting transfers between devices: 14.7 us -> 69.8 us
  other arithmetic: 25.6 us -> 0.62 us
  waiting for transfers between devices: 46.5 us -> 29.7 us
  between operations: 13.8 us -> 0.57 us
    dot_general x14 -> x0, matrix products: 109 us -> none  [the longest x2 35.9 us: on_device(): jnp.einsum('btij,btjf->bif', local_vals, pick_blocks(local_chooser, own_b...]
    pallas_call x0 -> x7, Pallas kernels: none -> 70.3 us  [the longest x2 34.9 us: tail_part(): pl.pallas_call(functools.partial(tail_kernel, last), in_specs=in_specs, o...]
    gather x6 -> x0, local copies, waits for them, and re-layouts: 60.8 us -> none  [the longest x2 26.3 us: gather_hubs(): return gathered[positions]]
    all_gather x2 -> x0, waiting for transfers between devices: 46.5 us -> none  [gather_hubs(): gathered = lax.all_gather(packed, 'col', axis=0, tiled=True)]
    ppermute x0 -> x27, starting transfers between devices: none -> 45.7 us  [the longest x24 43.3 us: fetch(): return lax.ppermute(array, 'col', pairs)]
    ppermute x0 -> x27, waiting for transfers between devices: none -> 29.7 us  [the longest x24 25.9 us: fetch(): return lax.ppermute(array, 'col', pairs)]
    all_to_all x3 -> x4, starting transfers between devices: 14.5 us -> 24.1 us  [the longest x2 13.2 us: exchange(): lax.all_to_all(picked.reshape(COLS, PAIR, width), 'col', 0, 0, tiled=True)]
    scatter x1 -> x0, local copies, waits for them, and re-layouts: 8.2 us -> none  [on_device(): jnp.zeros((hub_cap + 1,), jnp.int32).at[target].set(places)[:hub_cap]]
  transfers between devices with their start and end apart: 5 -> 31, of which waited for: 2 -> 12; matrix products, arithmetic and copies ran while one was open for 32% -> 2% of each run, Pallas kernels for 0% -> 17%
where the time goes in v2:
time: 182 us; the launch traced here: 179 us
  Pallas kernels  70.3 us (39%)
  starting transfers between devices  69.8 us (38%)
  waiting for transfers between devices  29.7 us (16%)
  local copies, waits for them, and re-layouts  8.31 us (5%)
    ppermute x24, starting transfers between devices, fetch(): return lax.ppermute(array, 'col', pairs)  43.3 us
    pallas_call x2, Pallas kernels, tail_part(): pl.pallas_call(functools.partial(tail_kernel, last), in_specs=in_specs, o...  34.9 us
    pallas_call x2, Pallas kernels, halo_start(): pl.pallas_call(halo_kernel, in_specs=[smem(), smem(), hbm()], out_specs=h...  26.1 us
    ppermute x24, waiting for transfers between devices, fetch(): return lax.ppermute(array, 'col', pairs)  25.9 us
    all_to_all x2, starting transfers between devices, exchange(): lax.all_to_all(picked.reshape(COLS, PAIR, width), 'col', 0, 0, tiled=True)  13.2 us
    all_to_all x2, starting transfers between devices, exchange(): lax.all_to_all(outgoing.reshape(ROWS, HALO, width), 'row', 0, 0, tiled=True)  10.8 us
    unnamed x48, local copies, waits for them, and re-layouts  8.29 us
    pallas_call x1, Pallas kernels, hub_start(): pl.pallas_call(hub_kernel, in_specs=[smem(), vmem(), vmem(), hbm()], out_...  5.44 us
  transfers between devices with their start and end apart: 31, of which 12 were waited for; matrix products, arithmetic and copies ran while one was open for 2% of the time, Pallas kernels for 17%

profile of v2, /device:TPU:6, one launch (start us, length us, event | category | flops | bytes accessed | tf_op | source)
XLA Modules:
  0.0 179.4 jit_solution(8769452089375814358)
XLA Ops:
  0.0 5.4 %hub_start.1 = (bf16[384,512]{1,0:T(8,128)(2,1)}, s32[384,1]{1,0:T(8,128)}, s32[128,1]{1,0:T(8,128)}, s32[16,128]{1,0:T(8,128)}) custom-call(s32[1]{0:T(128)} %bitcast.col_ref, s32[1,2048]{1,0:T(1,128)} %bitcast.34, s32[1,2048]{1,0:T(1,128)} %row_ref.1, bf16[4096,512]{1,0:T(8,128)(2,1)} %refs_14_.1), custom_call_target="tpu_custom_call" | custom-call | flops 1000 | bytes 1000 | tf_op jit(solution)/shard_map/hub_start/pallas_call | solution.py:146
  5.4 8.1 %all-to-all-start = ((bf16[16,24,512]{2,1,0:T(8,128)(2,1)}), bf16[16,24,512]{2,1,0:T(8,128)(2,1)S(1)}, u32[]{:S(2)}, u32[]{:S(2)}) async-start(bf16[16,24,512]{2,1,0:T(8,128)(2,1)} %bitcast.30), calls=%async_computation | async-start | bytes 786432 | tf_op jit(solution)/shard_map/all_to_all | solution.py:405
  13.6 1.1 collective-permute-done
  14.7 0.9 collective-permute-start.1
  15.6 2.7 %collective-permute-done.1 = s32[2,8]{1,0:T(2,128)S(1)} collective-permute-done((s32[2,8]{1,0:T(2,128)S(1)}, s32[2,8]{1,0:T(2,128)S(1)}, u32[]{:S(2)}, u32[]{:S(2)}) %collective-permute-start.1) | collective-permute-done | bytes 96 | tf_op jit(solution)/shard_map/ppermute | solution.py:399
  18.4 1.5 collective-permute-start.2
  19.9 8.0 %halo_start.2 = bf16[2048,512]{1,0:T(8,128)(2,1)} custom-call(s32[8,256]{1,0:T(8,128)} %bitcast.32, s32[1,8]{1,0:T(1,128)} %count_ref.3, bf16[4096,512]{1,0:T(8,128)(2,1)} %refs_14_.1), custom_call_target="tpu_custom_call" | custom-call | flops 1000 | bytes 1000 | tf_op jit(solution)/shard_map/halo_start/pallas_call | solution.py:219
  29.2 6.0 %all-to-all-start.1 = ((bf16[8,256,512]{2,1,0:T(8,128)(2,1)}), bf16[8,256,512]{2,1,0:T(8,128)(2,1)S(1)}, u32[]{:S(2)}, u32[]{:S(2)}) async-start(bf16[8,256,512]{2,1,0:T(8,128)(2,1)} %bitcast.21), calls=%async_computation.1 | async-start | bytes 4194304 | tf_op jit(solution)/shard_map/all_to_all | solution.py:408
  35.2 1.9 %hub_keep.2 = (bf16[64,512]{1,0:T(8,128)(2,1)}, bf16[64,512]{1,0:T(8,128)(2,1)}) custom-call(s32[128,1]{1,0:T(8,128)} %get-tuple-element.21.keep_ref, bf16[384,512]{1,0:T(8,128)(2,1)} %bitcast.28), custom_call_target="tpu_custom_call" | custom-call | flops 1000 | bytes 1000 | tf_op jit(solution)/shard_map/hub_keep/pallas_call | solution.py:166
  37.2 1.0 collective-permute-start.5
  38.1 2.6 %collective-permute-start.4 = (bf16[64,512]{1,0:T(8,128)(2,1)}, bf16[64,512]{1,0:T(8,128)(2,1)S(1)}, u32[]{:S(2)}, u32[]{:S(2)}) collective-permute-start(bf16[64,512]{1,0:T(8,128)(2,1)} %get-tuple-element.25), channel_id=1, source_target_pairs={{2,0},{3,1},{0,2},{1,3},{6,4},{7,5},{4,6},{5,7},{10,8},{11,9},{8,1... | collective-permute-start | bytes 196616 | tf_op jit(solution)/shard_map/ppermute | solution.py:379
  40.7 1.9 %collective-permute-start.3 = (bf16[64,512]{1,0:T(8,128)(2,1)}, bf16[64,512]{1,0:T(8,128)(2,1)S(1)}, u32[]{:S(2)}, u32[]{:S(2)}) collective-permute-start(bf16[64,512]{1,0:T(8,128)(2,1)} %get-tuple-element.25), channel_id=1, source_target_pairs={{1,0},{2,1},{3,2},{0,3},{5,4},{6,5},{7,6},{4,7},{9,8},{10,9},{11,1... | collective-permute-start | bytes 196616 | tf_op jit(solution)/shard_map/ppermute | solution.py:379
  42.6 1.2 collective-permute-start.11
  43.8 2.1 %collective-permute-start.9 = (bf16[64,512]{1,0:T(8,128)(2,1)}, bf16[64,512]{1,0:T(8,128)(2,1)S(1)}, u32[]{:S(2)}, u32[]{:S(2)}) collective-permute-start(bf16[64,512]{1,0:T(8,128)(2,1)} %get-tuple-element.26), channel_id=1, source_target_pairs={{4,0},{5,1},{6,2},{7,3},{8,4},{9,5},{10,6},{11,7},{12,8},{13,9},{1... | collective-permute-start | bytes 196616 | tf_op jit(solution)/shard_map/ppermute | solution.py:379
  48.3 3.3 %collective-permute-start.10 = (bf16[64,512]{1,0:T(8,128)(2,1)}, bf16[64,512]{1,0:T(8,128)(2,1)S(1)}, u32[]{:S(2)}, u32[]{:S(2)}) collective-permute-start(bf16[64,512]{1,0:T(8,128)(2,1)} %get-tuple-element.26), channel_id=1, source_target_pairs={{8,0},{9,1},{10,2},{11,3},{12,4},{13,5},{14,6},{15,7},{0,8},{1,9},... | collective-permute-start | bytes 196616 | tf_op jit(solution)/shard_map/ppermute | solution.py:379
  51.6 2.7 %collective-permute-done.10 = bf16[64,512]{1,0:T(8,128)(2,1)S(1)} collective-permute-done((bf16[64,512]{1,0:T(8,128)(2,1)}, bf16[64,512]{1,0:T(8,128)(2,1)S(1)}, u32[]{:S(2)}, u32[]{:S(2)}) %collective-permute-start.10) | collective-permute-done | bytes 65568 | tf_op jit(solution)/shard_map/ppermute | solution.py:379
  54.3 1.5 collective-permute-start.14
  56.1 2.5 %collective-permute-start.12 = (bf16[256,512]{1,0:T(8,128)(2,1)S(1)}, bf16[256,512]{1,0:T(8,128)(2,1)S(1)}, u32[]{:S(2)}, u32[]{:S(2)}) collective-permute-start(bf16[256,512]{1,0:T(8,128)(2,1)S(1)} %constant_dynamic-update-slice_fusion.4.refs_4_), channel_id=1, source_target_pairs={{1,0},{2,1},{3,2},{0,3},{5,4},{6,5},{7,6},{4,7},{9,8},{10,9},{11,1... | collective-permute-start | bytes 786440 | tf_op jit(solution)/shard_map/ppermute | solution.py:379
  58.6 1.1 collective-permute-start.8
  59.7 2.9 %collective-permute-start.7 = (bf16[256,512]{1,0:T(8,128)(2,1)S(1)}, bf16[256,512]{1,0:T(8,128)(2,1)}, u32[]{:S(2)}, u32[]{:S(2)}) collective-permute-start(bf16[256,512]{1,0:T(8,128)(2,1)S(1)} %constant_dynamic-update-slice_fusion.refs_0_), channel_id=1, source_target_pairs={{8,0},{9,1},{10,2},{11,3},{12,4},{13,5},{14,6},{15,7},{0,8},{1,9},... | collective-permute-start | bytes 786440 | tf_op jit(solution)/shard_map/ppermute | solution.py:379
  62.6 4.1 %collective-permute-done.14.refs_7_ = bf16[256,512]{1,0:T(8,128)(2,1)S(1)} collective-permute-done((bf16[256,512]{1,0:T(8,128)(2,1)S(1)}, bf16[256,512]{1,0:T(8,128)(2,1)S(1)}, u32[]{:S(2)}, u32[]{:S(2)}) %collective-permute-start.14) | collective-permute-done | bytes 262176 | tf_op jit(solution)/shard_map/ppermute | solution.py:379
  66.7 3.3 %collective-permute-start.6 = (bf16[256,512]{1,0:T(8,128)(2,1)S(1)}, bf16[256,512]{1,0:T(8,128)(2,1)}, u32[]{:S(2)}, u32[]{:S(2)}) collective-permute-start(bf16[256,512]{1,0:T(8,128)(2,1)S(1)} %constant_dynamic-update-slice_fusion.refs_0_), channel_id=1, source_target_pairs={{4,0},{5,1},{6,2},{7,3},{8,4},{9,5},{10,6},{11,7},{12,8},{13,9},{1... | collective-permute-start | bytes 786440 | tf_op jit(solution)/shard_map/ppermute | solution.py:379
  70.0 0.9 collective-permute-done.7.refs_2_
  70.9 3.0 %collective-permute-done.6.refs_1_ = bf16[256,512]{1,0:T(8,128)(2,1)} collective-permute-done((bf16[256,512]{1,0:T(8,128)(2,1)S(1)}, bf16[256,512]{1,0:T(8,128)(2,1)}, u32[]{:S(2)}, u32[]{:S(2)}) %collective-permute-start.6) | collective-permute-done | bytes 262176 | tf_op jit(solution)/shard_map/ppermute | solution.py:379
  73.9 1.3 copy-done
  75.2 18.8 %tail_part.2 = (bf16[4096,512]{1,0:T(8,128)(2,1)}, bf16[384,512]{1,0:T(8,128)(2,1)}) custom-call(bf16[256,512]{1,0:T(8,128)(2,1)} %copy-done.6, bf16[256,512]{1,0:T(8,128)(2,1)} %collective-permute-done.6.refs_1_, bf16[256,512]{1,0:T(8,128)(2,1)} %collective-permute-done.7.refs_2_, bf16[256,512]{1,0:T(8,128)(2,1)} %collective-permute-done.8.refs_3_, ...), custom_call_target="tpu_custom_call" | custom-call | flops 1000 | bytes 1000 | tf_op jit(solution)/shard_map/tail_part/pallas_call | solution.py:363
  94.0 5.2 %all-to-all-start.2 = ((bf16[16,24,512]{2,1,0:T(8,128)(2,1)}), bf16[16,24,512]{2,1,0:T(8,128)(2,1)S(1)}, u32[]{:S(2)}, u32[]{:S(2)}) async-start(bf16[16,24,512]{2,1,0:T(8,128)(2,1)} %bitcast.31), calls=%async_computation.2 | async-start | bytes 786432 | tf_op jit(solution)/shard_map/all_to_all | solution.py:405
  99.2 18.1 %halo_start.3 = bf16[2048,512]{1,0:T(8,128)(2,1)} custom-call(s32[8,256]{1,0:T(8,128)} %bitcast.33, s32[1,8]{1,0:T(1,128)} %count_ref.3, bf16[4096,512]{1,0:T(8,128)(2,1)} %get-tuple-element.32.table_ref.refs_14_), custom_call_target="tpu_custom_call" | custom-call | flops 1000 | bytes 1000 | tf_op jit(solution)/shard_map/halo_start/pallas_call | solution.py:219
  118.1 4.8 %all-to-all-start.3 = ((bf16[8,256,512]{2,1,0:T(8,128)(2,1)}), bf16[8,256,512]{2,1,0:T(8,128)(2,1)S(1)}, u32[]{:S(2)}, u32[]{:S(2)}) async-start(bf16[8,256,512]{2,1,0:T(8,128)(2,1)} %bitcast.22), calls=%async_computation.3 | async-start | bytes 4194304 | tf_op jit(solution)/shard_map/all_to_all | solution.py:408
  122.9 1.9 %hub_keep.3 = (bf16[64,512]{1,0:T(8,128)(2,1)}, bf16[64,512]{1,0:T(8,128)(2,1)}) custom-call(s32[128,1]{1,0:T(8,128)} %get-tuple-element.21.keep_ref, bf16[384,512]{1,0:T(8,128)(2,1)} %bitcast.29), custom_call_target="tpu_custom_call" | custom-call | flops 1000 | bytes 1000 | tf_op jit(solution)/shard_map/hub_keep/pallas_call | solution.py:166
  124.9 1.2 collective-permute-start.17
  126.1 2.9 %collective-permute-start.16 = (bf16[64,512]{1,0:T(8,128)(2,1)}, bf16[64,512]{1,0:T(8,128)(2,1)S(1)}, u32[]{:S(2)}, u32[]{:S(2)}) collective-permute-start(bf16[64,512]{1,0:T(8,128)(2,1)} %get-tuple-element.34), channel_id=1, source_target_pairs={{2,0},{3,1},{0,2},{1,3},{6,4},{7,5},{4,6},{5,7},{10,8},{11,9},{8,1... | collective-permute-start | bytes 196616 | tf_op jit(solution)/shard_map/ppermute | solution.py:379
  129.0 1.3 collective-permute-start.15
  130.3 2.3 %collective-permute-start.23 = (bf16[64,512]{1,0:T(8,128)(2,1)}, bf16[64,512]{1,0:T(8,128)(2,1)S(1)}, u32[]{:S(2)}, u32[]{:S(2)}) collective-permute-start(bf16[64,512]{1,0:T(8,128)(2,1)} %get-tuple-element.35), channel_id=1, source_target_pairs={{12,0},{13,1},{14,2},{15,3},{0,4},{1,5},{2,6},{3,7},{4,8},{5,9},{6... | collective-permute-start | bytes 196616 | tf_op jit(solution)/shard_map/ppermute | solution.py:379
  132.6 0.9 collective-permute-start.21
  135.2 1.9 %collective-permute-done.21 = bf16[64,512]{1,0:T(8,128)(2,1)S(1)} collective-permute-done((bf16[64,512]{1,0:T(8,128)(2,1)}, bf16[64,512]{1,0:T(8,128)(2,1)S(1)}, u32[]{:S(2)}, u32[]{:S(2)}) %collective-permute-start.21) | collective-permute-done | bytes 65568 | tf_op jit(solution)/shard_map/ppermute | solution.py:379
  137.1 1.9 %collective-permute-start.22 = (bf16[64,512]{1,0:T(8,128)(2,1)}, bf16[64,512]{1,0:T(8,128)(2,1)S(1)}, u32[]{:S(2)}, u32[]{:S(2)}) collective-permute-start(bf16[64,512]{1,0:T(8,128)(2,1)} %get-tuple-element.35), channel_id=1, source_target_pairs={{8,0},{9,1},{10,2},{11,3},{12,4},{13,5},{14,6},{15,7},{0,8},{1,9},... | collective-permute-start | bytes 196616 | tf_op jit(solution)/shard_map/ppermute | solution.py:379
  139.0 4.1 %collective-permute-done.22 = bf16[64,512]{1,0:T(8,128)(2,1)S(1)} collective-permute-done((bf16[64,512]{1,0:T(8,128)(2,1)}, bf16[64,512]{1,0:T(8,128)(2,1)S(1)}, u32[]{:S(2)}, u32[]{:S(2)}) %collective-permute-start.22) | collective-permute-done | bytes 65568 | tf_op jit(solution)/shard_map/ppermute | solution.py:379
  143.3 1.3 collective-permute-start.25
  144.6 1.8 collective-permute-start.24
  146.5 1.2 collective-permute-start.20
  147.6 2.7 %collective-permute-start.19 = (bf16[256,512]{1,0:T(8,128)(2,1)S(1)}, bf16[256,512]{1,0:T(8,128)(2,1)S(1)}, u32[]{:S(2)}, u32[]{:S(2)}) collective-permute-start(bf16[256,512]{1,0:T(8,128)(2,1)S(1)} %constant_dynamic-update-slice_fusion.8.refs_0_), channel_id=1, source_target_pairs={{8,0},{9,1},{10,2},{11,3},{12,4},{13,5},{14,6},{15,7},{0,8},{1,9},... | collective-permute-start | bytes 786440 | tf_op jit(solution)/shard_map/ppermute | solution.py:379
  150.4 4.9 %collective-permute-done.26.refs_7_ = bf16[256,512]{1,0:T(8,128)(2,1)S(1)} collective-permute-done((bf16[256,512]{1,0:T(8,128)(2,1)S(1)}, bf16[256,512]{1,0:T(8,128)(2,1)S(1)}, u32[]{:S(2)}, u32[]{:S(2)}) %collective-permute-start.26) | collective-permute-done | bytes 262176 | tf_op jit(solution)/shard_map/ppermute | solution.py:379
  155.2 2.1 %collective-permute-start.18 = (bf16[256,512]{1,0:T(8,128)(2,1)S(1)}, bf16[256,512]{1,0:T(8,128)(2,1)}, u32[]{:S(2)}, u32[]{:S(2)}) collective-permute-start(bf16[256,512]{1,0:T(8,128)(2,1)S(1)} %constant_dynamic-update-slice_fusion.8.refs_0_), channel_id=1, source_target_pairs={{4,0},{5,1},{6,2},{7,3},{8,4},{9,5},{10,6},{11,7},{12,8},{13,9},{1... | collective-permute-start | bytes 786440 | tf_op jit(solution)/shard_map/ppermute | solution.py:379
  157.4 1.3 collective-permute-done.19.refs_2_
  159.4 2.4 %collective-permute-done.18.refs_1_ = bf16[256,512]{1,0:T(8,128)(2,1)} collective-permute-done((bf16[256,512]{1,0:T(8,128)(2,1)S(1)}, bf16[256,512]{1,0:T(8,128)(2,1)}, u32[]{:S(2)}, u32[]{:S(2)}) %collective-permute-start.18) | collective-permute-done | bytes 262176 | tf_op jit(solution)/shard_map/ppermute | solution.py:379
  161.8 1.3 copy-done.1
  163.1 16.1 %tail_part.3 = bf16[4096,512]{1,0:T(8,128)(2,1)} custom-call(bf16[256,512]{1,0:T(8,128)(2,1)} %copy-done.4, bf16[256,512]{1,0:T(8,128)(2,1)} %collective-permute-done.18.refs_1_, bf16[256,512]{1,0:T(8,128)(2,1)} %copy-done.12, bf16[256,512]{1,0:T(8,128)(2,1)} %copy-done.11, bf16[256,512]{1,0:T(8,128)(2,1)} %copy-done.5, bf16[256,512]{1,0:T(8,128)(2,1)} %copy-done.10, ...), custom_call_target="tpu_custom_call" | custom-call | flops 1000 | bytes 1000 | tf_op jit(solution)/shard_map/tail_part/pallas_call | solution.py:363
  (76 shorter events, 7.7 us)
Async XLA Ops:
  0.0 13.5 %copy-start.16 = (s32[1,8]{1,0:T(1,128)S(1)}, s32[1,8]{1,0:T(1,128)}, u32[]{:S(2)}) copy-start(s32[1,8]{1,0:T(1,128)} %count_ref.3) | copy-start | bytes 100
  5.4 23.0 %all-to-all-start = ((bf16[16,24,512]{2,1,0:T(8,128)(2,1)}), bf16[16,24,512]{2,1,0:T(8,128)(2,1)S(1)}, u32[]{:S(2)}, u32[]{:S(2)}) async-start(bf16[16,24,512]{2,1,0:T(8,128)(2,1)} %bitcast.30), calls=%async_computation | async-start | bytes 786432 | tf_op jit(solution)/shard_map/all_to_all | solution.py:405
  13.5 1.2 collective-permute-start
  14.7 3.6 %collective-permute-start.1 = (s32[2,8]{1,0:T(2,128)S(1)}, s32[2,8]{1,0:T(2,128)S(1)}, u32[]{:S(2)}, u32[]{:S(2)}) collective-permute-start(s32[2,8]{1,0:T(2,128)S(1)} %pad_add_fusion.2), channel_id=1, source_target_pairs={{0,32},{16,48},{32,0},{48,16},{64,96},{80,112},{96,64},{112,80},{1... | collective-permute-start | bytes 200 | tf_op jit(solution)/shard_map/ppermute | solution.py:399
  18.4 9.5 %collective-permute-start.2 = (s32[4,8]{1,0:T(4,128)S(1)}, s32[4,8]{1,0:T(4,128)S(1)}, u32[]{:S(2)}, u32[]{:S(2)}) collective-permute-start(s32[4,8]{1,0:T(4,128)S(1)} %pad_add_fusion.1), channel_id=1, source_target_pairs={{0,64},{16,80},{32,96},{48,112},{64,0},{80,16},{96,32},{112,48},{1... | collective-permute-start | bytes 392 | tf_op jit(solution)/shard_map/ppermute | solution.py:399
  19.9 8.0 %copy-start.17 = (s32[1,8]{1,0:T(1,128)S(1)}, s32[1,8]{1,0:T(1,128)}, u32[]{:S(2)}) copy-start(s32[1,8]{1,0:T(1,128)} %count_ref.3) | copy-start | bytes 100
  28.5 0.8 copy-start.2
  29.2 44.6 %all-to-all-start.1 = ((bf16[8,256,512]{2,1,0:T(8,128)(2,1)}), bf16[8,256,512]{2,1,0:T(8,128)(2,1)S(1)}, u32[]{:S(2)}, u32[]{:S(2)}) async-start(bf16[8,256,512]{2,1,0:T(8,128)(2,1)} %bitcast.21), calls=%async_computation.1 | async-start | bytes 4194304 | tf_op jit(solution)/shard_map/all_to_all | solution.py:408
  37.2 21.4 %collective-permute-start.5 = (bf16[64,512]{1,0:T(8,128)(2,1)}, bf16[64,512]{1,0:T(8,128)(2,1)S(1)}, u32[]{:S(2)}, u32[]{:S(2)}) collective-permute-start(bf16[64,512]{1,0:T(8,128)(2,1)} %get-tuple-element.25), channel_id=1, source_target_pairs={{3,0},{0,1},{1,2},{2,3},{7,4},{4,5},{5,6},{6,7},{11,8},{8,9},{9,10... | collective-permute-start | bytes 196616 | tf_op jit(solution)/shard_map/ppermute | solution.py:379
  38.1 20.4 %collective-permute-start.4 = (bf16[64,512]{1,0:T(8,128)(2,1)}, bf16[64,512]{1,0:T(8,128)(2,1)S(1)}, u32[]{:S(2)}, u32[]{:S(2)}) collective-permute-start(bf16[64,512]{1,0:T(8,128)(2,1)} %get-tuple-element.25), channel_id=1, source_target_pairs={{2,0},{3,1},{0,2},{1,3},{6,4},{7,5},{4,6},{5,7},{10,8},{11,9},{8,1... | collective-permute-start | bytes 196616 | tf_op jit(solution)/shard_map/ppermute | solution.py:379
  40.7 15.3 %collective-permute-start.3 = (bf16[64,512]{1,0:T(8,128)(2,1)}, bf16[64,512]{1,0:T(8,128)(2,1)S(1)}, u32[]{:S(2)}, u32[]{:S(2)}) collective-permute-start(bf16[64,512]{1,0:T(8,128)(2,1)} %get-tuple-element.25), channel_id=1, source_target_pairs={{1,0},{2,1},{3,2},{0,3},{5,4},{6,5},{7,6},{4,7},{9,8},{10,9},{11,1... | collective-permute-start | bytes 196616 | tf_op jit(solution)/shard_map/ppermute | solution.py:379
  42.6 11.6 %collective-permute-start.11 = (bf16[64,512]{1,0:T(8,128)(2,1)}, bf16[64,512]{1,0:T(8,128)(2,1)S(1)}, u32[]{:S(2)}, u32[]{:S(2)}) collective-permute-start(bf16[64,512]{1,0:T(8,128)(2,1)} %get-tuple-element.26), channel_id=1, source_target_pairs={{12,0},{13,1},{14,2},{15,3},{0,4},{1,5},{2,6},{3,7},{4,8},{5,9},{6... | collective-permute-start | bytes 196616 | tf_op jit(solution)/shard_map/ppermute | solution.py:379
  43.8 4.5 %collective-permute-start.9 = (bf16[64,512]{1,0:T(8,128)(2,1)}, bf16[64,512]{1,0:T(8,128)(2,1)S(1)}, u32[]{:S(2)}, u32[]{:S(2)}) collective-permute-start(bf16[64,512]{1,0:T(8,128)(2,1)} %get-tuple-element.26), channel_id=1, source_target_pairs={{4,0},{5,1},{6,2},{7,3},{8,4},{9,5},{10,6},{11,7},{12,8},{13,9},{1... | collective-permute-start | bytes 196616 | tf_op jit(solution)/shard_map/ppermute | solution.py:379
  48.3 6.0 %collective-permute-start.10 = (bf16[64,512]{1,0:T(8,128)(2,1)}, bf16[64,512]{1,0:T(8,128)(2,1)S(1)}, u32[]{:S(2)}, u32[]{:S(2)}) collective-permute-start(bf16[64,512]{1,0:T(8,128)(2,1)} %get-tuple-element.26), channel_id=1, source_target_pairs={{8,0},{9,1},{10,2},{11,3},{12,4},{13,5},{14,6},{15,7},{0,8},{1,9},... | collective-permute-start | bytes 196616 | tf_op jit(solution)/shard_map/ppermute | solution.py:379
  54.3 19.6 %copy-start.7 = (bf16[256,512]{1,0:T(8,128)(2,1)}, bf16[256,512]{1,0:T(8,128)(2,1)S(1)}, u32[]{:S(2)}) copy-start(bf16[256,512]{1,0:T(8,128)(2,1)S(1)} %constant_dynamic-update-slice_fusion.4.refs_4_) | copy-start | bytes 786436
  54.3 12.4 %collective-permute-start.14 = (bf16[256,512]{1,0:T(8,128)(2,1)S(1)}, bf16[256,512]{1,0:T(8,128)(2,1)S(1)}, u32[]{:S(2)}, u32[]{:S(2)}) collective-permute-start(bf16[256,512]{1,0:T(8,128)(2,1)S(1)} %constant_dynamic-update-slice_fusion.4.refs_4_), channel_id=1, source_target_pairs={{3,0},{0,1},{1,2},{2,3},{7,4},{4,5},{5,6},{6,7},{11,8},{8,9},{9,10... | collective-permute-start | bytes 786440 | tf_op jit(solution)/shard_map/ppermute | solution.py:379
  55.8 14.2 %collective-permute-start.13 = (bf16[256,512]{1,0:T(8,128)(2,1)S(1)}, bf16[256,512]{1,0:T(8,128)(2,1)S(1)}, u32[]{:S(2)}, u32[]{:S(2)}) collective-permute-start(bf16[256,512]{1,0:T(8,128)(2,1)S(1)} %constant_dynamic-update-slice_fusion.4.refs_4_), channel_id=1, source_target_pairs={{2,0},{3,1},{0,2},{1,3},{6,4},{7,5},{4,6},{5,7},{10,8},{11,9},{8,1... | collective-permute-start | bytes 786440 | tf_op jit(solution)/shard_map/ppermute | solution.py:379
  56.1 13.9 %collective-permute-start.12 = (bf16[256,512]{1,0:T(8,128)(2,1)S(1)}, bf16[256,512]{1,0:T(8,128)(2,1)S(1)}, u32[]{:S(2)}, u32[]{:S(2)}) collective-permute-start(bf16[256,512]{1,0:T(8,128)(2,1)S(1)} %constant_dynamic-update-slice_fusion.4.refs_4_), channel_id=1, source_target_pairs={{1,0},{2,1},{3,2},{0,3},{5,4},{6,5},{7,6},{4,7},{9,8},{10,9},{11,1... | collective-permute-start | bytes 786440 | tf_op jit(solution)/shard_map/ppermute | solution.py:379
  58.6 15.3 %copy-start.6 = (bf16[256,512]{1,0:T(8,128)(2,1)}, bf16[256,512]{1,0:T(8,128)(2,1)S(1)}, u32[]{:S(2)}) copy-start(bf16[256,512]{1,0:T(8,128)(2,1)S(1)} %constant_dynamic-update-slice_fusion.refs_0_) | copy-start | bytes 786436
  58.6 11.4 %collective-permute-start.8 = (bf16[256,512]{1,0:T(8,128)(2,1)S(1)}, bf16[256,512]{1,0:T(8,128)(2,1)}, u32[]{:S(2)}, u32[]{:S(2)}) collective-permute-start(bf16[256,512]{1,0:T(8,128)(2,1)S(1)} %constant_dynamic-update-slice_fusion.refs_0_), channel_id=1, source_target_pairs={{12,0},{13,1},{14,2},{15,3},{0,4},{1,5},{2,6},{3,7},{4,8},{5,9},{6... | collective-permute-start | bytes 786440 | tf_op jit(solution)/shard_map/ppermute | solution.py:379
  59.7 11.2 %collective-permute-start.7 = (bf16[256,512]{1,0:T(8,128)(2,1)S(1)}, bf16[256,512]{1,0:T(8,128)(2,1)}, u32[]{:S(2)}, u32[]{:S(2)}) collective-permute-start(bf16[256,512]{1,0:T(8,128)(2,1)S(1)} %constant_dynamic-update-slice_fusion.refs_0_), channel_id=1, source_target_pairs={{8,0},{9,1},{10,2},{11,3},{12,4},{13,5},{14,6},{15,7},{0,8},{1,9},... | collective-permute-start | bytes 786440 | tf_op jit(solution)/shard_map/ppermute | solution.py:379
  66.7 7.2 %copy-start.13 = (bf16[256,512]{1,0:T(8,128)(2,1)}, bf16[256,512]{1,0:T(8,128)(2,1)S(1)}, u32[]{:S(2)}) copy-start(bf16[256,512]{1,0:T(8,128)(2,1)S(1)} %collective-permute-done.14.refs_7_) | copy-start | bytes 786436
  66.7 7.2 %collective-permute-start.6 = (bf16[256,512]{1,0:T(8,128)(2,1)S(1)}, bf16[256,512]{1,0:T(8,128)(2,1)}, u32[]{:S(2)}, u32[]{:S(2)}) collective-permute-start(bf16[256,512]{1,0:T(8,128)(2,1)S(1)} %constant_dynamic-update-slice_fusion.refs_0_), channel_id=1, source_target_pairs={{4,0},{5,1},{6,2},{7,3},{8,4},{9,5},{10,6},{11,7},{12,8},{13,9},{1... | collective-permute-start | bytes 786440 | tf_op jit(solution)/shard_map/ppermute | solution.py:379
  70.0 3.9 %copy-start.14 = (bf16[256,512]{1,0:T(8,128)(2,1)}, bf16[256,512]{1,0:T(8,128)(2,1)S(1)}, u32[]{:S(2)}) copy-start(bf16[256,512]{1,0:T(8,128)(2,1)S(1)} %collective-permute-done.13.refs_6_) | copy-start | bytes 786436
  70.0 3.9 %copy-start.15 = (bf16[256,512]{1,0:T(8,128)(2,1)}, bf16[256,512]{1,0:T(8,128)(2,1)S(1)}, u32[]{:S(2)}) copy-start(bf16[256,512]{1,0:T(8,128)(2,1)S(1)} %collective-permute-done.12.refs_5_) | copy-start | bytes 786436
  73.9 1.3 copy-start
  94.0 23.3 %all-to-all-start.2 = ((bf16[16,24,512]{2,1,0:T(8,128)(2,1)}), bf16[16,24,512]{2,1,0:T(8,128)(2,1)S(1)}, u32[]{:S(2)}, u32[]{:S(2)}) async-start(bf16[16,24,512]{2,1,0:T(8,128)(2,1)} %bitcast.31), calls=%async_computation.2 | async-start | bytes 786432 | tf_op jit(solution)/shard_map/all_to_all | solution.py:405
  117.3 0.8 copy-start.3
  118.1 43.6 %all-to-all-start.3 = ((bf16[8,256,512]{2,1,0:T(8,128)(2,1)}), bf16[8,256,512]{2,1,0:T(8,128)(2,1)S(1)}, u32[]{:S(2)}, u32[]{:S(2)}) async-start(bf16[8,256,512]{2,1,0:T(8,128)(2,1)} %bitcast.22), calls=%async_computation.3 | async-start | bytes 4194304 | tf_op jit(solution)/shard_map/all_to_all | solution.py:408
  124.9 21.6 %collective-permute-start.17 = (bf16[64,512]{1,0:T(8,128)(2,1)}, bf16[64,512]{1,0:T(8,128)(2,1)S(1)}, u32[]{:S(2)}, u32[]{:S(2)}) collective-permute-start(bf16[64,512]{1,0:T(8,128)(2,1)} %get-tuple-element.34), channel_id=1, source_target_pairs={{3,0},{0,1},{1,2},{2,3},{7,4},{4,5},{5,6},{6,7},{11,8},{8,9},{9,10... | collective-permute-start | bytes 196616 | tf_op jit(solution)/shard_map/ppermute | solution.py:379
  126.1 20.3 %collective-permute-start.16 = (bf16[64,512]{1,0:T(8,128)(2,1)}, bf16[64,512]{1,0:T(8,128)(2,1)S(1)}, u32[]{:S(2)}, u32[]{:S(2)}) collective-permute-start(bf16[64,512]{1,0:T(8,128)(2,1)} %get-tuple-element.34), channel_id=1, source_target_pairs={{2,0},{3,1},{0,2},{1,3},{6,4},{7,5},{4,6},{5,7},{10,8},{11,9},{8,1... | collective-permute-start | bytes 196616 | tf_op jit(solution)/shard_map/ppermute | solution.py:379
  129.0 15.7 %collective-permute-start.15 = (bf16[64,512]{1,0:T(8,128)(2,1)}, bf16[64,512]{1,0:T(8,128)(2,1)S(1)}, u32[]{:S(2)}, u32[]{:S(2)}) collective-permute-start(bf16[64,512]{1,0:T(8,128)(2,1)} %get-tuple-element.34), channel_id=1, source_target_pairs={{1,0},{2,1},{3,2},{0,3},{5,4},{6,5},{7,6},{4,7},{9,8},{10,9},{11,1... | collective-permute-start | bytes 196616 | tf_op jit(solution)/shard_map/ppermute | solution.py:379
  130.3 12.8 %collective-permute-start.23 = (bf16[64,512]{1,0:T(8,128)(2,1)}, bf16[64,512]{1,0:T(8,128)(2,1)S(1)}, u32[]{:S(2)}, u32[]{:S(2)}) collective-permute-start(bf16[64,512]{1,0:T(8,128)(2,1)} %get-tuple-element.35), channel_id=1, source_target_pairs={{12,0},{13,1},{14,2},{15,3},{0,4},{1,5},{2,6},{3,7},{4,8},{5,9},{6... | collective-permute-start | bytes 196616 | tf_op jit(solution)/shard_map/ppermute | solution.py:379
  132.6 4.5 %collective-permute-start.21 = (bf16[64,512]{1,0:T(8,128)(2,1)}, bf16[64,512]{1,0:T(8,128)(2,1)S(1)}, u32[]{:S(2)}, u32[]{:S(2)}) collective-permute-start(bf16[64,512]{1,0:T(8,128)(2,1)} %get-tuple-element.35), channel_id=1, source_target_pairs={{4,0},{5,1},{6,2},{7,3},{8,4},{9,5},{10,6},{11,7},{12,8},{13,9},{1... | collective-permute-start | bytes 196616 | tf_op jit(solution)/shard_map/ppermute | solution.py:379
  137.1 6.0 %collective-permute-start.22 = (bf16[64,512]{1,0:T(8,128)(2,1)}, bf16[64,512]{1,0:T(8,128)(2,1)S(1)}, u32[]{:S(2)}, u32[]{:S(2)}) collective-permute-start(bf16[64,512]{1,0:T(8,128)(2,1)} %get-tuple-element.35), channel_id=1, source_target_pairs={{8,0},{9,1},{10,2},{11,3},{12,4},{13,5},{14,6},{15,7},{0,8},{1,9},... | collective-permute-start | bytes 196616 | tf_op jit(solution)/shard_map/ppermute | solution.py:379
  143.1 18.6 %copy-start.5 = (bf16[256,512]{1,0:T(8,128)(2,1)}, bf16[256,512]{1,0:T(8,128)(2,1)S(1)}, u32[]{:S(2)}) copy-start(bf16[256,512]{1,0:T(8,128)(2,1)S(1)} %constant_dynamic-update-slice_fusion.12.refs_4_) | copy-start | bytes 786436
  143.1 12.1 %collective-permute-start.26 = (bf16[256,512]{1,0:T(8,128)(2,1)S(1)}, bf16[256,512]{1,0:T(8,128)(2,1)S(1)}, u32[]{:S(2)}, u32[]{:S(2)}) collective-permute-start(bf16[256,512]{1,0:T(8,128)(2,1)S(1)} %constant_dynamic-update-slice_fusion.12.refs_4_), channel_id=1, source_target_pairs={{3,0},{0,1},{1,2},{2,3},{7,4},{4,5},{5,6},{6,7},{11,8},{8,9},{9,10... | collective-permute-start | bytes 786440 | tf_op jit(solution)/shard_map/ppermute | solution.py:379
  143.3 14.0 %collective-permute-start.25 = (bf16[256,512]{1,0:T(8,128)(2,1)S(1)}, bf16[256,512]{1,0:T(8,128)(2,1)S(1)}, u32[]{:S(2)}, u32[]{:S(2)}) collective-permute-start(bf16[256,512]{1,0:T(8,128)(2,1)S(1)} %constant_dynamic-update-slice_fusion.12.refs_4_), channel_id=1, source_target_pairs={{2,0},{3,1},{0,2},{1,3},{6,4},{7,5},{4,6},{5,7},{10,8},{11,9},{8,1... | collective-permute-start | bytes 786440 | tf_op jit(solution)/shard_map/ppermute | solution.py:379
  144.6 12.7 %collective-permute-start.24 = (bf16[256,512]{1,0:T(8,128)(2,1)S(1)}, bf16[256,512]{1,0:T(8,128)(2,1)S(1)}, u32[]{:S(2)}, u32[]{:S(2)}) collective-permute-start(bf16[256,512]{1,0:T(8,128)(2,1)S(1)} %constant_dynamic-update-slice_fusion.12.refs_4_), channel_id=1, source_target_pairs={{1,0},{2,1},{3,2},{0,3},{5,4},{6,5},{7,6},{4,7},{9,8},{10,9},{11,1... | collective-permute-start | bytes 786440 | tf_op jit(solution)/shard_map/ppermute | solution.py:379
  146.5 15.3 %copy-start.4 = (bf16[256,512]{1,0:T(8,128)(2,1)}, bf16[256,512]{1,0:T(8,128)(2,1)S(1)}, u32[]{:S(2)}) copy-start(bf16[256,512]{1,0:T(8,128)(2,1)S(1)} %constant_dynamic-update-slice_fusion.8.refs_0_) | copy-start | bytes 786436
  146.5 10.9 %collective-permute-start.20 = (bf16[256,512]{1,0:T(8,128)(2,1)S(1)}, bf16[256,512]{1,0:T(8,128)(2,1)S(1)}, u32[]{:S(2)}, u32[]{:S(2)}) collective-permute-start(bf16[256,512]{1,0:T(8,128)(2,1)S(1)} %constant_dynamic-update-slice_fusion.8.refs_0_), channel_id=1, source_target_pairs={{12,0},{13,1},{14,2},{15,3},{0,4},{1,5},{2,6},{3,7},{4,8},{5,9},{6... | collective-permute-start | bytes 786440 | tf_op jit(solution)/shard_map/ppermute | solution.py:379
  147.6 11.0 %collective-permute-start.19 = (bf16[256,512]{1,0:T(8,128)(2,1)S(1)}, bf16[256,512]{1,0:T(8,128)(2,1)S(1)}, u32[]{:S(2)}, u32[]{:S(2)}) collective-permute-start(bf16[256,512]{1,0:T(8,128)(2,1)S(1)} %constant_dynamic-update-slice_fusion.8.refs_0_), channel_id=1, source_target_pairs={{8,0},{9,1},{10,2},{11,3},{12,4},{13,5},{14,6},{15,7},{0,8},{1,9},... | collective-permute-start | bytes 786440 | tf_op jit(solution)/shard_map/ppermute | solution.py:379
  155.2 6.5 %copy-start.8 = (bf16[256,512]{1,0:T(8,128)(2,1)}, bf16[256,512]{1,0:T(8,128)(2,1)S(1)}, u32[]{:S(2)}) copy-start(bf16[256,512]{1,0:T(8,128)(2,1)S(1)} %collective-permute-done.26.refs_7_) | copy-start | bytes 786436
  155.2 6.5 %collective-permute-start.18 = (bf16[256,512]{1,0:T(8,128)(2,1)S(1)}, bf16[256,512]{1,0:T(8,128)(2,1)}, u32[]{:S(2)}, u32[]{:S(2)}) collective-permute-start(bf16[256,512]{1,0:T(8,128)(2,1)S(1)} %constant_dynamic-update-slice_fusion.8.refs_0_), channel_id=1, source_target_pairs={{4,0},{5,1},{6,2},{7,3},{8,4},{9,5},{10,6},{11,7},{12,8},{13,9},{1... | collective-permute-start | bytes 786440 | tf_op jit(solution)/shard_map/ppermute | solution.py:379
  157.3 4.4 %copy-start.9 = (bf16[256,512]{1,0:T(8,128)(2,1)}, bf16[256,512]{1,0:T(8,128)(2,1)S(1)}, u32[]{:S(2)}) copy-start(bf16[256,512]{1,0:T(8,128)(2,1)S(1)} %collective-permute-done.25.refs_6_) | copy-start | bytes 786436
  157.4 4.4 %copy-start.10 = (bf16[256,512]{1,0:T(8,128)(2,1)}, bf16[256,512]{1,0:T(8,128)(2,1)S(1)}, u32[]{:S(2)}) copy-start(bf16[256,512]{1,0:T(8,128)(2,1)S(1)} %collective-permute-done.24.refs_5_) | copy-start | bytes 786436
  157.4 1.3 copy-start.11
  161.7 1.4 copy-start.1
  (1 other events, 0.7 us)

commit v3 on v2

--- a/solution.py
+++ b/solution.py
@@ -16,6 +16,7 @@
 COLS = 16
 SIDE = 4
 HALO = 256
+NOTE = 16
 HUBS = 2048
 PAIR = 24
 SHARE = 128
@@ -168,15 +169,16 @@
         in_specs=[vmem(), vmem()],
         out_specs=[vmem(), vmem()],
         out_shape=[half, half],
-        compiler_params=params(60),
+        compiler_params=params(8),
         cost_estimate=cost(),
         name="hub_keep",
     )(keep_index, arrived)
 
 
-def halo_kernel(rows_ref, count_ref, table_ref, out_ref, held, wide, picked, staged, sem, out_sem):
+def halo_kernel(noted, rows_ref, count_ref, table_ref, out_ref, held, wide, picked, staged, sem, out_sem):
     lanes = 4
     unroll = 32
+    height = HALO + (NOTE if noted else 0)
     copies = load_table(table_ref, held, sem)
     chunk = held.shape[0] // SIDE
     for k in range(SIDE):
@@ -189,7 +191,7 @@
 
     out = [
         pltpu.make_async_copy(
-            staged.at[pl.ds(peer * HALO, HALO)], out_ref.at[pl.ds(peer * HALO, HALO)], out_sem.at[peer]
+            staged.at[pl.ds(peer * height, height)], out_ref.at[pl.ds(peer * height, height)], out_sem.at[peer]
         )
         for peer in range(ROWS)
     ]
@@ -200,32 +202,36 @@
         def _(group):
             for u in range(unroll):
                 slot = group * unroll + u
-                move_row(wide, rows_ref[peer, slot], picked, slot)
+                move_row(wide, rows_ref[peer * HALO + slot], picked, slot)
 
         for half in range(HALO // TB):
             live = iota((TB, TB), 0) + half * TB < count
-            top = peer * HALO + half * TB
+            top = peer * height + half * TB
             for j in range(lanes):
                 part = picked[pl.ds(half * TB * lanes + j, TB, stride=lanes), :]
                 staged[top : top + TB, j * TB : (j + 1) * TB] = jnp.where(live, part, 0.0).astype(BF16)
+        if noted:
+            top = peer * height + HALO
+            staged[top : top + NOTE, :] = jnp.full((NOTE, lanes * TB), count, I32).astype(F32).astype(BF16)
         out[peer].start()
     for copy in out:
         copy.wait()
 
 
-def halo_start(rows, count, table):
+def halo_start(noted, rows, count, table):
     nodes, width = table.shape
+    height = ROWS * (HALO + (NOTE if noted else 0))
     lanes = width // TB
     return pl.pallas_call(
-        halo_kernel,
+        functools.partial(halo_kernel, noted),
         in_specs=[smem(), smem(), hbm()],
         out_specs=hbm(),
-        out_shape=shape(BF16, ROWS * HALO, width),
+        out_shape=shape(BF16, height, width),
         scratch_shapes=[
             pltpu.VMEM((nodes, width), BF16),
             pltpu.VMEM((nodes * lanes, TB), F32),
             pltpu.VMEM((HALO * lanes, TB), F32),
-            pltpu.VMEM((ROWS * HALO, width), BF16),
+            pltpu.VMEM((height, width), BF16),
             pltpu.SemaphoreType.DMA((SIDE,)),
             pltpu.SemaphoreType.DMA((ROWS,)),
         ],
@@ -256,26 +262,28 @@
 
 def tail_kernel(last, *refs):
     pieces = refs[:8]
-    row_ref, count_ref, cols_ref, far_ref, pos_ref = refs[8:13]
-    halo_ref, table_ref, tiles_ref, far_tiles_ref, weight_ref = refs[13:18]
-    rest = refs[18:]
+    cols_ref, far_ref, pos_ref, halo_ref, table_ref, tiles_ref, far_tiles_ref, weight_ref = refs[8:16]
+    rest = refs[16:]
     if last:
-        out_ref = rest[0]
-        rest = rest[1:]
+        counts, out_ref = rest[:2]
+        rest = rest[2:]
     else:
-        send_ref, out_ref, picked_ref, total = rest[:3] + rest[-1:]
-        rest = rest[3:-1]
+        send_ref, out_ref, picked_ref, counts = rest[:4]
+        notes, total = rest[-2:]
+        rest = rest[4:-2]
     held, wide, placed, store, table, tiles, far_tiles, weight, joined, result, sem, out_sem = rest
     lanes = 4
     size = HUBS // 8
     width = store.shape[1]
     halo_rows = ROWS * HALO
+    height = halo_ref.shape[0] // ROWS
     pairs = [(pieces[k], held.at[pl.ds(k * size, size)]) for k in range(8)]
-    pairs.append((table_ref, table))
+    pairs += [(table_ref, table), (tiles_ref, tiles), (far_tiles_ref, far_tiles)]
+    for p in range(ROWS):
+        pairs.append((halo_ref.at[pl.ds(p * height, HALO)], store.at[pl.ds(p * HALO, HALO)]))
+        if not last:
+            pairs.append((halo_ref.at[pl.ds(p * height + HALO, NOTE)], notes.at[pl.ds(p * NOTE, NOTE)]))
     pairs.append((weight_ref, weight))
-    pairs.append((tiles_ref, tiles))
-    pairs.append((halo_ref, store.at[pl.ds(0, halo_rows)]))
-    pairs.append((far_tiles_ref, far_tiles))
     copies = start_chunks(pairs, sem)
     for k in range(8):
         copies[k].wait()
@@ -293,9 +301,12 @@
         store[halo_rows : halo_rows + HUBS, j * TB : (j + 1) * TB] = placed[pl.ds(j, HUBS, stride=lanes), :].astype(BF16)
     for copy in copies[8:]:
         copy.wait()
+    if not last:
+        for p in range(ROWS):
+            counts[p : p + 1, :] = notes[p * NOTE : (p + 1) * NOTE, 0:TB].astype(F32)[0:1, :]
+        counts[ROWS : 2 * ROWS, :] = jnp.full((ROWS, TB), 1024.0, F32)
     out = chunk_copies(result, out_ref, out_sem)
     group = TALL // TB
-    my_row = row_ref[0]
     for k in range(result.shape[0] // TALL):
         for b in range(group):
             block = k * group + b
@@ -306,10 +317,9 @@
             mass = near[0].astype(F32) + near[1].astype(F32)
             for t in range(2):
                 col = far_ref[t, block]
-                peer = lax.bitwise_and(lax.shift_right_logical(col, 1), ROWS - 1)
-                count = count_ref[lax.bitwise_xor(peer, my_row), my_row]
-                live = jnp.where(col < 2 * ROWS, count - lax.bitwise_and(col, 1) * TB, TB)
-                mass = mass + jnp.where(iota((TB, TB), 1) < live, far[t].astype(F32), 0.0)
+                peer = jnp.minimum(lax.shift_right_logical(col, 1), ROWS)
+                slots = (iota((1, TB), 1) + lax.bitwise_and(col, 1) * TB).astype(F32)
+                mass = mass + jnp.where(slots < counts[pl.ds(peer, 1), :], far[t].astype(F32), 0.0)
             inverse = 1.0 / jnp.sum(mass, axis=1, keepdims=True)
             joined[b * TB : (b + 1) * TB, width : 2 * width] = (total_rows * inverse).astype(BF16)
         span = slice(k * TALL, (k + 1) * TALL)
@@ -332,11 +342,11 @@
         copy.wait()
 
 
-def tail_part(last, hubs, row, count, cols, far_cols, pos, halos, table, tiles, far_tiles, weight, send=None):
+def tail_part(last, hubs, cols, far_cols, pos, halos, table, tiles, far_tiles, weight, extra):
     nodes, width = table.shape
     lanes = width // TB
-    in_specs = [hbm()] * 8 + [smem()] * 5 + [hbm()] * 5
-    args = [*hubs, row, count, cols, far_cols, pos, halos, table, tiles, far_tiles, weight]
+    in_specs = [hbm()] * 8 + [smem()] * 3 + [hbm()] * 5 + [vmem()]
+    args = [*hubs, cols, far_cols, pos, halos, table, tiles, far_tiles, weight, extra]
     out_specs = [hbm()]
     out_shape = [shape(BF16, nodes, width)]
     scratch = [
@@ -350,23 +360,21 @@
         pltpu.VMEM(weight.shape, BF16),
         pltpu.VMEM((TALL, 2 * width), BF16),
         pltpu.VMEM((nodes, width), BF16),
-        pltpu.SemaphoreType.DMA((13,)),
+        pltpu.SemaphoreType.DMA((32,)),
         pltpu.SemaphoreType.DMA((nodes // TALL,)),
     ]
     if not last:
         sent = COLS * PAIR
-        in_specs.append(vmem())
-        args.append(send)
-        out_specs.append(vmem())
-        out_shape.append(shape(BF16, sent, width))
-        scratch.append(pltpu.VMEM((sent, width), F32))
+        out_specs += [vmem(), vmem()]
+        out_shape += [shape(BF16, sent, width), shape(F32, 2 * ROWS, TB)]
+        scratch += [pltpu.VMEM((ROWS * NOTE, width), BF16), pltpu.VMEM((sent, width), F32)]
     return pl.pallas_call(
         functools.partial(tail_kernel, last),
         in_specs=in_specs,
         out_specs=out_specs,
         out_shape=out_shape,
         scratch_shapes=scratch,
-        compiler_params=params(60),
+        compiler_params=params(54),
         cost_estimate=cost(),
         name="tail_part",
     )(*args)
@@ -392,20 +400,12 @@
     return left + right
 
 
-def share_counts(count):
-    table = count
-    for bit in (1, 2, 4):
-        pairs = [(i, i ^ bit) for i in range(ROWS)]
-        table = jnp.concatenate([table, lax.ppermute(table, "row", pairs)], axis=0)
-    return table
-
-
 def exchange(picked, keep, outgoing):
     width = picked.shape[1]
     arrived = lax.all_to_all(picked.reshape(COLS, PAIR, width), "col", 0, 0, tiled=True)
     arrived, outgoing = lax.optimization_barrier((arrived.reshape(-1, width), outgoing))
     hubs = spread_hubs(*hub_keep(keep, arrived))
-    halos = lax.all_to_all(outgoing.reshape(ROWS, HALO, width), "row", 0, 0, tiled=True)
+    halos = lax.all_to_all(outgoing.reshape(ROWS, -1, width), "row", 0, 0, tiled=True)
     return hubs, halos.reshape(-1, width)
 
 
@@ -422,20 +422,18 @@
     remote_cols,
     remote_tiles,
 ):
-    my_row = lax.axis_index("row").astype(I32).reshape(1)
     my_col = lax.axis_index("col").astype(I32).reshape(1)
-    rows = send_rows[0]
+    rows = send_rows.reshape(-1)
     cols = local_cols[0].T
     far_cols = remote_cols[0].T
     tiles, far_tiles = local_tiles[0], remote_tiles[0]
-    counts = share_counts(halo_count)
     picked, send, keep, pos = hub_start(my_col, hub_owner.reshape(1, -1), hub_row, features)
-    outgoing, counts = lax.optimization_barrier((halo_start(rows, halo_count, features), counts))
-    hubs, halos = exchange(picked, keep, outgoing)
-    shared = (my_row, counts, cols, far_cols, pos)
-    middle, picked = tail_part(False, hubs, *shared, halos, features, tiles, far_tiles, w_first, send)
-    hubs, halos = exchange(picked, keep, halo_start(rows, halo_count, middle))
-    return tail_part(True, hubs, *shared, halos, middle, tiles, far_tiles, w_second)[0]
+    hubs, halos = exchange(picked, keep, halo_start(True, rows, halo_count, features))
+    middle, picked, counts = tail_part(
+        False, hubs, cols, far_cols, pos, halos, features, tiles, far_tiles, w_first, send
+    )
+    hubs, halos = exchange(picked, keep, halo_start(False, rows, halo_count, middle))
+    return tail_part(True, hubs, cols, far_cols, pos, halos, middle, tiles, far_tiles, w_second, counts)[0]
 
 
 def solution(mesh):

time: 182 us -> 156 us (0.86); the launches traced: 179 us -> 156 us
  Pallas kernels: 70.3 us -> 53.9 us
  local copies, waits for them, and re-layouts: 8.31 us -> 4.81 us
  waiting for transfers between devices: 29.7 us -> 26.2 us
    pallas_call x2, Pallas kernels: 26.1 us -> 12.7 us  [halo_start(): pl.pallas_call(functools.partial(halo_kernel, noted), in_specs=[smem(), s...]
    all_to_all x2, waiting for transfers between devices: 0.01 us -> 6.2 us  [exchange(): lax.all_to_all(picked.reshape(COLS, PAIR, width), 'col', 0, 0, tiled=True)]
    ppermute x24, waiting for transfers between devices: 25.9 us -> 20 us  [fetch(): return lax.ppermute(array, 'col', pairs)]
    ppermute x3 -> x0, waiting for transfers between devices: 3.85 us -> none  [share_counts(): table = jnp.concatenate([table, lax.ppermute(table, 'row', pairs)], axis=0)]
    unnamed x48 -> x49, local copies, waits for them, and re-layouts: 8.29 us -> 4.78 us
    pallas_call x2, Pallas kernels: 3.89 us -> 0.53 us  [hub_keep(): pl.pallas_call(keep_kernel, in_specs=[vmem(), vmem()], out_specs=[vmem(),...]
    ppermute x24, starting transfers between devices: 43.3 us -> 46.6 us  [fetch(): return lax.ppermute(array, 'col', pairs)]
    ppermute x3 -> x0, starting transfers between devices: 2.48 us -> none  [share_counts(): table = jnp.concatenate([table, lax.ppermute(table, 'row', pairs)], axis=0)]
  transfers between devices with their start and end apart: 31 -> 28, of which waited for: 12 -> 12; matrix products, arithmetic and copies ran while one was open for 2% -> 0% of each run, Pallas kernels for 17% -> 8%
where the time goes in v3:
time: 156 us
  starting transfers between devices  70.2 us (45%)
  Pallas kernels  53.9 us (35%)
  waiting for transfers between devices  26.2 us (17%)
  local copies, waits for them, and re-layouts  4.81 us (3%)
    ppermute x24, starting transfers between devices, fetch(): return lax.ppermute(array, 'col', pairs)  46.6 us
    pallas_call x2, Pallas kernels, tail_part(): pl.pallas_call(functools.partial(tail_kernel, last), in_specs=in_specs, o...  35.3 us
    ppermute x24, waiting for transfers between devices, fetch(): return lax.ppermute(array, 'col', pairs)  20 us
    all_to_all x2, starting transfers between devices, exchange(): lax.all_to_all(picked.reshape(COLS, PAIR, width), 'col', 0, 0, tiled=True)  14.2 us
    pallas_call x2, Pallas kernels, halo_start(): pl.pallas_call(functools.partial(halo_kernel, noted), in_specs=[smem(), s...  12.7 us
    all_to_all x2, starting transfers between devices, exchange(): lax.all_to_all(outgoing.reshape(ROWS, -1, width), 'row', 0, 0, tiled=True)  9.42 us
    all_to_all x2, waiting for transfers between devices, exchange(): lax.all_to_all(picked.reshape(COLS, PAIR, width), 'col', 0, 0, tiled=True)  6.2 us
    pallas_call x1, Pallas kernels, hub_start(): pl.pallas_call(hub_kernel, in_specs=[smem(), vmem(), vmem(), hbm()], out_...  5.43 us
  transfers between devices with their start and end apart: 28, of which 12 were waited for; matrix products, arithmetic and copies ran while one was open for 0% of the time, Pallas kernels for 8%

profile of v3, /device:TPU:6, one launch (start us, length us, event | category | flops | bytes accessed | tf_op | source)
XLA Modules:
  0.0 155.6 jit_solution(12781670618140514170)
XLA Ops:
  0.0 5.4 %hub_start.1 = (bf16[384,512]{1,0:T(8,128)(2,1)}, s32[384,1]{1,0:T(8,128)}, s32[128,1]{1,0:T(8,128)}, s32[16,128]{1,0:T(8,128)}) custom-call(s32[1]{0:T(128)} %bitcast.col_ref, s32[1,2048]{1,0:T(1,128)} %bitcast.34, s32[1,2048]{1,0:T(1,128)} %row_ref.1, bf16[4096,512]{1,0:T(8,128)(2,1)} %refs_12_.1), custom_call_target="tpu_custom_call" | custom-call | flops 1000 | bytes 1000 | tf_op jit(solution)/shard_map/hub_start/pallas_call | solution.py:147
  5.4 8.1 %all-to-all-start = ((bf16[16,24,512]{2,1,0:T(8,128)(2,1)}), bf16[16,24,512]{2,1,0:T(8,128)(2,1)S(1)}, u32[]{:S(2)}, u32[]{:S(2)}) async-start(bf16[16,24,512]{2,1,0:T(8,128)(2,1)} %bitcast.31), calls=%async_computation | async-start | bytes 786432 | tf_op jit(solution)/shard_map/all_to_all | solution.py:405
  13.5 0.6 copy.12
  14.1 6.2 %halo_start.2 = bf16[2176,512]{1,0:T(8,128)(2,1)} custom-call(s32[2048]{0:T(1024)} %bitcast.32, s32[1,8]{1,0:T(1,128)} %count_ref.3, bf16[4096,512]{1,0:T(8,128)(2,1)} %refs_12_.1), custom_call_target="tpu_custom_call" | custom-call | flops 1000 | bytes 1000 | tf_op jit(solution)/shard_map/halo_start/pallas_call | solution.py:225
  20.3 3.2 %all-to-all-done = bf16[16,24,512]{2,1,0:T(8,128)(2,1)S(1)} async-done(((bf16[16,24,512]{2,1,0:T(8,128)(2,1)}), bf16[16,24,512]{2,1,0:T(8,128)(2,1)S(1)}, u32[]{:S(2)}, u32[]{:S(2)}) %all-to-all-start) | async-done | bytes 393248 | tf_op jit(solution)/shard_map/all_to_all | solution.py:405
  23.6 4.9 %all-to-all-start.1 = ((bf16[8,272,512]{2,1,0:T(8,128)(2,1)}), bf16[8,272,512]{2,1,0:T(8,128)(2,1)S(1)}, u32[]{:S(2)}, u32[]{:S(2)}) async-start(bf16[8,272,512]{2,1,0:T(8,128)(2,1)} %bitcast.23), calls=%async_computation.1 | async-start | bytes 4456448 | tf_op jit(solution)/shard_map/all_to_all | solution.py:408
  28.8 0.6 collective-permute-start.2
  29.4 1.5 collective-permute-start.1
  30.9 1.5 collective-permute-start
  32.3 0.6 collective-permute-start.8
  32.9 2.7 %collective-permute-start.6 = (bf16[64,512]{1,0:T(8,128)(2,1)S(1)}, bf16[64,512]{1,0:T(8,128)(2,1)S(1)}, u32[]{:S(2)}, u32[]{:S(2)}) collective-permute-start(bf16[64,512]{1,0:T(8,128)(2,1)S(1)} %get-tuple-element.24), channel_id=1, source_target_pairs={{4,0},{5,1},{6,2},{7,3},{8,4},{9,5},{10,6},{11,7},{12,8},{13,9},{1... | collective-permute-start | bytes 196616 | tf_op jit(solution)/shard_map/ppermute | solution.py:387
  35.6 1.9 %collective-permute-done.6 = bf16[64,512]{1,0:T(8,128)(2,1)S(1)} collective-permute-done((bf16[64,512]{1,0:T(8,128)(2,1)S(1)}, bf16[64,512]{1,0:T(8,128)(2,1)S(1)}, u32[]{:S(2)}, u32[]{:S(2)}) %collective-permute-start.6) | collective-permute-done | bytes 65568 | tf_op jit(solution)/shard_map/ppermute | solution.py:387
  37.5 2.4 %collective-permute-start.7 = (bf16[64,512]{1,0:T(8,128)(2,1)S(1)}, bf16[64,512]{1,0:T(8,128)(2,1)S(1)}, u32[]{:S(2)}, u32[]{:S(2)}) collective-permute-start(bf16[64,512]{1,0:T(8,128)(2,1)S(1)} %get-tuple-element.24), channel_id=1, source_target_pairs={{8,0},{9,1},{10,2},{11,3},{12,4},{13,5},{14,6},{15,7},{0,8},{1,9},... | collective-permute-start | bytes 196616 | tf_op jit(solution)/shard_map/ppermute | solution.py:387
  39.8 3.4 %collective-permute-done.7 = bf16[64,512]{1,0:T(8,128)(2,1)S(1)} collective-permute-done((bf16[64,512]{1,0:T(8,128)(2,1)S(1)}, bf16[64,512]{1,0:T(8,128)(2,1)S(1)}, u32[]{:S(2)}, u32[]{:S(2)}) %collective-permute-start.7) | collective-permute-done | bytes 65568 | tf_op jit(solution)/shard_map/ppermute | solution.py:387
  43.3 0.7 collective-permute-start.11
  44.0 2.2 %collective-permute-start.10 = (bf16[256,512]{1,0:T(8,128)(2,1)S(1)}, bf16[256,512]{1,0:T(8,128)(2,1)S(1)}, u32[]{:S(2)}, u32[]{:S(2)}) collective-permute-start(bf16[256,512]{1,0:T(8,128)(2,1)S(1)} %constant_dynamic-update-slice_fusion.4.refs_4_), channel_id=1, source_target_pairs={{2,0},{3,1},{0,2},{1,3},{6,4},{7,5},{4,6},{5,7},{10,8},{11,9},{8,1... | collective-permute-start | bytes 786440 | tf_op jit(solution)/shard_map/ppermute | solution.py:387
  46.1 2.5 %collective-permute-start.9 = (bf16[256,512]{1,0:T(8,128)(2,1)S(1)}, bf16[256,512]{1,0:T(8,128)(2,1)S(1)}, u32[]{:S(2)}, u32[]{:S(2)}) collective-permute-start(bf16[256,512]{1,0:T(8,128)(2,1)S(1)} %constant_dynamic-update-slice_fusion.4.refs_4_), channel_id=1, source_target_pairs={{1,0},{2,1},{3,2},{0,3},{5,4},{6,5},{7,6},{4,7},{9,8},{10,9},{11,1... | collective-permute-start | bytes 786440 | tf_op jit(solution)/shard_map/ppermute | solution.py:387
  48.7 1.0 collective-permute-start.5
  49.7 4.1 %collective-permute-start.4 = (bf16[256,512]{1,0:T(8,128)(2,1)S(1)}, bf16[256,512]{1,0:T(8,128)(2,1)S(1)}, u32[]{:S(2)}, u32[]{:S(2)}) collective-permute-start(bf16[256,512]{1,0:T(8,128)(2,1)S(1)} %constant_dynamic-update-slice_fusion.refs_0_), channel_id=1, source_target_pairs={{8,0},{9,1},{10,2},{11,3},{12,4},{13,5},{14,6},{15,7},{0,8},{1,9},... | collective-permute-start | bytes 786440 | tf_op jit(solution)/shard_map/ppermute | solution.py:387
  53.8 1.7 %collective-permute-done.11.refs_7_ = bf16[256,512]{1,0:T(8,128)(2,1)S(1)} collective-permute-done((bf16[256,512]{1,0:T(8,128)(2,1)S(1)}, bf16[256,512]{1,0:T(8,128)(2,1)S(1)}, u32[]{:S(2)}, u32[]{:S(2)}) %collective-permute-start.11) | collective-permute-done | bytes 262176 | tf_op jit(solution)/shard_map/ppermute | solution.py:387
  55.5 3.4 %collective-permute-start.3 = (bf16[256,512]{1,0:T(8,128)(2,1)S(1)}, bf16[256,512]{1,0:T(8,128)(2,1)}, u32[]{:S(2)}, u32[]{:S(2)}) collective-permute-start(bf16[256,512]{1,0:T(8,128)(2,1)S(1)} %constant_dynamic-update-slice_fusion.refs_0_), channel_id=1, source_target_pairs={{4,0},{5,1},{6,2},{7,3},{8,4},{9,5},{10,6},{11,7},{12,8},{13,9},{1... | collective-permute-start | bytes 786440 | tf_op jit(solution)/shard_map/ppermute | solution.py:387
  59.0 2.8 %collective-permute-done.4.refs_2_ = bf16[256,512]{1,0:T(8,128)(2,1)S(1)} collective-permute-done((bf16[256,512]{1,0:T(8,128)(2,1)S(1)}, bf16[256,512]{1,0:T(8,128)(2,1)S(1)}, u32[]{:S(2)}, u32[]{:S(2)}) %collective-permute-start.4) | collective-permute-done | bytes 262176 | tf_op jit(solution)/shard_map/ppermute | solution.py:387
  61.8 0.7 copy-done.16
  62.9 1.3 copy-done.1
  64.2 19.0 %tail_part.2 = (bf16[4096,512]{1,0:T(8,128)(2,1)}, bf16[384,512]{1,0:T(8,128)(2,1)}, f32[16,128]{1,0:T(8,128)}) custom-call(bf16[256,512]{1,0:T(8,128)(2,1)} %copy-done.5, bf16[256,512]{1,0:T(8,128)(2,1)} %collective-permute-done.3.refs_1_, bf16[256,512]{1,0:T(8,128)(2,1)} %copy-done.16, bf16[256,512]{1,0:T(8,128)(2,1)} %copy-done.15, ...), custom_call_target="tpu_custom_call" | custom-call | flops 1000 | bytes 1000 | tf_op jit(solution)/shard_map/tail_part/pallas_call | solution.py:371
  83.3 6.1 %all-to-all-start.2 = ((bf16[16,24,512]{2,1,0:T(8,128)(2,1)}), bf16[16,24,512]{2,1,0:T(8,128)(2,1)S(1)}, u32[]{:S(2)}, u32[]{:S(2)}) async-start(bf16[16,24,512]{2,1,0:T(8,128)(2,1)} %bitcast.30), calls=%async_computation.2 | async-start | bytes 786432 | tf_op jit(solution)/shard_map/all_to_all | solution.py:405
  89.4 6.4 %halo_start.3 = bf16[2048,512]{1,0:T(8,128)(2,1)} custom-call(s32[2048]{0:T(1024)} %bitcast.33, s32[1,8]{1,0:T(1,128)} %count_ref.3, bf16[4096,512]{1,0:T(8,128)(2,1)} %get-tuple-element.29.table_ref.refs_12_), custom_call_target="tpu_custom_call" | custom-call | flops 1000 | bytes 1000 | tf_op jit(solution)/shard_map/halo_start/pallas_call | solution.py:225
  95.9 3.0 %all-to-all-done.2 = bf16[16,24,512]{2,1,0:T(8,128)(2,1)S(1)} async-done(((bf16[16,24,512]{2,1,0:T(8,128)(2,1)}), bf16[16,24,512]{2,1,0:T(8,128)(2,1)S(1)}, u32[]{:S(2)}, u32[]{:S(2)}) %all-to-all-start.2) | async-done | bytes 393248 | tf_op jit(solution)/shard_map/all_to_all | solution.py:405
  98.8 4.5 %all-to-all-start.3 = ((bf16[8,256,512]{2,1,0:T(8,128)(2,1)}), bf16[8,256,512]{2,1,0:T(8,128)(2,1)S(1)}, u32[]{:S(2)}, u32[]{:S(2)}) async-start(bf16[8,256,512]{2,1,0:T(8,128)(2,1)} %bitcast.24), calls=%async_computation.3 | async-start | bytes 4194304 | tf_op jit(solution)/shard_map/all_to_all | solution.py:408
  103.6 0.6 collective-permute-start.14
  104.2 1.5 collective-permute-start.13
  105.7 1.5 collective-permute-start.12
  107.1 0.7 collective-permute-start.20
  107.9 2.5 %collective-permute-start.18 = (bf16[64,512]{1,0:T(8,128)(2,1)S(1)}, bf16[64,512]{1,0:T(8,128)(2,1)S(1)}, u32[]{:S(2)}, u32[]{:S(2)}) collective-permute-start(bf16[64,512]{1,0:T(8,128)(2,1)S(1)} %get-tuple-element.32), channel_id=1, source_target_pairs={{4,0},{5,1},{6,2},{7,3},{8,4},{9,5},{10,6},{11,7},{12,8},{13,9},{1... | collective-permute-start | bytes 196616 | tf_op jit(solution)/shard_map/ppermute | solution.py:387
  110.4 1.9 %collective-permute-done.18 = bf16[64,512]{1,0:T(8,128)(2,1)S(1)} collective-permute-done((bf16[64,512]{1,0:T(8,128)(2,1)S(1)}, bf16[64,512]{1,0:T(8,128)(2,1)S(1)}, u32[]{:S(2)}, u32[]{:S(2)}) %collective-permute-start.18) | collective-permute-done | bytes 65568 | tf_op jit(solution)/shard_map/ppermute | solution.py:387
  112.3 2.7 %collective-permute-start.19 = (bf16[64,512]{1,0:T(8,128)(2,1)S(1)}, bf16[64,512]{1,0:T(8,128)(2,1)S(1)}, u32[]{:S(2)}, u32[]{:S(2)}) collective-permute-start(bf16[64,512]{1,0:T(8,128)(2,1)S(1)} %get-tuple-element.32), channel_id=1, source_target_pairs={{8,0},{9,1},{10,2},{11,3},{12,4},{13,5},{14,6},{15,7},{0,8},{1,9},... | collective-permute-start | bytes 196616 | tf_op jit(solution)/shard_map/ppermute | solution.py:387
  115.0 3.0 %collective-permute-done.19 = bf16[64,512]{1,0:T(8,128)(2,1)S(1)} collective-permute-done((bf16[64,512]{1,0:T(8,128)(2,1)S(1)}, bf16[64,512]{1,0:T(8,128)(2,1)S(1)}, u32[]{:S(2)}, u32[]{:S(2)}) %collective-permute-start.19) | collective-permute-done | bytes 65568 | tf_op jit(solution)/shard_map/ppermute | solution.py:387
  118.1 0.7 collective-permute-start.23
  118.8 2.2 %collective-permute-start.22 = (bf16[256,512]{1,0:T(8,128)(2,1)S(1)}, bf16[256,512]{1,0:T(8,128)(2,1)S(1)}, u32[]{:S(2)}, u32[]{:S(2)}) collective-permute-start(bf16[256,512]{1,0:T(8,128)(2,1)S(1)} %constant_dynamic-update-slice_fusion.12.refs_4_), channel_id=1, source_target_pairs={{2,0},{3,1},{0,2},{1,3},{6,4},{7,5},{4,6},{5,7},{10,8},{11,9},{8,1... | collective-permute-start | bytes 786440 | tf_op jit(solution)/shard_map/ppermute | solution.py:387
  120.9 2.5 %collective-permute-start.21 = (bf16[256,512]{1,0:T(8,128)(2,1)S(1)}, bf16[256,512]{1,0:T(8,128)(2,1)S(1)}, u32[]{:S(2)}, u32[]{:S(2)}) collective-permute-start(bf16[256,512]{1,0:T(8,128)(2,1)S(1)} %constant_dynamic-update-slice_fusion.12.refs_4_), channel_id=1, source_target_pairs={{1,0},{2,1},{3,2},{0,3},{5,4},{6,5},{7,6},{4,7},{9,8},{10,9},{11,1... | collective-permute-start | bytes 786440 | tf_op jit(solution)/shard_map/ppermute | solution.py:387
  123.5 1.0 collective-permute-start.17
  124.5 4.1 %collective-permute-start.16 = (bf16[256,512]{1,0:T(8,128)(2,1)S(1)}, bf16[256,512]{1,0:T(8,128)(2,1)S(1)}, u32[]{:S(2)}, u32[]{:S(2)}) collective-permute-start(bf16[256,512]{1,0:T(8,128)(2,1)S(1)} %constant_dynamic-update-slice_fusion.8.refs_0_), channel_id=1, source_target_pairs={{8,0},{9,1},{10,2},{11,3},{12,4},{13,5},{14,6},{15,7},{0,8},{1,9},... | collective-permute-start | bytes 786440 | tf_op jit(solution)/shard_map/ppermute | solution.py:387
  128.6 1.7 %collective-permute-done.23.refs_7_ = bf16[256,512]{1,0:T(8,128)(2,1)S(1)} collective-permute-done((bf16[256,512]{1,0:T(8,128)(2,1)S(1)}, bf16[256,512]{1,0:T(8,128)(2,1)S(1)}, u32[]{:S(2)}, u32[]{:S(2)}) %collective-permute-start.23) | collective-permute-done | bytes 262176 | tf_op jit(solution)/shard_map/ppermute | solution.py:387
  130.4 3.6 %collective-permute-start.15 = (bf16[256,512]{1,0:T(8,128)(2,1)S(1)}, bf16[256,512]{1,0:T(8,128)(2,1)}, u32[]{:S(2)}, u32[]{:S(2)}) collective-permute-start(bf16[256,512]{1,0:T(8,128)(2,1)S(1)} %constant_dynamic-update-slice_fusion.8.refs_0_), channel_id=1, source_target_pairs={{4,0},{5,1},{6,2},{7,3},{8,4},{9,5},{10,6},{11,7},{12,8},{13,9},{1... | collective-permute-start | bytes 786440 | tf_op jit(solution)/shard_map/ppermute | solution.py:387
  134.0 2.7 %collective-permute-done.16.refs_2_ = bf16[256,512]{1,0:T(8,128)(2,1)S(1)} collective-permute-done((bf16[256,512]{1,0:T(8,128)(2,1)S(1)}, bf16[256,512]{1,0:T(8,128)(2,1)S(1)}, u32[]{:S(2)}, u32[]{:S(2)}) %collective-permute-start.16) | collective-permute-done | bytes 262176 | tf_op jit(solution)/shard_map/ppermute | solution.py:387
  136.6 0.7 copy-done.11
  137.9 1.3 copy-done.2
  139.2 16.3 %tail_part.3 = bf16[4096,512]{1,0:T(8,128)(2,1)} custom-call(bf16[256,512]{1,0:T(8,128)(2,1)} %copy-done.3, bf16[256,512]{1,0:T(8,128)(2,1)} %collective-permute-done.15.refs_1_, bf16[256,512]{1,0:T(8,128)(2,1)} %copy-done.11, bf16[256,512]{1,0:T(8,128)(2,1)} %copy-done.10, bf16[256,512]{1,0:T(8,128)(2,1)} %copy-done.4, bf16[256,512]{1,0:T(8,128)(2,1)} %copy-done.9, ...), custom_call_target="tpu_custom_call" | custom-call | flops 1000 | bytes 1000 | tf_op jit(solution)/shard_map/tail_part/pallas_call | solution.py:371
  (68 shorter events, 1.5 us)
Async XLA Ops:
  0.0 13.5 %copy-start.17 = (s32[1,8,256]{2,1,0:T(8,128)S(1)}, s32[1,8,256]{2,1,0:T(8,128)}, u32[]{:S(2)}) copy-start(s32[1,8,256]{2,1,0:T(8,128)} %param.14) | copy-start | bytes 24580
  5.4 18.2 %all-to-all-start = ((bf16[16,24,512]{2,1,0:T(8,128)(2,1)}), bf16[16,24,512]{2,1,0:T(8,128)(2,1)S(1)}, u32[]{:S(2)}, u32[]{:S(2)}) async-start(bf16[16,24,512]{2,1,0:T(8,128)(2,1)} %bitcast.31), calls=%async_computation | async-start | bytes 786432 | tf_op jit(solution)/shard_map/all_to_all | solution.py:405
  23.6 4.9 %copy-start = (s32[128,1]{1,0:T(8,128)S(1)}, s32[128,1]{1,0:T(8,128)}, u32[]{:S(2)}) copy-start(s32[128,1]{1,0:T(8,128)} %get-tuple-element.20.keep_ref) | copy-start | bytes 1540
  23.6 39.3 %all-to-all-start.1 = ((bf16[8,272,512]{2,1,0:T(8,128)(2,1)}), bf16[8,272,512]{2,1,0:T(8,128)(2,1)S(1)}, u32[]{:S(2)}, u32[]{:S(2)}) async-start(bf16[8,272,512]{2,1,0:T(8,128)(2,1)} %bitcast.23), calls=%async_computation.1 | async-start | bytes 4456448 | tf_op jit(solution)/shard_map/all_to_all | solution.py:408
  28.8 19.9 %collective-permute-start.2 = (bf16[64,512]{1,0:T(8,128)(2,1)S(1)}, bf16[64,512]{1,0:T(8,128)(2,1)S(1)}, u32[]{:S(2)}, u32[]{:S(2)}) collective-permute-start(bf16[64,512]{1,0:T(8,128)(2,1)S(1)} %get-tuple-element.23), channel_id=1, source_target_pairs={{3,0},{0,1},{1,2},{2,3},{7,4},{4,5},{5,6},{6,7},{11,8},{8,9},{9,10... | collective-permute-start | bytes 196616 | tf_op jit(solution)/shard_map/ppermute | solution.py:387
  29.4 19.3 %collective-permute-start.1 = (bf16[64,512]{1,0:T(8,128)(2,1)S(1)}, bf16[64,512]{1,0:T(8,128)(2,1)S(1)}, u32[]{:S(2)}, u32[]{:S(2)}) collective-permute-start(bf16[64,512]{1,0:T(8,128)(2,1)S(1)} %get-tuple-element.23), channel_id=1, source_target_pairs={{2,0},{3,1},{0,2},{1,3},{6,4},{7,5},{4,6},{5,7},{10,8},{11,9},{8,1... | collective-permute-start | bytes 196616 | tf_op jit(solution)/shard_map/ppermute | solution.py:387
  30.9 15.3 %collective-permute-start = (bf16[64,512]{1,0:T(8,128)(2,1)S(1)}, bf16[64,512]{1,0:T(8,128)(2,1)S(1)}, u32[]{:S(2)}, u32[]{:S(2)}) collective-permute-start(bf16[64,512]{1,0:T(8,128)(2,1)S(1)} %get-tuple-element.23), channel_id=1, source_target_pairs={{1,0},{2,1},{3,2},{0,3},{5,4},{6,5},{7,6},{4,7},{9,8},{10,9},{11,1... | collective-permute-start | bytes 196616 | tf_op jit(solution)/shard_map/ppermute | solution.py:387
  32.3 10.9 %collective-permute-start.8 = (bf16[64,512]{1,0:T(8,128)(2,1)S(1)}, bf16[64,512]{1,0:T(8,128)(2,1)S(1)}, u32[]{:S(2)}, u32[]{:S(2)}) collective-permute-start(bf16[64,512]{1,0:T(8,128)(2,1)S(1)} %get-tuple-element.24), channel_id=1, source_target_pairs={{12,0},{13,1},{14,2},{15,3},{0,4},{1,5},{2,6},{3,7},{4,8},{5,9},{6... | collective-permute-start | bytes 196616 | tf_op jit(solution)/shard_map/ppermute | solution.py:387
  32.9 4.6 %collective-permute-start.6 = (bf16[64,512]{1,0:T(8,128)(2,1)S(1)}, bf16[64,512]{1,0:T(8,128)(2,1)S(1)}, u32[]{:S(2)}, u32[]{:S(2)}) collective-permute-start(bf16[64,512]{1,0:T(8,128)(2,1)S(1)} %get-tuple-element.24), channel_id=1, source_target_pairs={{4,0},{5,1},{6,2},{7,3},{8,4},{9,5},{10,6},{11,7},{12,8},{13,9},{1... | collective-permute-start | bytes 196616 | tf_op jit(solution)/shard_map/ppermute | solution.py:387
  37.5 5.8 %collective-permute-start.7 = (bf16[64,512]{1,0:T(8,128)(2,1)S(1)}, bf16[64,512]{1,0:T(8,128)(2,1)S(1)}, u32[]{:S(2)}, u32[]{:S(2)}) collective-permute-start(bf16[64,512]{1,0:T(8,128)(2,1)S(1)} %get-tuple-element.24), channel_id=1, source_target_pairs={{8,0},{9,1},{10,2},{11,3},{12,4},{13,5},{14,6},{15,7},{0,8},{1,9},... | collective-permute-start | bytes 196616 | tf_op jit(solution)/shard_map/ppermute | solution.py:387
  43.3 19.6 %copy-start.6 = (bf16[256,512]{1,0:T(8,128)(2,1)}, bf16[256,512]{1,0:T(8,128)(2,1)S(1)}, u32[]{:S(2)}) copy-start(bf16[256,512]{1,0:T(8,128)(2,1)S(1)} %constant_dynamic-update-slice_fusion.4.refs_4_) | copy-start | bytes 786436
  43.3 12.3 %collective-permute-start.11 = (bf16[256,512]{1,0:T(8,128)(2,1)S(1)}, bf16[256,512]{1,0:T(8,128)(2,1)S(1)}, u32[]{:S(2)}, u32[]{:S(2)}) collective-permute-start(bf16[256,512]{1,0:T(8,128)(2,1)S(1)} %constant_dynamic-update-slice_fusion.4.refs_4_), channel_id=1, source_target_pairs={{3,0},{0,1},{1,2},{2,3},{7,4},{4,5},{5,6},{6,7},{11,8},{8,9},{9,10... | collective-permute-start | bytes 786440 | tf_op jit(solution)/shard_map/ppermute | solution.py:387
  44.0 15.0 %collective-permute-start.10 = (bf16[256,512]{1,0:T(8,128)(2,1)S(1)}, bf16[256,512]{1,0:T(8,128)(2,1)S(1)}, u32[]{:S(2)}, u32[]{:S(2)}) collective-permute-start(bf16[256,512]{1,0:T(8,128)(2,1)S(1)} %constant_dynamic-update-slice_fusion.4.refs_4_), channel_id=1, source_target_pairs={{2,0},{3,1},{0,2},{1,3},{6,4},{7,5},{4,6},{5,7},{10,8},{11,9},{8,1... | collective-permute-start | bytes 786440 | tf_op jit(solution)/shard_map/ppermute | solution.py:387
  46.1 12.8 %collective-permute-start.9 = (bf16[256,512]{1,0:T(8,128)(2,1)S(1)}, bf16[256,512]{1,0:T(8,128)(2,1)S(1)}, u32[]{:S(2)}, u32[]{:S(2)}) collective-permute-start(bf16[256,512]{1,0:T(8,128)(2,1)S(1)} %constant_dynamic-update-slice_fusion.4.refs_4_), channel_id=1, source_target_pairs={{1,0},{2,1},{3,2},{0,3},{5,4},{6,5},{7,6},{4,7},{9,8},{10,9},{11,1... | collective-permute-start | bytes 786440 | tf_op jit(solution)/shard_map/ppermute | solution.py:387
  48.7 14.1 %copy-start.5 = (bf16[256,512]{1,0:T(8,128)(2,1)}, bf16[256,512]{1,0:T(8,128)(2,1)S(1)}, u32[]{:S(2)}) copy-start(bf16[256,512]{1,0:T(8,128)(2,1)S(1)} %constant_dynamic-update-slice_fusion.refs_0_) | copy-start | bytes 786436
  48.7 10.3 %collective-permute-start.5 = (bf16[256,512]{1,0:T(8,128)(2,1)S(1)}, bf16[256,512]{1,0:T(8,128)(2,1)S(1)}, u32[]{:S(2)}, u32[]{:S(2)}) collective-permute-start(bf16[256,512]{1,0:T(8,128)(2,1)S(1)} %constant_dynamic-update-slice_fusion.refs_0_), channel_id=1, source_target_pairs={{12,0},{13,1},{14,2},{15,3},{0,4},{1,5},{2,6},{3,7},{4,8},{5,9},{6... | collective-permute-start | bytes 786440 | tf_op jit(solution)/shard_map/ppermute | solution.py:387
  49.7 12.1 %collective-permute-start.4 = (bf16[256,512]{1,0:T(8,128)(2,1)S(1)}, bf16[256,512]{1,0:T(8,128)(2,1)S(1)}, u32[]{:S(2)}, u32[]{:S(2)}) collective-permute-start(bf16[256,512]{1,0:T(8,128)(2,1)S(1)} %constant_dynamic-update-slice_fusion.refs_0_), channel_id=1, source_target_pairs={{8,0},{9,1},{10,2},{11,3},{12,4},{13,5},{14,6},{15,7},{0,8},{1,9},... | collective-permute-start | bytes 786440 | tf_op jit(solution)/shard_map/ppermute | solution.py:387
  55.5 7.3 %copy-start.12 = (bf16[256,512]{1,0:T(8,128)(2,1)}, bf16[256,512]{1,0:T(8,128)(2,1)S(1)}, u32[]{:S(2)}) copy-start(bf16[256,512]{1,0:T(8,128)(2,1)S(1)} %collective-permute-done.11.refs_7_) | copy-start | bytes 786436
  55.5 7.3 %collective-permute-start.3 = (bf16[256,512]{1,0:T(8,128)(2,1)S(1)}, bf16[256,512]{1,0:T(8,128)(2,1)}, u32[]{:S(2)}, u32[]{:S(2)}) collective-permute-start(bf16[256,512]{1,0:T(8,128)(2,1)S(1)} %constant_dynamic-update-slice_fusion.refs_0_), channel_id=1, source_target_pairs={{4,0},{5,1},{6,2},{7,3},{8,4},{9,5},{10,6},{11,7},{12,8},{13,9},{1... | collective-permute-start | bytes 786440 | tf_op jit(solution)/shard_map/ppermute | solution.py:387
  59.0 3.9 %copy-start.13 = (bf16[256,512]{1,0:T(8,128)(2,1)}, bf16[256,512]{1,0:T(8,128)(2,1)S(1)}, u32[]{:S(2)}) copy-start(bf16[256,512]{1,0:T(8,128)(2,1)S(1)} %collective-permute-done.10.refs_6_) | copy-start | bytes 786436
  59.0 2.9 %copy-start.14 = (bf16[256,512]{1,0:T(8,128)(2,1)}, bf16[256,512]{1,0:T(8,128)(2,1)S(1)}, u32[]{:S(2)}) copy-start(bf16[256,512]{1,0:T(8,128)(2,1)S(1)} %collective-permute-done.9.refs_5_) | copy-start | bytes 786436
  59.0 2.8 %copy-start.15 = (bf16[256,512]{1,0:T(8,128)(2,1)}, bf16[256,512]{1,0:T(8,128)(2,1)S(1)}, u32[]{:S(2)}) copy-start(bf16[256,512]{1,0:T(8,128)(2,1)S(1)} %collective-permute-done.5.refs_3_) | copy-start | bytes 786436
  61.8 0.7 copy-start.16
  62.8 1.4 copy-start.1
  83.3 15.5 %all-to-all-start.2 = ((bf16[16,24,512]{2,1,0:T(8,128)(2,1)}), bf16[16,24,512]{2,1,0:T(8,128)(2,1)S(1)}, u32[]{:S(2)}, u32[]{:S(2)}) async-start(bf16[16,24,512]{2,1,0:T(8,128)(2,1)} %bitcast.30), calls=%async_computation.2 | async-start | bytes 786432 | tf_op jit(solution)/shard_map/all_to_all | solution.py:405
  98.8 39.0 %all-to-all-start.3 = ((bf16[8,256,512]{2,1,0:T(8,128)(2,1)}), bf16[8,256,512]{2,1,0:T(8,128)(2,1)S(1)}, u32[]{:S(2)}, u32[]{:S(2)}) async-start(bf16[8,256,512]{2,1,0:T(8,128)(2,1)} %bitcast.24), calls=%async_computation.3 | async-start | bytes 4194304 | tf_op jit(solution)/shard_map/all_to_all | solution.py:408
  103.6 19.9 %collective-permute-start.14 = (bf16[64,512]{1,0:T(8,128)(2,1)S(1)}, bf16[64,512]{1,0:T(8,128)(2,1)S(1)}, u32[]{:S(2)}, u32[]{:S(2)}) collective-permute-start(bf16[64,512]{1,0:T(8,128)(2,1)S(1)} %get-tuple-element.31), channel_id=1, source_target_pairs={{3,0},{0,1},{1,2},{2,3},{7,4},{4,5},{5,6},{6,7},{11,8},{8,9},{9,10... | collective-permute-start | bytes 196616 | tf_op jit(solution)/shard_map/ppermute | solution.py:387
  104.2 19.3 %collective-permute-start.13 = (bf16[64,512]{1,0:T(8,128)(2,1)S(1)}, bf16[64,512]{1,0:T(8,128)(2,1)S(1)}, u32[]{:S(2)}, u32[]{:S(2)}) collective-permute-start(bf16[64,512]{1,0:T(8,128)(2,1)S(1)} %get-tuple-element.31), channel_id=1, source_target_pairs={{2,0},{3,1},{0,2},{1,3},{6,4},{7,5},{4,6},{5,7},{10,8},{11,9},{8,1... | collective-permute-start | bytes 196616 | tf_op jit(solution)/shard_map/ppermute | solution.py:387
  105.7 15.3 %collective-permute-start.12 = (bf16[64,512]{1,0:T(8,128)(2,1)S(1)}, bf16[64,512]{1,0:T(8,128)(2,1)S(1)}, u32[]{:S(2)}, u32[]{:S(2)}) collective-permute-start(bf16[64,512]{1,0:T(8,128)(2,1)S(1)} %get-tuple-element.31), channel_id=1, source_target_pairs={{1,0},{2,1},{3,2},{0,3},{5,4},{6,5},{7,6},{4,7},{9,8},{10,9},{11,1... | collective-permute-start | bytes 196616 | tf_op jit(solution)/shard_map/ppermute | solution.py:387
  107.1 10.9 %collective-permute-start.20 = (bf16[64,512]{1,0:T(8,128)(2,1)S(1)}, bf16[64,512]{1,0:T(8,128)(2,1)S(1)}, u32[]{:S(2)}, u32[]{:S(2)}) collective-permute-start(bf16[64,512]{1,0:T(8,128)(2,1)S(1)} %get-tuple-element.32), channel_id=1, source_target_pairs={{12,0},{13,1},{14,2},{15,3},{0,4},{1,5},{2,6},{3,7},{4,8},{5,9},{6... | collective-permute-start | bytes 196616 | tf_op jit(solution)/shard_map/ppermute | solution.py:387
  107.9 4.4 %collective-permute-start.18 = (bf16[64,512]{1,0:T(8,128)(2,1)S(1)}, bf16[64,512]{1,0:T(8,128)(2,1)S(1)}, u32[]{:S(2)}, u32[]{:S(2)}) collective-permute-start(bf16[64,512]{1,0:T(8,128)(2,1)S(1)} %get-tuple-element.32), channel_id=1, source_target_pairs={{4,0},{5,1},{6,2},{7,3},{8,4},{9,5},{10,6},{11,7},{12,8},{13,9},{1... | collective-permute-start | bytes 196616 | tf_op jit(solution)/shard_map/ppermute | solution.py:387
  112.3 5.8 %collective-permute-start.19 = (bf16[64,512]{1,0:T(8,128)(2,1)S(1)}, bf16[64,512]{1,0:T(8,128)(2,1)S(1)}, u32[]{:S(2)}, u32[]{:S(2)}) collective-permute-start(bf16[64,512]{1,0:T(8,128)(2,1)S(1)} %get-tuple-element.32), channel_id=1, source_target_pairs={{8,0},{9,1},{10,2},{11,3},{12,4},{13,5},{14,6},{15,7},{0,8},{1,9},... | collective-permute-start | bytes 196616 | tf_op jit(solution)/shard_map/ppermute | solution.py:387
  118.1 19.7 %copy-start.4 = (bf16[256,512]{1,0:T(8,128)(2,1)}, bf16[256,512]{1,0:T(8,128)(2,1)S(1)}, u32[]{:S(2)}) copy-start(bf16[256,512]{1,0:T(8,128)(2,1)S(1)} %constant_dynamic-update-slice_fusion.12.refs_4_) | copy-start | bytes 786436
  118.1 12.3 %collective-permute-start.23 = (bf16[256,512]{1,0:T(8,128)(2,1)S(1)}, bf16[256,512]{1,0:T(8,128)(2,1)S(1)}, u32[]{:S(2)}, u32[]{:S(2)}) collective-permute-start(bf16[256,512]{1,0:T(8,128)(2,1)S(1)} %constant_dynamic-update-slice_fusion.12.refs_4_), channel_id=1, source_target_pairs={{3,0},{0,1},{1,2},{2,3},{7,4},{4,5},{5,6},{6,7},{11,8},{8,9},{9,10... | collective-permute-start | bytes 786440 | tf_op jit(solution)/shard_map/ppermute | solution.py:387
  118.8 15.1 %collective-permute-start.22 = (bf16[256,512]{1,0:T(8,128)(2,1)S(1)}, bf16[256,512]{1,0:T(8,128)(2,1)S(1)}, u32[]{:S(2)}, u32[]{:S(2)}) collective-permute-start(bf16[256,512]{1,0:T(8,128)(2,1)S(1)} %constant_dynamic-update-slice_fusion.12.refs_4_), channel_id=1, source_target_pairs={{2,0},{3,1},{0,2},{1,3},{6,4},{7,5},{4,6},{5,7},{10,8},{11,9},{8,1... | collective-permute-start | bytes 786440 | tf_op jit(solution)/shard_map/ppermute | solution.py:387
  120.9 13.0 %collective-permute-start.21 = (bf16[256,512]{1,0:T(8,128)(2,1)S(1)}, bf16[256,512]{1,0:T(8,128)(2,1)S(1)}, u32[]{:S(2)}, u32[]{:S(2)}) collective-permute-start(bf16[256,512]{1,0:T(8,128)(2,1)S(1)} %constant_dynamic-update-slice_fusion.12.refs_4_), channel_id=1, source_target_pairs={{1,0},{2,1},{3,2},{0,3},{5,4},{6,5},{7,6},{4,7},{9,8},{10,9},{11,1... | collective-permute-start | bytes 786440 | tf_op jit(solution)/shard_map/ppermute | solution.py:387
  123.5 14.3 %copy-start.3 = (bf16[256,512]{1,0:T(8,128)(2,1)}, bf16[256,512]{1,0:T(8,128)(2,1)S(1)}, u32[]{:S(2)}) copy-start(bf16[256,512]{1,0:T(8,128)(2,1)S(1)} %constant_dynamic-update-slice_fusion.8.refs_0_) | copy-start | bytes 786436
  123.5 10.4 %collective-permute-start.17 = (bf16[256,512]{1,0:T(8,128)(2,1)S(1)}, bf16[256,512]{1,0:T(8,128)(2,1)S(1)}, u32[]{:S(2)}, u32[]{:S(2)}) collective-permute-start(bf16[256,512]{1,0:T(8,128)(2,1)S(1)} %constant_dynamic-update-slice_fusion.8.refs_0_), channel_id=1, source_target_pairs={{12,0},{13,1},{14,2},{15,3},{0,4},{1,5},{2,6},{3,7},{4,8},{5,9},{6... | collective-permute-start | bytes 786440 | tf_op jit(solution)/shard_map/ppermute | solution.py:387
  124.5 12.1 %collective-permute-start.16 = (bf16[256,512]{1,0:T(8,128)(2,1)S(1)}, bf16[256,512]{1,0:T(8,128)(2,1)S(1)}, u32[]{:S(2)}, u32[]{:S(2)}) collective-permute-start(bf16[256,512]{1,0:T(8,128)(2,1)S(1)} %constant_dynamic-update-slice_fusion.8.refs_0_), channel_id=1, source_target_pairs={{8,0},{9,1},{10,2},{11,3},{12,4},{13,5},{14,6},{15,7},{0,8},{1,9},... | collective-permute-start | bytes 786440 | tf_op jit(solution)/shard_map/ppermute | solution.py:387
  130.4 7.5 %copy-start.7 = (bf16[256,512]{1,0:T(8,128)(2,1)}, bf16[256,512]{1,0:T(8,128)(2,1)S(1)}, u32[]{:S(2)}) copy-start(bf16[256,512]{1,0:T(8,128)(2,1)S(1)} %collective-permute-done.23.refs_7_) | copy-start | bytes 786436
  130.4 7.5 %collective-permute-start.15 = (bf16[256,512]{1,0:T(8,128)(2,1)S(1)}, bf16[256,512]{1,0:T(8,128)(2,1)}, u32[]{:S(2)}, u32[]{:S(2)}) collective-permute-start(bf16[256,512]{1,0:T(8,128)(2,1)S(1)} %constant_dynamic-update-slice_fusion.8.refs_0_), channel_id=1, source_target_pairs={{4,0},{5,1},{6,2},{7,3},{8,4},{9,5},{10,6},{11,7},{12,8},{13,9},{1... | collective-permute-start | bytes 786440 | tf_op jit(solution)/shard_map/ppermute | solution.py:387
  133.9 3.9 %copy-start.8 = (bf16[256,512]{1,0:T(8,128)(2,1)}, bf16[256,512]{1,0:T(8,128)(2,1)S(1)}, u32[]{:S(2)}) copy-start(bf16[256,512]{1,0:T(8,128)(2,1)S(1)} %collective-permute-done.22.refs_6_) | copy-start | bytes 786436
  133.9 3.9 %copy-start.9 = (bf16[256,512]{1,0:T(8,128)(2,1)}, bf16[256,512]{1,0:T(8,128)(2,1)S(1)}, u32[]{:S(2)}) copy-start(bf16[256,512]{1,0:T(8,128)(2,1)S(1)} %collective-permute-done.21.refs_5_) | copy-start | bytes 786436
  134.0 2.7 %copy-start.10 = (bf16[256,512]{1,0:T(8,128)(2,1)}, bf16[256,512]{1,0:T(8,128)(2,1)S(1)}, u32[]{:S(2)}) copy-start(bf16[256,512]{1,0:T(8,128)(2,1)S(1)} %collective-permute-done.17.refs_3_) | copy-start | bytes 786436
  136.6 0.7 copy-start.11
  137.8 1.4 copy-start.2

commit v4 on v3

--- a/solution.py
+++ b/solution.py
@@ -130,7 +130,10 @@
 def hub_kernel(col_ref, owner_ref, row_ref, table_ref, out_ref, send_ref, keep_ref, pos_ref, held, sem):
     copies = load_table(table_ref, held, sem)
     send, keep, pos = write_index(col_ref[0], owner_ref[...], row_ref[...])
-    send_ref[...] = send
+    lists = SIDE - 1
+    parts = [send[k * TB : (k + 1) * TB, :].astype(F32) for k in range(lists)]
+    square = jnp.concatenate(parts + [jnp.zeros((TB, TB - lists), F32)], axis=1)
+    send_ref[...] = square.T[0:8, :].astype(I32)
     keep_ref[...] = keep
     pos_ref[...] = pos
     chunk = held.shape[0] // SIDE
@@ -148,7 +151,7 @@
         hub_kernel,
         in_specs=[smem(), vmem(), vmem(), hbm()],
         out_specs=[vmem()] * 4,
-        out_shape=[shape(BF16, sent, width), shape(I32, sent, 1), shape(I32, SHARE, 1), shape(I32, HUBS // TB, TB)],
+        out_shape=[shape(BF16, sent, width), shape(I32, 8, TB), shape(I32, SHARE, 1), shape(I32, HUBS // TB, TB)],
         scratch_shapes=[pltpu.VMEM((nodes, width), BF16), pltpu.SemaphoreType.DMA((SIDE,))],
         compiler_params=params(60),
         cost_estimate=cost(),
@@ -269,7 +272,7 @@
         rest = rest[2:]
     else:
         send_ref, out_ref, picked_ref, counts = rest[:4]
-        notes, total = rest[-2:]
+        notes, full = rest[-2:]
         rest = rest[4:-2]
     held, wide, placed, store, table, tiles, far_tiles, weight, joined, result, sem, out_sem = rest
     lanes = 4
@@ -331,13 +334,19 @@
         result[span, :] = rows
         out[k].start()
         if not last:
-            part = choose(send_ref[...], k * TALL, TALL, rows)
-            if k == 0:
-                total[...] = part
-            else:
-                total[...] = total[...] + part
+            widen(rows.astype(F32), full, k * TALL)
     if not last:
-        picked_ref[...] = total[...].astype(BF16)
+        sent = picked_ref.shape[0]
+        for k in range(sent // TB):
+
+            @pl.loop(0, TB // unroll)
+            def _(n):
+                for u in range(unroll):
+                    slot = n * unroll + u
+                    move_row(full, send_ref[k, slot], placed, k * TB + slot)
+
+        for j in range(lanes):
+            picked_ref[:, j * TB : (j + 1) * TB] = placed[pl.ds(j, sent, stride=lanes), :].astype(BF16)
     for copy in out:
         copy.wait()
 
@@ -345,7 +354,7 @@
 def tail_part(last, hubs, cols, far_cols, pos, halos, table, tiles, far_tiles, weight, extra):
     nodes, width = table.shape
     lanes = width // TB
-    in_specs = [hbm()] * 8 + [smem()] * 3 + [hbm()] * 5 + [vmem()]
+    in_specs = [hbm()] * 8 + [smem()] * 3 + [hbm()] * 5 + [vmem() if last else smem()]
     args = [*hubs, cols, far_cols, pos, halos, table, tiles, far_tiles, weight, extra]
     out_specs = [hbm()]
     out_shape = [shape(BF16, nodes, width)]
@@ -367,7 +376,7 @@
         sent = COLS * PAIR
         out_specs += [vmem(), vmem()]
         out_shape += [shape(BF16, sent, width), shape(F32, 2 * ROWS, TB)]
-        scratch += [pltpu.VMEM((ROWS * NOTE, width), BF16), pltpu.VMEM((sent, width), F32)]
+        scratch += [pltpu.VMEM((ROWS * NOTE, width), BF16), pltpu.VMEM((nodes * lanes, TB), F32)]
     return pl.pallas_call(
         functools.partial(tail_kernel, last),
         in_specs=in_specs,

time: 156 us -> 155 us (level)
  Pallas kernels: 53.9 us -> 51.8 us
where the time goes in v4:
time: 155 us; the launch traced here: 154 us
  starting transfers between devices  69.8 us (45%)
  Pallas kernels  51.8 us (33%)
  waiting for transfers between devices  27.3 us (18%)
  local copies, waits for them, and re-layouts  4.8 us (3%)
    ppermute x24, starting transfers between devices, fetch(): return lax.ppermute(array, 'col', pairs)  46.2 us
    pallas_call x2, Pallas kernels, tail_part(): pl.pallas_call(functools.partial(tail_kernel, last), in_specs=in_specs, o...  33.9 us
    ppermute x24, waiting for transfers between devices, fetch(): return lax.ppermute(array, 'col', pairs)  20.4 us
    all_to_all x2, starting transfers between devices, exchange(): lax.all_to_all(picked.reshape(COLS, PAIR, width), 'col', 0, 0, tiled=True)  14.2 us
    pallas_call x2, Pallas kernels, halo_start(): pl.pallas_call(functools.partial(halo_kernel, noted), in_specs=[smem(), s...  12 us
    all_to_all x2, starting transfers between devices, exchange(): lax.all_to_all(outgoing.reshape(ROWS, -1, width), 'row', 0, 0, tiled=True)  9.42 us
    all_to_all x2, waiting for transfers between devices, exchange(): lax.all_to_all(picked.reshape(COLS, PAIR, width), 'col', 0, 0, tiled=True)  6.88 us
    pallas_call x1, Pallas kernels, hub_start(): pl.pallas_call(hub_kernel, in_specs=[smem(), vmem(), vmem(), hbm()], out_...  5.48 us
  transfers between devices with their start and end apart: 28, of which 12 were waited for; matrix products, arithmetic and copies ran while one was open for 0% of the time, Pallas kernels for 8%

profile of v4, /device:TPU:6, one launch (start us, length us, event | category | flops | bytes accessed | tf_op | source)
XLA Modules:
  0.0 154.2 jit_solution(10262240454298453095)
XLA Ops:
  0.0 5.5 %hub_start.1 = (bf16[384,512]{1,0:T(8,128)(2,1)}, s32[8,128]{1,0:T(8,128)}, s32[128,1]{1,0:T(8,128)}, s32[16,128]{1,0:T(8,128)}) custom-call(s32[1]{0:T(128)} %bitcast.col_ref, s32[1,2048]{1,0:T(1,128)} %bitcast.34, s32[1,2048]{1,0:T(1,128)} %row_ref.1, bf16[4096,512]{1,0:T(8,128)(2,1)} %refs_12_.1), custom_call_target="tpu_custom_call" | custom-call | flops 1000 | bytes 1000 | tf_op jit(solution)/shard_map/hub_start/pallas_call | solution.py:150
  5.5 8.1 %all-to-all-start = ((bf16[16,24,512]{2,1,0:T(8,128)(2,1)}), bf16[16,24,512]{2,1,0:T(8,128)(2,1)S(1)}, u32[]{:S(2)}, u32[]{:S(2)}) async-start(bf16[16,24,512]{2,1,0:T(8,128)(2,1)} %bitcast.31), calls=%async_computation | async-start | bytes 786432 | tf_op jit(solution)/shard_map/all_to_all | solution.py:414
  13.6 0.6 copy.12
  14.2 6.0 %halo_start.2 = bf16[2176,512]{1,0:T(8,128)(2,1)} custom-call(s32[2048]{0:T(1024)} %bitcast.32, s32[1,8]{1,0:T(1,128)} %count_ref.3, bf16[4096,512]{1,0:T(8,128)(2,1)} %refs_12_.1), custom_call_target="tpu_custom_call" | custom-call | flops 1000 | bytes 1000 | tf_op jit(solution)/shard_map/halo_start/pallas_call | solution.py:228
  20.2 3.5 %all-to-all-done = bf16[16,24,512]{2,1,0:T(8,128)(2,1)S(1)} async-done(((bf16[16,24,512]{2,1,0:T(8,128)(2,1)}), bf16[16,24,512]{2,1,0:T(8,128)(2,1)S(1)}, u32[]{:S(2)}, u32[]{:S(2)}) %all-to-all-start) | async-done | bytes 393248 | tf_op jit(solution)/shard_map/all_to_all | solution.py:414
  23.7 4.9 %all-to-all-start.1 = ((bf16[8,272,512]{2,1,0:T(8,128)(2,1)}), bf16[8,272,512]{2,1,0:T(8,128)(2,1)S(1)}, u32[]{:S(2)}, u32[]{:S(2)}) async-start(bf16[8,272,512]{2,1,0:T(8,128)(2,1)} %bitcast.22), calls=%async_computation.1 | async-start | bytes 4456448 | tf_op jit(solution)/shard_map/all_to_all | solution.py:417
  28.8 0.6 collective-permute-start.2
  29.5 1.5 collective-permute-start.1
  30.9 1.5 collective-permute-start
  32.4 0.8 collective-permute-start.8
  33.2 2.5 %collective-permute-start.6 = (bf16[64,512]{1,0:T(8,128)(2,1)S(1)}, bf16[64,512]{1,0:T(8,128)(2,1)S(1)}, u32[]{:S(2)}, u32[]{:S(2)}) collective-permute-start(bf16[64,512]{1,0:T(8,128)(2,1)S(1)} %get-tuple-element.24), channel_id=1, source_target_pairs={{4,0},{5,1},{6,2},{7,3},{8,4},{9,5},{10,6},{11,7},{12,8},{13,9},{1... | collective-permute-start | bytes 196616 | tf_op jit(solution)/shard_map/ppermute | solution.py:396
  35.6 1.9 %collective-permute-done.6 = bf16[64,512]{1,0:T(8,128)(2,1)S(1)} collective-permute-done((bf16[64,512]{1,0:T(8,128)(2,1)S(1)}, bf16[64,512]{1,0:T(8,128)(2,1)S(1)}, u32[]{:S(2)}, u32[]{:S(2)}) %collective-permute-start.6) | collective-permute-done | bytes 65568 | tf_op jit(solution)/shard_map/ppermute | solution.py:396
  37.5 2.3 %collective-permute-start.7 = (bf16[64,512]{1,0:T(8,128)(2,1)S(1)}, bf16[64,512]{1,0:T(8,128)(2,1)S(1)}, u32[]{:S(2)}, u32[]{:S(2)}) collective-permute-start(bf16[64,512]{1,0:T(8,128)(2,1)S(1)} %get-tuple-element.24), channel_id=1, source_target_pairs={{8,0},{9,1},{10,2},{11,3},{12,4},{13,5},{14,6},{15,7},{0,8},{1,9},... | collective-permute-start | bytes 196616 | tf_op jit(solution)/shard_map/ppermute | solution.py:396
  39.9 3.4 %collective-permute-done.7 = bf16[64,512]{1,0:T(8,128)(2,1)S(1)} collective-permute-done((bf16[64,512]{1,0:T(8,128)(2,1)S(1)}, bf16[64,512]{1,0:T(8,128)(2,1)S(1)}, u32[]{:S(2)}, u32[]{:S(2)}) %collective-permute-start.7) | collective-permute-done | bytes 65568 | tf_op jit(solution)/shard_map/ppermute | solution.py:396
  43.3 0.7 collective-permute-start.11
  44.0 2.2 %collective-permute-start.10 = (bf16[256,512]{1,0:T(8,128)(2,1)S(1)}, bf16[256,512]{1,0:T(8,128)(2,1)S(1)}, u32[]{:S(2)}, u32[]{:S(2)}) collective-permute-start(bf16[256,512]{1,0:T(8,128)(2,1)S(1)} %constant_dynamic-update-slice_fusion.4.refs_4_), channel_id=1, source_target_pairs={{2,0},{3,1},{0,2},{1,3},{6,4},{7,5},{4,6},{5,7},{10,8},{11,9},{8,1... | collective-permute-start | bytes 786440 | tf_op jit(solution)/shard_map/ppermute | solution.py:396
  46.2 2.5 %collective-permute-start.9 = (bf16[256,512]{1,0:T(8,128)(2,1)S(1)}, bf16[256,512]{1,0:T(8,128)(2,1)S(1)}, u32[]{:S(2)}, u32[]{:S(2)}) collective-permute-start(bf16[256,512]{1,0:T(8,128)(2,1)S(1)} %constant_dynamic-update-slice_fusion.4.refs_4_), channel_id=1, source_target_pairs={{1,0},{2,1},{3,2},{0,3},{5,4},{6,5},{7,6},{4,7},{9,8},{10,9},{11,1... | collective-permute-start | bytes 786440 | tf_op jit(solution)/shard_map/ppermute | solution.py:396
  48.8 1.0 collective-permute-start.5
  49.7 4.1 %collective-permute-start.4 = (bf16[256,512]{1,0:T(8,128)(2,1)S(1)}, bf16[256,512]{1,0:T(8,128)(2,1)S(1)}, u32[]{:S(2)}, u32[]{:S(2)}) collective-permute-start(bf16[256,512]{1,0:T(8,128)(2,1)S(1)} %constant_dynamic-update-slice_fusion.refs_0_), channel_id=1, source_target_pairs={{8,0},{9,1},{10,2},{11,3},{12,4},{13,5},{14,6},{15,7},{0,8},{1,9},... | collective-permute-start | bytes 786440 | tf_op jit(solution)/shard_map/ppermute | solution.py:396
  53.9 1.7 %collective-permute-done.11.refs_7_ = bf16[256,512]{1,0:T(8,128)(2,1)S(1)} collective-permute-done((bf16[256,512]{1,0:T(8,128)(2,1)S(1)}, bf16[256,512]{1,0:T(8,128)(2,1)S(1)}, u32[]{:S(2)}, u32[]{:S(2)}) %collective-permute-start.11) | collective-permute-done | bytes 262176 | tf_op jit(solution)/shard_map/ppermute | solution.py:396
  55.6 3.4 %collective-permute-start.3 = (bf16[256,512]{1,0:T(8,128)(2,1)S(1)}, bf16[256,512]{1,0:T(8,128)(2,1)}, u32[]{:S(2)}, u32[]{:S(2)}) collective-permute-start(bf16[256,512]{1,0:T(8,128)(2,1)S(1)} %constant_dynamic-update-slice_fusion.refs_0_), channel_id=1, source_target_pairs={{4,0},{5,1},{6,2},{7,3},{8,4},{9,5},{10,6},{11,7},{12,8},{13,9},{1... | collective-permute-start | bytes 786440 | tf_op jit(solution)/shard_map/ppermute | solution.py:396
  59.1 2.8 %collective-permute-done.4.refs_2_ = bf16[256,512]{1,0:T(8,128)(2,1)S(1)} collective-permute-done((bf16[256,512]{1,0:T(8,128)(2,1)S(1)}, bf16[256,512]{1,0:T(8,128)(2,1)S(1)}, u32[]{:S(2)}, u32[]{:S(2)}) %collective-permute-start.4) | collective-permute-done | bytes 262176 | tf_op jit(solution)/shard_map/ppermute | solution.py:396
  61.9 0.7 copy-done.16
  62.9 1.3 copy-done.1
  64.3 17.6 %tail_part.2 = (bf16[4096,512]{1,0:T(8,128)(2,1)}, bf16[384,512]{1,0:T(8,128)(2,1)}, f32[16,128]{1,0:T(8,128)}) custom-call(bf16[256,512]{1,0:T(8,128)(2,1)} %copy-done.5, bf16[256,512]{1,0:T(8,128)(2,1)} %collective-permute-done.3.refs_1_, bf16[256,512]{1,0:T(8,128)(2,1)} %copy-done.16, bf16[256,512]{1,0:T(8,128)(2,1)} %copy-done.15, ...), custom_call_target="tpu_custom_call" | custom-call | flops 1000 | bytes 1000 | tf_op jit(solution)/shard_map/tail_part/pallas_call | solution.py:380
  81.9 6.1 %all-to-all-start.2 = ((bf16[16,24,512]{2,1,0:T(8,128)(2,1)}), bf16[16,24,512]{2,1,0:T(8,128)(2,1)S(1)}, u32[]{:S(2)}, u32[]{:S(2)}) async-start(bf16[16,24,512]{2,1,0:T(8,128)(2,1)} %bitcast.30), calls=%async_computation.2 | async-start | bytes 786432 | tf_op jit(solution)/shard_map/all_to_all | solution.py:414
  88.0 6.0 %halo_start.3 = bf16[2048,512]{1,0:T(8,128)(2,1)} custom-call(s32[2048]{0:T(1024)} %bitcast.33, s32[1,8]{1,0:T(1,128)} %count_ref.3, bf16[4096,512]{1,0:T(8,128)(2,1)} %get-tuple-element.29.table_ref.refs_12_), custom_call_target="tpu_custom_call" | custom-call | flops 1000 | bytes 1000 | tf_op jit(solution)/shard_map/halo_start/pallas_call | solution.py:228
  94.0 3.4 %all-to-all-done.2 = bf16[16,24,512]{2,1,0:T(8,128)(2,1)S(1)} async-done(((bf16[16,24,512]{2,1,0:T(8,128)(2,1)}), bf16[16,24,512]{2,1,0:T(8,128)(2,1)S(1)}, u32[]{:S(2)}, u32[]{:S(2)}) %all-to-all-start.2) | async-done | bytes 393248 | tf_op jit(solution)/shard_map/all_to_all | solution.py:414
  97.4 4.5 %all-to-all-start.3 = ((bf16[8,256,512]{2,1,0:T(8,128)(2,1)}), bf16[8,256,512]{2,1,0:T(8,128)(2,1)S(1)}, u32[]{:S(2)}, u32[]{:S(2)}) async-start(bf16[8,256,512]{2,1,0:T(8,128)(2,1)} %bitcast.24), calls=%async_computation.3 | async-start | bytes 4194304 | tf_op jit(solution)/shard_map/all_to_all | solution.py:417
  102.2 0.6 collective-permute-start.14
  102.8 1.5 collective-permute-start.13
  104.3 1.5 collective-permute-start.12
  105.7 0.8 collective-permute-start.20
  106.6 2.4 %collective-permute-start.18 = (bf16[64,512]{1,0:T(8,128)(2,1)S(1)}, bf16[64,512]{1,0:T(8,128)(2,1)S(1)}, u32[]{:S(2)}, u32[]{:S(2)}) collective-permute-start(bf16[64,512]{1,0:T(8,128)(2,1)S(1)} %get-tuple-element.32), channel_id=1, source_target_pairs={{4,0},{5,1},{6,2},{7,3},{8,4},{9,5},{10,6},{11,7},{12,8},{13,9},{1... | collective-permute-start | bytes 196616 | tf_op jit(solution)/shard_map/ppermute | solution.py:396
  109.0 1.9 %collective-permute-done.18 = bf16[64,512]{1,0:T(8,128)(2,1)S(1)} collective-permute-done((bf16[64,512]{1,0:T(8,128)(2,1)S(1)}, bf16[64,512]{1,0:T(8,128)(2,1)S(1)}, u32[]{:S(2)}, u32[]{:S(2)}) %collective-permute-start.18) | collective-permute-done | bytes 65568 | tf_op jit(solution)/shard_map/ppermute | solution.py:396
  110.9 2.4 %collective-permute-start.19 = (bf16[64,512]{1,0:T(8,128)(2,1)S(1)}, bf16[64,512]{1,0:T(8,128)(2,1)S(1)}, u32[]{:S(2)}, u32[]{:S(2)}) collective-permute-start(bf16[64,512]{1,0:T(8,128)(2,1)S(1)} %get-tuple-element.32), channel_id=1, source_target_pairs={{8,0},{9,1},{10,2},{11,3},{12,4},{13,5},{14,6},{15,7},{0,8},{1,9},... | collective-permute-start | bytes 196616 | tf_op jit(solution)/shard_map/ppermute | solution.py:396
  113.3 3.4 %collective-permute-done.19 = bf16[64,512]{1,0:T(8,128)(2,1)S(1)} collective-permute-done((bf16[64,512]{1,0:T(8,128)(2,1)S(1)}, bf16[64,512]{1,0:T(8,128)(2,1)S(1)}, u32[]{:S(2)}, u32[]{:S(2)}) %collective-permute-start.19) | collective-permute-done | bytes 65568 | tf_op jit(solution)/shard_map/ppermute | solution.py:396
  116.7 0.7 collective-permute-start.23
  117.3 2.2 %collective-permute-start.22 = (bf16[256,512]{1,0:T(8,128)(2,1)S(1)}, bf16[256,512]{1,0:T(8,128)(2,1)S(1)}, u32[]{:S(2)}, u32[]{:S(2)}) collective-permute-start(bf16[256,512]{1,0:T(8,128)(2,1)S(1)} %constant_dynamic-update-slice_fusion.12.refs_4_), channel_id=1, source_target_pairs={{2,0},{3,1},{0,2},{1,3},{6,4},{7,5},{4,6},{5,7},{10,8},{11,9},{8,1... | collective-permute-start | bytes 786440 | tf_op jit(solution)/shard_map/ppermute | solution.py:396
  119.5 2.5 %collective-permute-start.21 = (bf16[256,512]{1,0:T(8,128)(2,1)S(1)}, bf16[256,512]{1,0:T(8,128)(2,1)S(1)}, u32[]{:S(2)}, u32[]{:S(2)}) collective-permute-start(bf16[256,512]{1,0:T(8,128)(2,1)S(1)} %constant_dynamic-update-slice_fusion.12.refs_4_), channel_id=1, source_target_pairs={{1,0},{2,1},{3,2},{0,3},{5,4},{6,5},{7,6},{4,7},{9,8},{10,9},{11,1... | collective-permute-start | bytes 786440 | tf_op jit(solution)/shard_map/ppermute | solution.py:396
  122.1 1.0 collective-permute-start.17
  123.1 4.1 %collective-permute-start.16 = (bf16[256,512]{1,0:T(8,128)(2,1)S(1)}, bf16[256,512]{1,0:T(8,128)(2,1)S(1)}, u32[]{:S(2)}, u32[]{:S(2)}) collective-permute-start(bf16[256,512]{1,0:T(8,128)(2,1)S(1)} %constant_dynamic-update-slice_fusion.8.refs_0_), channel_id=1, source_target_pairs={{8,0},{9,1},{10,2},{11,3},{12,4},{13,5},{14,6},{15,7},{0,8},{1,9},... | collective-permute-start | bytes 786440 | tf_op jit(solution)/shard_map/ppermute | solution.py:396
  127.2 1.7 %collective-permute-done.23.refs_7_ = bf16[256,512]{1,0:T(8,128)(2,1)S(1)} collective-permute-done((bf16[256,512]{1,0:T(8,128)(2,1)S(1)}, bf16[256,512]{1,0:T(8,128)(2,1)S(1)}, u32[]{:S(2)}, u32[]{:S(2)}) %collective-permute-start.23) | collective-permute-done | bytes 262176 | tf_op jit(solution)/shard_map/ppermute | solution.py:396
  128.9 3.6 %collective-permute-start.15 = (bf16[256,512]{1,0:T(8,128)(2,1)S(1)}, bf16[256,512]{1,0:T(8,128)(2,1)}, u32[]{:S(2)}, u32[]{:S(2)}) collective-permute-start(bf16[256,512]{1,0:T(8,128)(2,1)S(1)} %constant_dynamic-update-slice_fusion.8.refs_0_), channel_id=1, source_target_pairs={{4,0},{5,1},{6,2},{7,3},{8,4},{9,5},{10,6},{11,7},{12,8},{13,9},{1... | collective-permute-start | bytes 786440 | tf_op jit(solution)/shard_map/ppermute | solution.py:396
  132.5 2.7 %collective-permute-done.16.refs_2_ = bf16[256,512]{1,0:T(8,128)(2,1)S(1)} collective-permute-done((bf16[256,512]{1,0:T(8,128)(2,1)S(1)}, bf16[256,512]{1,0:T(8,128)(2,1)S(1)}, u32[]{:S(2)}, u32[]{:S(2)}) %collective-permute-start.16) | collective-permute-done | bytes 262176 | tf_op jit(solution)/shard_map/ppermute | solution.py:396
  135.2 0.7 copy-done.11
  136.4 1.3 copy-done.2
  137.8 16.3 %tail_part.3 = bf16[4096,512]{1,0:T(8,128)(2,1)} custom-call(bf16[256,512]{1,0:T(8,128)(2,1)} %copy-done.3, bf16[256,512]{1,0:T(8,128)(2,1)} %collective-permute-done.15.refs_1_, bf16[256,512]{1,0:T(8,128)(2,1)} %copy-done.11, bf16[256,512]{1,0:T(8,128)(2,1)} %copy-done.10, bf16[256,512]{1,0:T(8,128)(2,1)} %copy-done.4, bf16[256,512]{1,0:T(8,128)(2,1)} %copy-done.9, ...), custom_call_target="tpu_custom_call" | custom-call | flops 1000 | bytes 1000 | tf_op jit(solution)/shard_map/tail_part/pallas_call | solution.py:380
  (68 shorter events, 1.5 us)
Async XLA Ops:
  0.0 13.6 %copy-start.17 = (s32[1,8,256]{2,1,0:T(8,128)S(1)}, s32[1,8,256]{2,1,0:T(8,128)}, u32[]{:S(2)}) copy-start(s32[1,8,256]{2,1,0:T(8,128)} %param.14) | copy-start | bytes 24580
  5.5 18.2 %all-to-all-start = ((bf16[16,24,512]{2,1,0:T(8,128)(2,1)}), bf16[16,24,512]{2,1,0:T(8,128)(2,1)S(1)}, u32[]{:S(2)}, u32[]{:S(2)}) async-start(bf16[16,24,512]{2,1,0:T(8,128)(2,1)} %bitcast.31), calls=%async_computation | async-start | bytes 786432 | tf_op jit(solution)/shard_map/all_to_all | solution.py:414
  23.7 4.9 %copy-start = (s32[128,1]{1,0:T(8,128)S(1)}, s32[128,1]{1,0:T(8,128)}, u32[]{:S(2)}) copy-start(s32[128,1]{1,0:T(8,128)} %get-tuple-element.20.keep_ref) | copy-start | bytes 1540
  23.7 39.3 %all-to-all-start.1 = ((bf16[8,272,512]{2,1,0:T(8,128)(2,1)}), bf16[8,272,512]{2,1,0:T(8,128)(2,1)S(1)}, u32[]{:S(2)}, u32[]{:S(2)}) async-start(bf16[8,272,512]{2,1,0:T(8,128)(2,1)} %bitcast.22), calls=%async_computation.1 | async-start | bytes 4456448 | tf_op jit(solution)/shard_map/all_to_all | solution.py:417
  28.8 19.9 %collective-permute-start.2 = (bf16[64,512]{1,0:T(8,128)(2,1)S(1)}, bf16[64,512]{1,0:T(8,128)(2,1)S(1)}, u32[]{:S(2)}, u32[]{:S(2)}) collective-permute-start(bf16[64,512]{1,0:T(8,128)(2,1)S(1)} %get-tuple-element.23), channel_id=1, source_target_pairs={{3,0},{0,1},{1,2},{2,3},{7,4},{4,5},{5,6},{6,7},{11,8},{8,9},{9,10... | collective-permute-start | bytes 196616 | tf_op jit(solution)/shard_map/ppermute | solution.py:396
  29.5 19.3 %collective-permute-start.1 = (bf16[64,512]{1,0:T(8,128)(2,1)S(1)}, bf16[64,512]{1,0:T(8,128)(2,1)S(1)}, u32[]{:S(2)}, u32[]{:S(2)}) collective-permute-start(bf16[64,512]{1,0:T(8,128)(2,1)S(1)} %get-tuple-element.23), channel_id=1, source_target_pairs={{2,0},{3,1},{0,2},{1,3},{6,4},{7,5},{4,6},{5,7},{10,8},{11,9},{8,1... | collective-permute-start | bytes 196616 | tf_op jit(solution)/shard_map/ppermute | solution.py:396
  30.9 15.3 %collective-permute-start = (bf16[64,512]{1,0:T(8,128)(2,1)S(1)}, bf16[64,512]{1,0:T(8,128)(2,1)S(1)}, u32[]{:S(2)}, u32[]{:S(2)}) collective-permute-start(bf16[64,512]{1,0:T(8,128)(2,1)S(1)} %get-tuple-element.23), channel_id=1, source_target_pairs={{1,0},{2,1},{3,2},{0,3},{5,4},{6,5},{7,6},{4,7},{9,8},{10,9},{11,1... | collective-permute-start | bytes 196616 | tf_op jit(solution)/shard_map/ppermute | solution.py:396
  32.4 10.9 %collective-permute-start.8 = (bf16[64,512]{1,0:T(8,128)(2,1)S(1)}, bf16[64,512]{1,0:T(8,128)(2,1)S(1)}, u32[]{:S(2)}, u32[]{:S(2)}) collective-permute-start(bf16[64,512]{1,0:T(8,128)(2,1)S(1)} %get-tuple-element.24), channel_id=1, source_target_pairs={{12,0},{13,1},{14,2},{15,3},{0,4},{1,5},{2,6},{3,7},{4,8},{5,9},{6... | collective-permute-start | bytes 196616 | tf_op jit(solution)/shard_map/ppermute | solution.py:396
  33.2 4.4 %collective-permute-start.6 = (bf16[64,512]{1,0:T(8,128)(2,1)S(1)}, bf16[64,512]{1,0:T(8,128)(2,1)S(1)}, u32[]{:S(2)}, u32[]{:S(2)}) collective-permute-start(bf16[64,512]{1,0:T(8,128)(2,1)S(1)} %get-tuple-element.24), channel_id=1, source_target_pairs={{4,0},{5,1},{6,2},{7,3},{8,4},{9,5},{10,6},{11,7},{12,8},{13,9},{1... | collective-permute-start | bytes 196616 | tf_op jit(solution)/shard_map/ppermute | solution.py:396
  37.5 5.8 %collective-permute-start.7 = (bf16[64,512]{1,0:T(8,128)(2,1)S(1)}, bf16[64,512]{1,0:T(8,128)(2,1)S(1)}, u32[]{:S(2)}, u32[]{:S(2)}) collective-permute-start(bf16[64,512]{1,0:T(8,128)(2,1)S(1)} %get-tuple-element.24), channel_id=1, source_target_pairs={{8,0},{9,1},{10,2},{11,3},{12,4},{13,5},{14,6},{15,7},{0,8},{1,9},... | collective-permute-start | bytes 196616 | tf_op jit(solution)/shard_map/ppermute | solution.py:396
  43.3 19.6 %copy-start.6 = (bf16[256,512]{1,0:T(8,128)(2,1)}, bf16[256,512]{1,0:T(8,128)(2,1)S(1)}, u32[]{:S(2)}) copy-start(bf16[256,512]{1,0:T(8,128)(2,1)S(1)} %constant_dynamic-update-slice_fusion.4.refs_4_) | copy-start | bytes 786436
  43.3 12.3 %collective-permute-start.11 = (bf16[256,512]{1,0:T(8,128)(2,1)S(1)}, bf16[256,512]{1,0:T(8,128)(2,1)S(1)}, u32[]{:S(2)}, u32[]{:S(2)}) collective-permute-start(bf16[256,512]{1,0:T(8,128)(2,1)S(1)} %constant_dynamic-update-slice_fusion.4.refs_4_), channel_id=1, source_target_pairs={{3,0},{0,1},{1,2},{2,3},{7,4},{4,5},{5,6},{6,7},{11,8},{8,9},{9,10... | collective-permute-start | bytes 786440 | tf_op jit(solution)/shard_map/ppermute | solution.py:396
  44.0 15.0 %collective-permute-start.10 = (bf16[256,512]{1,0:T(8,128)(2,1)S(1)}, bf16[256,512]{1,0:T(8,128)(2,1)S(1)}, u32[]{:S(2)}, u32[]{:S(2)}) collective-permute-start(bf16[256,512]{1,0:T(8,128)(2,1)S(1)} %constant_dynamic-update-slice_fusion.4.refs_4_), channel_id=1, source_target_pairs={{2,0},{3,1},{0,2},{1,3},{6,4},{7,5},{4,6},{5,7},{10,8},{11,9},{8,1... | collective-permute-start | bytes 786440 | tf_op jit(solution)/shard_map/ppermute | solution.py:396
  46.2 12.8 %collective-permute-start.9 = (bf16[256,512]{1,0:T(8,128)(2,1)S(1)}, bf16[256,512]{1,0:T(8,128)(2,1)S(1)}, u32[]{:S(2)}, u32[]{:S(2)}) collective-permute-start(bf16[256,512]{1,0:T(8,128)(2,1)S(1)} %constant_dynamic-update-slice_fusion.4.refs_4_), channel_id=1, source_target_pairs={{1,0},{2,1},{3,2},{0,3},{5,4},{6,5},{7,6},{4,7},{9,8},{10,9},{11,1... | collective-permute-start | bytes 786440 | tf_op jit(solution)/shard_map/ppermute | solution.py:396
  48.8 14.1 %copy-start.5 = (bf16[256,512]{1,0:T(8,128)(2,1)}, bf16[256,512]{1,0:T(8,128)(2,1)S(1)}, u32[]{:S(2)}) copy-start(bf16[256,512]{1,0:T(8,128)(2,1)S(1)} %constant_dynamic-update-slice_fusion.refs_0_) | copy-start | bytes 786436
  48.8 10.3 %collective-permute-start.5 = (bf16[256,512]{1,0:T(8,128)(2,1)S(1)}, bf16[256,512]{1,0:T(8,128)(2,1)S(1)}, u32[]{:S(2)}, u32[]{:S(2)}) collective-permute-start(bf16[256,512]{1,0:T(8,128)(2,1)S(1)} %constant_dynamic-update-slice_fusion.refs_0_), channel_id=1, source_target_pairs={{12,0},{13,1},{14,2},{15,3},{0,4},{1,5},{2,6},{3,7},{4,8},{5,9},{6... | collective-permute-start | bytes 786440 | tf_op jit(solution)/shard_map/ppermute | solution.py:396
  49.7 12.1 %collective-permute-start.4 = (bf16[256,512]{1,0:T(8,128)(2,1)S(1)}, bf16[256,512]{1,0:T(8,128)(2,1)S(1)}, u32[]{:S(2)}, u32[]{:S(2)}) collective-permute-start(bf16[256,512]{1,0:T(8,128)(2,1)S(1)} %constant_dynamic-update-slice_fusion.refs_0_), channel_id=1, source_target_pairs={{8,0},{9,1},{10,2},{11,3},{12,4},{13,5},{14,6},{15,7},{0,8},{1,9},... | collective-permute-start | bytes 786440 | tf_op jit(solution)/shard_map/ppermute | solution.py:396
  55.6 7.3 %copy-start.12 = (bf16[256,512]{1,0:T(8,128)(2,1)}, bf16[256,512]{1,0:T(8,128)(2,1)S(1)}, u32[]{:S(2)}) copy-start(bf16[256,512]{1,0:T(8,128)(2,1)S(1)} %collective-permute-done.11.refs_7_) | copy-start | bytes 786436
  55.6 7.3 %collective-permute-start.3 = (bf16[256,512]{1,0:T(8,128)(2,1)S(1)}, bf16[256,512]{1,0:T(8,128)(2,1)}, u32[]{:S(2)}, u32[]{:S(2)}) collective-permute-start(bf16[256,512]{1,0:T(8,128)(2,1)S(1)} %constant_dynamic-update-slice_fusion.refs_0_), channel_id=1, source_target_pairs={{4,0},{5,1},{6,2},{7,3},{8,4},{9,5},{10,6},{11,7},{12,8},{13,9},{1... | collective-permute-start | bytes 786440 | tf_op jit(solution)/shard_map/ppermute | solution.py:396
  59.0 3.9 %copy-start.13 = (bf16[256,512]{1,0:T(8,128)(2,1)}, bf16[256,512]{1,0:T(8,128)(2,1)S(1)}, u32[]{:S(2)}) copy-start(bf16[256,512]{1,0:T(8,128)(2,1)S(1)} %collective-permute-done.10.refs_6_) | copy-start | bytes 786436
  59.0 2.9 %copy-start.14 = (bf16[256,512]{1,0:T(8,128)(2,1)}, bf16[256,512]{1,0:T(8,128)(2,1)S(1)}, u32[]{:S(2)}) copy-start(bf16[256,512]{1,0:T(8,128)(2,1)S(1)} %collective-permute-done.9.refs_5_) | copy-start | bytes 786436
  59.1 2.8 %copy-start.15 = (bf16[256,512]{1,0:T(8,128)(2,1)}, bf16[256,512]{1,0:T(8,128)(2,1)S(1)}, u32[]{:S(2)}) copy-start(bf16[256,512]{1,0:T(8,128)(2,1)S(1)} %collective-permute-done.5.refs_3_) | copy-start | bytes 786436
  61.9 0.7 copy-start.16
  62.9 1.4 copy-start.1
  81.9 15.5 %all-to-all-start.2 = ((bf16[16,24,512]{2,1,0:T(8,128)(2,1)}), bf16[16,24,512]{2,1,0:T(8,128)(2,1)S(1)}, u32[]{:S(2)}, u32[]{:S(2)}) async-start(bf16[16,24,512]{2,1,0:T(8,128)(2,1)} %bitcast.30), calls=%async_computation.2 | async-start | bytes 786432 | tf_op jit(solution)/shard_map/all_to_all | solution.py:414
  97.4 39.0 %all-to-all-start.3 = ((bf16[8,256,512]{2,1,0:T(8,128)(2,1)}), bf16[8,256,512]{2,1,0:T(8,128)(2,1)S(1)}, u32[]{:S(2)}, u32[]{:S(2)}) async-start(bf16[8,256,512]{2,1,0:T(8,128)(2,1)} %bitcast.24), calls=%async_computation.3 | async-start | bytes 4194304 | tf_op jit(solution)/shard_map/all_to_all | solution.py:417
  102.2 19.9 %collective-permute-start.14 = (bf16[64,512]{1,0:T(8,128)(2,1)S(1)}, bf16[64,512]{1,0:T(8,128)(2,1)S(1)}, u32[]{:S(2)}, u32[]{:S(2)}) collective-permute-start(bf16[64,512]{1,0:T(8,128)(2,1)S(1)} %get-tuple-element.31), channel_id=1, source_target_pairs={{3,0},{0,1},{1,2},{2,3},{7,4},{4,5},{5,6},{6,7},{11,8},{8,9},{9,10... | collective-permute-start | bytes 196616 | tf_op jit(solution)/shard_map/ppermute | solution.py:396
  102.8 19.3 %collective-permute-start.13 = (bf16[64,512]{1,0:T(8,128)(2,1)S(1)}, bf16[64,512]{1,0:T(8,128)(2,1)S(1)}, u32[]{:S(2)}, u32[]{:S(2)}) collective-permute-start(bf16[64,512]{1,0:T(8,128)(2,1)S(1)} %get-tuple-element.31), channel_id=1, source_target_pairs={{2,0},{3,1},{0,2},{1,3},{6,4},{7,5},{4,6},{5,7},{10,8},{11,9},{8,1... | collective-permute-start | bytes 196616 | tf_op jit(solution)/shard_map/ppermute | solution.py:396
  104.3 15.3 %collective-permute-start.12 = (bf16[64,512]{1,0:T(8,128)(2,1)S(1)}, bf16[64,512]{1,0:T(8,128)(2,1)S(1)}, u32[]{:S(2)}, u32[]{:S(2)}) collective-permute-start(bf16[64,512]{1,0:T(8,128)(2,1)S(1)} %get-tuple-element.31), channel_id=1, source_target_pairs={{1,0},{2,1},{3,2},{0,3},{5,4},{6,5},{7,6},{4,7},{9,8},{10,9},{11,1... | collective-permute-start | bytes 196616 | tf_op jit(solution)/shard_map/ppermute | solution.py:396
  105.7 10.9 %collective-permute-start.20 = (bf16[64,512]{1,0:T(8,128)(2,1)S(1)}, bf16[64,512]{1,0:T(8,128)(2,1)S(1)}, u32[]{:S(2)}, u32[]{:S(2)}) collective-permute-start(bf16[64,512]{1,0:T(8,128)(2,1)S(1)} %get-tuple-element.32), channel_id=1, source_target_pairs={{12,0},{13,1},{14,2},{15,3},{0,4},{1,5},{2,6},{3,7},{4,8},{5,9},{6... | collective-permute-start | bytes 196616 | tf_op jit(solution)/shard_map/ppermute | solution.py:396
  106.6 4.3 %collective-permute-start.18 = (bf16[64,512]{1,0:T(8,128)(2,1)S(1)}, bf16[64,512]{1,0:T(8,128)(2,1)S(1)}, u32[]{:S(2)}, u32[]{:S(2)}) collective-permute-start(bf16[64,512]{1,0:T(8,128)(2,1)S(1)} %get-tuple-element.32), channel_id=1, source_target_pairs={{4,0},{5,1},{6,2},{7,3},{8,4},{9,5},{10,6},{11,7},{12,8},{13,9},{1... | collective-permute-start | bytes 196616 | tf_op jit(solution)/shard_map/ppermute | solution.py:396
  110.9 5.8 %collective-permute-start.19 = (bf16[64,512]{1,0:T(8,128)(2,1)S(1)}, bf16[64,512]{1,0:T(8,128)(2,1)S(1)}, u32[]{:S(2)}, u32[]{:S(2)}) collective-permute-start(bf16[64,512]{1,0:T(8,128)(2,1)S(1)} %get-tuple-element.32), channel_id=1, source_target_pairs={{8,0},{9,1},{10,2},{11,3},{12,4},{13,5},{14,6},{15,7},{0,8},{1,9},... | collective-permute-start | bytes 196616 | tf_op jit(solution)/shard_map/ppermute | solution.py:396
  116.7 19.7 %copy-start.4 = (bf16[256,512]{1,0:T(8,128)(2,1)}, bf16[256,512]{1,0:T(8,128)(2,1)S(1)}, u32[]{:S(2)}) copy-start(bf16[256,512]{1,0:T(8,128)(2,1)S(1)} %constant_dynamic-update-slice_fusion.12.refs_4_) | copy-start | bytes 786436
  116.7 12.3 %collective-permute-start.23 = (bf16[256,512]{1,0:T(8,128)(2,1)S(1)}, bf16[256,512]{1,0:T(8,128)(2,1)S(1)}, u32[]{:S(2)}, u32[]{:S(2)}) collective-permute-start(bf16[256,512]{1,0:T(8,128)(2,1)S(1)} %constant_dynamic-update-slice_fusion.12.refs_4_), channel_id=1, source_target_pairs={{3,0},{0,1},{1,2},{2,3},{7,4},{4,5},{5,6},{6,7},{11,8},{8,9},{9,10... | collective-permute-start | bytes 786440 | tf_op jit(solution)/shard_map/ppermute | solution.py:396
  117.3 15.2 %collective-permute-start.22 = (bf16[256,512]{1,0:T(8,128)(2,1)S(1)}, bf16[256,512]{1,0:T(8,128)(2,1)S(1)}, u32[]{:S(2)}, u32[]{:S(2)}) collective-permute-start(bf16[256,512]{1,0:T(8,128)(2,1)S(1)} %constant_dynamic-update-slice_fusion.12.refs_4_), channel_id=1, source_target_pairs={{2,0},{3,1},{0,2},{1,3},{6,4},{7,5},{4,6},{5,7},{10,8},{11,9},{8,1... | collective-permute-start | bytes 786440 | tf_op jit(solution)/shard_map/ppermute | solution.py:396
  119.5 13.0 %collective-permute-start.21 = (bf16[256,512]{1,0:T(8,128)(2,1)S(1)}, bf16[256,512]{1,0:T(8,128)(2,1)S(1)}, u32[]{:S(2)}, u32[]{:S(2)}) collective-permute-start(bf16[256,512]{1,0:T(8,128)(2,1)S(1)} %constant_dynamic-update-slice_fusion.12.refs_4_), channel_id=1, source_target_pairs={{1,0},{2,1},{3,2},{0,3},{5,4},{6,5},{7,6},{4,7},{9,8},{10,9},{11,1... | collective-permute-start | bytes 786440 | tf_op jit(solution)/shard_map/ppermute | solution.py:396
  122.1 14.3 %copy-start.3 = (bf16[256,512]{1,0:T(8,128)(2,1)}, bf16[256,512]{1,0:T(8,128)(2,1)S(1)}, u32[]{:S(2)}) copy-start(bf16[256,512]{1,0:T(8,128)(2,1)S(1)} %constant_dynamic-update-slice_fusion.8.refs_0_) | copy-start | bytes 786436
  122.1 10.4 %collective-permute-start.17 = (bf16[256,512]{1,0:T(8,128)(2,1)S(1)}, bf16[256,512]{1,0:T(8,128)(2,1)S(1)}, u32[]{:S(2)}, u32[]{:S(2)}) collective-permute-start(bf16[256,512]{1,0:T(8,128)(2,1)S(1)} %constant_dynamic-update-slice_fusion.8.refs_0_), channel_id=1, source_target_pairs={{12,0},{13,1},{14,2},{15,3},{0,4},{1,5},{2,6},{3,7},{4,8},{5,9},{6... | collective-permute-start | bytes 786440 | tf_op jit(solution)/shard_map/ppermute | solution.py:396
  123.1 12.1 %collective-permute-start.16 = (bf16[256,512]{1,0:T(8,128)(2,1)S(1)}, bf16[256,512]{1,0:T(8,128)(2,1)S(1)}, u32[]{:S(2)}, u32[]{:S(2)}) collective-permute-start(bf16[256,512]{1,0:T(8,128)(2,1)S(1)} %constant_dynamic-update-slice_fusion.8.refs_0_), channel_id=1, source_target_pairs={{8,0},{9,1},{10,2},{11,3},{12,4},{13,5},{14,6},{15,7},{0,8},{1,9},... | collective-permute-start | bytes 786440 | tf_op jit(solution)/shard_map/ppermute | solution.py:396
  128.9 7.5 %copy-start.7 = (bf16[256,512]{1,0:T(8,128)(2,1)}, bf16[256,512]{1,0:T(8,128)(2,1)S(1)}, u32[]{:S(2)}) copy-start(bf16[256,512]{1,0:T(8,128)(2,1)S(1)} %collective-permute-done.23.refs_7_) | copy-start | bytes 786436
  128.9 7.5 %collective-permute-start.15 = (bf16[256,512]{1,0:T(8,128)(2,1)S(1)}, bf16[256,512]{1,0:T(8,128)(2,1)}, u32[]{:S(2)}, u32[]{:S(2)}) collective-permute-start(bf16[256,512]{1,0:T(8,128)(2,1)S(1)} %constant_dynamic-update-slice_fusion.8.refs_0_), channel_id=1, source_target_pairs={{4,0},{5,1},{6,2},{7,3},{8,4},{9,5},{10,6},{11,7},{12,8},{13,9},{1... | collective-permute-start | bytes 786440 | tf_op jit(solution)/shard_map/ppermute | solution.py:396
  132.5 3.9 %copy-start.8 = (bf16[256,512]{1,0:T(8,128)(2,1)}, bf16[256,512]{1,0:T(8,128)(2,1)S(1)}, u32[]{:S(2)}) copy-start(bf16[256,512]{1,0:T(8,128)(2,1)S(1)} %collective-permute-done.22.refs_6_) | copy-start | bytes 786436
  132.5 3.9 %copy-start.9 = (bf16[256,512]{1,0:T(8,128)(2,1)}, bf16[256,512]{1,0:T(8,128)(2,1)S(1)}, u32[]{:S(2)}) copy-start(bf16[256,512]{1,0:T(8,128)(2,1)S(1)} %collective-permute-done.21.refs_5_) | copy-start | bytes 786436
  132.5 2.7 %copy-start.10 = (bf16[256,512]{1,0:T(8,128)(2,1)}, bf16[256,512]{1,0:T(8,128)(2,1)S(1)}, u32[]{:S(2)}) copy-start(bf16[256,512]{1,0:T(8,128)(2,1)S(1)} %collective-permute-done.17.refs_3_) | copy-start | bytes 786436
  135.2 0.7 copy-start.11
  136.4 1.4 copy-start.2

commit v5 on v4

--- a/solution.py
+++ b/solution.py
@@ -412,8 +412,9 @@
 def exchange(picked, keep, outgoing):
     width = picked.shape[1]
     arrived = lax.all_to_all(picked.reshape(COLS, PAIR, width), "col", 0, 0, tiled=True)
-    arrived, outgoing = lax.optimization_barrier((arrived.reshape(-1, width), outgoing))
-    hubs = spread_hubs(*hub_keep(keep, arrived))
+    first, second = hub_keep(keep, arrived.reshape(-1, width))
+    first, second, outgoing = lax.optimization_barrier((first, second, outgoing))
+    hubs = spread_hubs(first, second)
     halos = lax.all_to_all(outgoing.reshape(ROWS, -1, width), "row", 0, 0, tiled=True)
     return hubs, halos.reshape(-1, width)
 

time: 155 us -> 155 us (level)
  no operation moved by 1% of the time
where the time goes in v5:
time: 155 us; the launch traced here: 154 us
  starting transfers between devices  69.7 us (45%)
  Pallas kernels  52.2 us (34%)
  waiting for transfers between devices  26.6 us (17%)
  local copies, waits for them, and re-layouts  4.8 us (3%)
    ppermute x24, starting transfers between devices, fetch(): return lax.ppermute(array, 'col', pairs)  46.2 us
    pallas_call x2, Pallas kernels, tail_part(): pl.pallas_call(functools.partial(tail_kernel, last), in_specs=in_specs, o...  33.8 us
    ppermute x24, waiting for transfers between devices, fetch(): return lax.ppermute(array, 'col', pairs)  20.1 us
    all_to_all x2, starting transfers between devices, exchange(): lax.all_to_all(picked.reshape(COLS, PAIR, width), 'col', 0, 0, tiled=True)  14.2 us
    pallas_call x2, Pallas kernels, halo_start(): pl.pallas_call(functools.partial(halo_kernel, noted), in_specs=[smem(), s...  12.3 us
    all_to_all x2, starting transfers between devices, exchange(): lax.all_to_all(outgoing.reshape(ROWS, -1, width), 'row', 0, 0, tiled=True)  9.31 us
    all_to_all x2, waiting for transfers between devices, exchange(): lax.all_to_all(picked.reshape(COLS, PAIR, width), 'col', 0, 0, tiled=True)  6.52 us
    pallas_call x1, Pallas kernels, hub_start(): pl.pallas_call(hub_kernel, in_specs=[smem(), vmem(), vmem(), hbm()], out_...  5.48 us
  transfers between devices with their start and end apart: 28, of which 12 were waited for; matrix products, arithmetic and copies ran while one was open for 0% of the time, Pallas kernels for 8%

profile of v5, /device:TPU:6, one launch (start us, length us, event | category | flops | bytes accessed | tf_op | source)
XLA Modules:
  0.0 153.8 jit_solution(10388073539882984738)
XLA Ops:
  0.0 5.5 %hub_start.1 = (bf16[384,512]{1,0:T(8,128)(2,1)}, s32[8,128]{1,0:T(8,128)}, s32[128,1]{1,0:T(8,128)}, s32[16,128]{1,0:T(8,128)}) custom-call(s32[1]{0:T(128)} %bitcast.col_ref, s32[1,2048]{1,0:T(1,128)} %bitcast.34, s32[1,2048]{1,0:T(1,128)} %row_ref.1, bf16[4096,512]{1,0:T(8,128)(2,1)} %refs_12_.1), custom_call_target="tpu_custom_call" | custom-call | flops 1000 | bytes 1000 | tf_op jit(solution)/shard_map/hub_start/pallas_call | solution.py:150
  5.5 8.1 %all-to-all-start = ((bf16[16,24,512]{2,1,0:T(8,128)(2,1)}), bf16[16,24,512]{2,1,0:T(8,128)(2,1)S(1)}, u32[]{:S(2)}, u32[]{:S(2)}) async-start(bf16[16,24,512]{2,1,0:T(8,128)(2,1)} %bitcast.31), calls=%async_computation | async-start | bytes 786432 | tf_op jit(solution)/shard_map/all_to_all | solution.py:414
  13.6 0.6 copy.12
  14.2 6.2 %halo_start.2 = bf16[2176,512]{1,0:T(8,128)(2,1)} custom-call(s32[2048]{0:T(1024)} %bitcast.32, s32[1,8]{1,0:T(1,128)} %count_ref.3, bf16[4096,512]{1,0:T(8,128)(2,1)} %refs_12_.1), custom_call_target="tpu_custom_call" | custom-call | flops 1000 | bytes 1000 | tf_op jit(solution)/shard_map/halo_start/pallas_call | solution.py:228
  20.4 3.2 %all-to-all-done = bf16[16,24,512]{2,1,0:T(8,128)(2,1)S(1)} async-done(((bf16[16,24,512]{2,1,0:T(8,128)(2,1)}), bf16[16,24,512]{2,1,0:T(8,128)(2,1)S(1)}, u32[]{:S(2)}, u32[]{:S(2)}) %all-to-all-start) | async-done | bytes 393248 | tf_op jit(solution)/shard_map/all_to_all | solution.py:414
  23.9 4.8 %all-to-all-start.1 = ((bf16[8,272,512]{2,1,0:T(8,128)(2,1)}), bf16[8,272,512]{2,1,0:T(8,128)(2,1)S(1)}, u32[]{:S(2)}, u32[]{:S(2)}) async-start(bf16[8,272,512]{2,1,0:T(8,128)(2,1)} %bitcast.22), calls=%async_computation.1 | async-start | bytes 4456448 | tf_op jit(solution)/shard_map/all_to_all | solution.py:418
  28.7 0.6 collective-permute-start.2
  29.3 1.5 collective-permute-start.1
  30.7 1.5 collective-permute-start
  32.2 0.6 collective-permute-start.8
  32.8 2.7 %collective-permute-start.6 = (bf16[64,512]{1,0:T(8,128)(2,1)S(1)}, bf16[64,512]{1,0:T(8,128)(2,1)S(1)}, u32[]{:S(2)}, u32[]{:S(2)}) collective-permute-start(bf16[64,512]{1,0:T(8,128)(2,1)S(1)} %get-tuple-element.27), channel_id=1, source_target_pairs={{4,0},{5,1},{6,2},{7,3},{8,4},{9,5},{10,6},{11,7},{12,8},{13,9},{1... | collective-permute-start | bytes 196616 | tf_op jit(solution)/shard_map/ppermute | solution.py:396
  35.4 1.9 %collective-permute-done.6 = bf16[64,512]{1,0:T(8,128)(2,1)S(1)} collective-permute-done((bf16[64,512]{1,0:T(8,128)(2,1)S(1)}, bf16[64,512]{1,0:T(8,128)(2,1)S(1)}, u32[]{:S(2)}, u32[]{:S(2)}) %collective-permute-start.6) | collective-permute-done | bytes 65568 | tf_op jit(solution)/shard_map/ppermute | solution.py:396
  37.3 2.3 %collective-permute-start.7 = (bf16[64,512]{1,0:T(8,128)(2,1)S(1)}, bf16[64,512]{1,0:T(8,128)(2,1)S(1)}, u32[]{:S(2)}, u32[]{:S(2)}) collective-permute-start(bf16[64,512]{1,0:T(8,128)(2,1)S(1)} %get-tuple-element.27), channel_id=1, source_target_pairs={{8,0},{9,1},{10,2},{11,3},{12,4},{13,5},{14,6},{15,7},{0,8},{1,9},... | collective-permute-start | bytes 196616 | tf_op jit(solution)/shard_map/ppermute | solution.py:396
  39.7 3.4 %collective-permute-done.7 = bf16[64,512]{1,0:T(8,128)(2,1)S(1)} collective-permute-done((bf16[64,512]{1,0:T(8,128)(2,1)S(1)}, bf16[64,512]{1,0:T(8,128)(2,1)S(1)}, u32[]{:S(2)}, u32[]{:S(2)}) %collective-permute-start.7) | collective-permute-done | bytes 65568 | tf_op jit(solution)/shard_map/ppermute | solution.py:396
  43.1 0.7 collective-permute-start.11
  43.8 2.2 %collective-permute-start.10 = (bf16[256,512]{1,0:T(8,128)(2,1)S(1)}, bf16[256,512]{1,0:T(8,128)(2,1)S(1)}, u32[]{:S(2)}, u32[]{:S(2)}) collective-permute-start(bf16[256,512]{1,0:T(8,128)(2,1)S(1)} %constant_dynamic-update-slice_fusion.4.refs_4_), channel_id=1, source_target_pairs={{2,0},{3,1},{0,2},{1,3},{6,4},{7,5},{4,6},{5,7},{10,8},{11,9},{8,1... | collective-permute-start | bytes 786440 | tf_op jit(solution)/shard_map/ppermute | solution.py:396
  46.0 2.5 %collective-permute-start.9 = (bf16[256,512]{1,0:T(8,128)(2,1)S(1)}, bf16[256,512]{1,0:T(8,128)(2,1)S(1)}, u32[]{:S(2)}, u32[]{:S(2)}) collective-permute-start(bf16[256,512]{1,0:T(8,128)(2,1)S(1)} %constant_dynamic-update-slice_fusion.4.refs_4_), channel_id=1, source_target_pairs={{1,0},{2,1},{3,2},{0,3},{5,4},{6,5},{7,6},{4,7},{9,8},{10,9},{11,1... | collective-permute-start | bytes 786440 | tf_op jit(solution)/shard_map/ppermute | solution.py:396
  48.6 1.0 collective-permute-start.5
  49.6 4.1 %collective-permute-start.4 = (bf16[256,512]{1,0:T(8,128)(2,1)S(1)}, bf16[256,512]{1,0:T(8,128)(2,1)S(1)}, u32[]{:S(2)}, u32[]{:S(2)}) collective-permute-start(bf16[256,512]{1,0:T(8,128)(2,1)S(1)} %constant_dynamic-update-slice_fusion.refs_0_), channel_id=1, source_target_pairs={{8,0},{9,1},{10,2},{11,3},{12,4},{13,5},{14,6},{15,7},{0,8},{1,9},... | collective-permute-start | bytes 786440 | tf_op jit(solution)/shard_map/ppermute | solution.py:396
  53.7 1.6 %collective-permute-done.11.refs_7_ = bf16[256,512]{1,0:T(8,128)(2,1)S(1)} collective-permute-done((bf16[256,512]{1,0:T(8,128)(2,1)S(1)}, bf16[256,512]{1,0:T(8,128)(2,1)S(1)}, u32[]{:S(2)}, u32[]{:S(2)}) %collective-permute-start.11) | collective-permute-done | bytes 262176 | tf_op jit(solution)/shard_map/ppermute | solution.py:396
  55.3 3.5 %collective-permute-start.3 = (bf16[256,512]{1,0:T(8,128)(2,1)S(1)}, bf16[256,512]{1,0:T(8,128)(2,1)}, u32[]{:S(2)}, u32[]{:S(2)}) collective-permute-start(bf16[256,512]{1,0:T(8,128)(2,1)S(1)} %constant_dynamic-update-slice_fusion.refs_0_), channel_id=1, source_target_pairs={{4,0},{5,1},{6,2},{7,3},{8,4},{9,5},{10,6},{11,7},{12,8},{13,9},{1... | collective-permute-start | bytes 786440 | tf_op jit(solution)/shard_map/ppermute | solution.py:396
  58.9 2.8 %collective-permute-done.4.refs_2_ = bf16[256,512]{1,0:T(8,128)(2,1)S(1)} collective-permute-done((bf16[256,512]{1,0:T(8,128)(2,1)S(1)}, bf16[256,512]{1,0:T(8,128)(2,1)S(1)}, u32[]{:S(2)}, u32[]{:S(2)}) %collective-permute-start.4) | collective-permute-done | bytes 262176 | tf_op jit(solution)/shard_map/ppermute | solution.py:396
  61.7 0.7 copy-done.16
  62.7 1.3 copy-done.1
  64.1 17.6 %tail_part.2 = (bf16[4096,512]{1,0:T(8,128)(2,1)}, bf16[384,512]{1,0:T(8,128)(2,1)}, f32[16,128]{1,0:T(8,128)}) custom-call(bf16[256,512]{1,0:T(8,128)(2,1)} %copy-done.5, bf16[256,512]{1,0:T(8,128)(2,1)} %collective-permute-done.3.refs_1_, bf16[256,512]{1,0:T(8,128)(2,1)} %copy-done.16, bf16[256,512]{1,0:T(8,128)(2,1)} %copy-done.15, ...), custom_call_target="tpu_custom_call" | custom-call | flops 1000 | bytes 1000 | tf_op jit(solution)/shard_map/tail_part/pallas_call | solution.py:380
  81.7 6.1 %all-to-all-start.2 = ((bf16[16,24,512]{2,1,0:T(8,128)(2,1)}), bf16[16,24,512]{2,1,0:T(8,128)(2,1)S(1)}, u32[]{:S(2)}, u32[]{:S(2)}) async-start(bf16[16,24,512]{2,1,0:T(8,128)(2,1)} %bitcast.30), calls=%async_computation.2 | async-start | bytes 786432 | tf_op jit(solution)/shard_map/all_to_all | solution.py:414
  87.8 6.1 %halo_start.3 = bf16[2048,512]{1,0:T(8,128)(2,1)} custom-call(s32[2048]{0:T(1024)} %bitcast.33, s32[1,8]{1,0:T(1,128)} %count_ref.3, bf16[4096,512]{1,0:T(8,128)(2,1)} %get-tuple-element.34.table_ref.refs_12_), custom_call_target="tpu_custom_call" | custom-call | flops 1000 | bytes 1000 | tf_op jit(solution)/shard_map/halo_start/pallas_call | solution.py:228
  93.9 3.3 %all-to-all-done.2 = bf16[16,24,512]{2,1,0:T(8,128)(2,1)S(1)} async-done(((bf16[16,24,512]{2,1,0:T(8,128)(2,1)}), bf16[16,24,512]{2,1,0:T(8,128)(2,1)S(1)}, u32[]{:S(2)}, u32[]{:S(2)}) %all-to-all-start.2) | async-done | bytes 393248 | tf_op jit(solution)/shard_map/all_to_all | solution.py:414
  97.5 4.5 %all-to-all-start.3 = ((bf16[8,256,512]{2,1,0:T(8,128)(2,1)}), bf16[8,256,512]{2,1,0:T(8,128)(2,1)S(1)}, u32[]{:S(2)}, u32[]{:S(2)}) async-start(bf16[8,256,512]{2,1,0:T(8,128)(2,1)} %bitcast.24), calls=%async_computation.3 | async-start | bytes 4194304 | tf_op jit(solution)/shard_map/all_to_all | solution.py:418
  102.0 0.6 collective-permute-start.14
  102.5 1.5 collective-permute-start.13
  104.0 1.5 collective-permute-start.12
  105.5 0.6 collective-permute-start.20
  106.0 2.7 %collective-permute-start.18 = (bf16[64,512]{1,0:T(8,128)(2,1)S(1)}, bf16[64,512]{1,0:T(8,128)(2,1)S(1)}, u32[]{:S(2)}, u32[]{:S(2)}) collective-permute-start(bf16[64,512]{1,0:T(8,128)(2,1)S(1)} %get-tuple-element.36), channel_id=1, source_target_pairs={{4,0},{5,1},{6,2},{7,3},{8,4},{9,5},{10,6},{11,7},{12,8},{13,9},{1... | collective-permute-start | bytes 196616 | tf_op jit(solution)/shard_map/ppermute | solution.py:396
  108.7 1.9 %collective-permute-done.18 = bf16[64,512]{1,0:T(8,128)(2,1)S(1)} collective-permute-done((bf16[64,512]{1,0:T(8,128)(2,1)S(1)}, bf16[64,512]{1,0:T(8,128)(2,1)S(1)}, u32[]{:S(2)}, u32[]{:S(2)}) %collective-permute-start.18) | collective-permute-done | bytes 65568 | tf_op jit(solution)/shard_map/ppermute | solution.py:396
  110.6 2.5 %collective-permute-start.19 = (bf16[64,512]{1,0:T(8,128)(2,1)S(1)}, bf16[64,512]{1,0:T(8,128)(2,1)S(1)}, u32[]{:S(2)}, u32[]{:S(2)}) collective-permute-start(bf16[64,512]{1,0:T(8,128)(2,1)S(1)} %get-tuple-element.36), channel_id=1, source_target_pairs={{8,0},{9,1},{10,2},{11,3},{12,4},{13,5},{14,6},{15,7},{0,8},{1,9},... | collective-permute-start | bytes 196616 | tf_op jit(solution)/shard_map/ppermute | solution.py:396
  113.1 3.2 %collective-permute-done.19 = bf16[64,512]{1,0:T(8,128)(2,1)S(1)} collective-permute-done((bf16[64,512]{1,0:T(8,128)(2,1)S(1)}, bf16[64,512]{1,0:T(8,128)(2,1)S(1)}, u32[]{:S(2)}, u32[]{:S(2)}) %collective-permute-start.19) | collective-permute-done | bytes 65568 | tf_op jit(solution)/shard_map/ppermute | solution.py:396
  116.4 0.7 collective-permute-start.23
  117.1 2.2 %collective-permute-start.22 = (bf16[256,512]{1,0:T(8,128)(2,1)S(1)}, bf16[256,512]{1,0:T(8,128)(2,1)S(1)}, u32[]{:S(2)}, u32[]{:S(2)}) collective-permute-start(bf16[256,512]{1,0:T(8,128)(2,1)S(1)} %constant_dynamic-update-slice_fusion.12.refs_4_), channel_id=1, source_target_pairs={{2,0},{3,1},{0,2},{1,3},{6,4},{7,5},{4,6},{5,7},{10,8},{11,9},{8,1... | collective-permute-start | bytes 786440 | tf_op jit(solution)/shard_map/ppermute | solution.py:396
  119.3 2.5 %collective-permute-start.21 = (bf16[256,512]{1,0:T(8,128)(2,1)S(1)}, bf16[256,512]{1,0:T(8,128)(2,1)S(1)}, u32[]{:S(2)}, u32[]{:S(2)}) collective-permute-start(bf16[256,512]{1,0:T(8,128)(2,1)S(1)} %constant_dynamic-update-slice_fusion.12.refs_4_), channel_id=1, source_target_pairs={{1,0},{2,1},{3,2},{0,3},{5,4},{6,5},{7,6},{4,7},{9,8},{10,9},{11,1... | collective-permute-start | bytes 786440 | tf_op jit(solution)/shard_map/ppermute | solution.py:396
  121.9 1.0 collective-permute-start.17
  122.8 4.1 %collective-permute-start.16 = (bf16[256,512]{1,0:T(8,128)(2,1)S(1)}, bf16[256,512]{1,0:T(8,128)(2,1)S(1)}, u32[]{:S(2)}, u32[]{:S(2)}) collective-permute-start(bf16[256,512]{1,0:T(8,128)(2,1)S(1)} %constant_dynamic-update-slice_fusion.8.refs_0_), channel_id=1, source_target_pairs={{8,0},{9,1},{10,2},{11,3},{12,4},{13,5},{14,6},{15,7},{0,8},{1,9},... | collective-permute-start | bytes 786440 | tf_op jit(solution)/shard_map/ppermute | solution.py:396
  127.0 1.6 %collective-permute-done.23.refs_7_ = bf16[256,512]{1,0:T(8,128)(2,1)S(1)} collective-permute-done((bf16[256,512]{1,0:T(8,128)(2,1)S(1)}, bf16[256,512]{1,0:T(8,128)(2,1)S(1)}, u32[]{:S(2)}, u32[]{:S(2)}) %collective-permute-start.23) | collective-permute-done | bytes 262176 | tf_op jit(solution)/shard_map/ppermute | solution.py:396
  128.6 3.5 %collective-permute-start.15 = (bf16[256,512]{1,0:T(8,128)(2,1)S(1)}, bf16[256,512]{1,0:T(8,128)(2,1)}, u32[]{:S(2)}, u32[]{:S(2)}) collective-permute-start(bf16[256,512]{1,0:T(8,128)(2,1)S(1)} %constant_dynamic-update-slice_fusion.8.refs_0_), channel_id=1, source_target_pairs={{4,0},{5,1},{6,2},{7,3},{8,4},{9,5},{10,6},{11,7},{12,8},{13,9},{1... | collective-permute-start | bytes 786440 | tf_op jit(solution)/shard_map/ppermute | solution.py:396
  132.1 2.8 %collective-permute-done.16.refs_2_ = bf16[256,512]{1,0:T(8,128)(2,1)S(1)} collective-permute-done((bf16[256,512]{1,0:T(8,128)(2,1)S(1)}, bf16[256,512]{1,0:T(8,128)(2,1)S(1)}, u32[]{:S(2)}, u32[]{:S(2)}) %collective-permute-start.16) | collective-permute-done | bytes 262176 | tf_op jit(solution)/shard_map/ppermute | solution.py:396
  135.0 0.7 copy-done.11
  136.0 1.3 copy-done.2
  137.3 16.3 %tail_part.3 = bf16[4096,512]{1,0:T(8,128)(2,1)} custom-call(bf16[256,512]{1,0:T(8,128)(2,1)} %copy-done.3, bf16[256,512]{1,0:T(8,128)(2,1)} %collective-permute-done.15.refs_1_, bf16[256,512]{1,0:T(8,128)(2,1)} %copy-done.11, bf16[256,512]{1,0:T(8,128)(2,1)} %copy-done.10, bf16[256,512]{1,0:T(8,128)(2,1)} %copy-done.4, bf16[256,512]{1,0:T(8,128)(2,1)} %copy-done.9, ...), custom_call_target="tpu_custom_call" | custom-call | flops 1000 | bytes 1000 | tf_op jit(solution)/shard_map/tail_part/pallas_call | solution.py:380
  (68 shorter events, 1.4 us)
Async XLA Ops:
  0.0 13.6 %copy-start.17 = (s32[1,8,256]{2,1,0:T(8,128)S(1)}, s32[1,8,256]{2,1,0:T(8,128)}, u32[]{:S(2)}) copy-start(s32[1,8,256]{2,1,0:T(8,128)} %param.14) | copy-start | bytes 24580
  5.5 18.2 %all-to-all-start = ((bf16[16,24,512]{2,1,0:T(8,128)(2,1)}), bf16[16,24,512]{2,1,0:T(8,128)(2,1)S(1)}, u32[]{:S(2)}, u32[]{:S(2)}) async-start(bf16[16,24,512]{2,1,0:T(8,128)(2,1)} %bitcast.31), calls=%async_computation | async-start | bytes 786432 | tf_op jit(solution)/shard_map/all_to_all | solution.py:414
  14.2 9.5 %copy-start = (s32[128,1]{1,0:T(8,128)S(1)}, s32[128,1]{1,0:T(8,128)}, u32[]{:S(2)}) copy-start(s32[128,1]{1,0:T(8,128)} %get-tuple-element.22.keep_ref) | copy-start | bytes 1540
  23.9 38.8 %all-to-all-start.1 = ((bf16[8,272,512]{2,1,0:T(8,128)(2,1)}), bf16[8,272,512]{2,1,0:T(8,128)(2,1)S(1)}, u32[]{:S(2)}, u32[]{:S(2)}) async-start(bf16[8,272,512]{2,1,0:T(8,128)(2,1)} %bitcast.22), calls=%async_computation.1 | async-start | bytes 4456448 | tf_op jit(solution)/shard_map/all_to_all | solution.py:418
  28.7 19.8 %collective-permute-start.2 = (bf16[64,512]{1,0:T(8,128)(2,1)S(1)}, bf16[64,512]{1,0:T(8,128)(2,1)S(1)}, u32[]{:S(2)}, u32[]{:S(2)}) collective-permute-start(bf16[64,512]{1,0:T(8,128)(2,1)S(1)} %get-tuple-element.26), channel_id=1, source_target_pairs={{3,0},{0,1},{1,2},{2,3},{7,4},{4,5},{5,6},{6,7},{11,8},{8,9},{9,10... | collective-permute-start | bytes 196616 | tf_op jit(solution)/shard_map/ppermute | solution.py:396
  29.3 19.3 %collective-permute-start.1 = (bf16[64,512]{1,0:T(8,128)(2,1)S(1)}, bf16[64,512]{1,0:T(8,128)(2,1)S(1)}, u32[]{:S(2)}, u32[]{:S(2)}) collective-permute-start(bf16[64,512]{1,0:T(8,128)(2,1)S(1)} %get-tuple-element.26), channel_id=1, source_target_pairs={{2,0},{3,1},{0,2},{1,3},{6,4},{7,5},{4,6},{5,7},{10,8},{11,9},{8,1... | collective-permute-start | bytes 196616 | tf_op jit(solution)/shard_map/ppermute | solution.py:396
  30.7 15.3 %collective-permute-start = (bf16[64,512]{1,0:T(8,128)(2,1)S(1)}, bf16[64,512]{1,0:T(8,128)(2,1)S(1)}, u32[]{:S(2)}, u32[]{:S(2)}) collective-permute-start(bf16[64,512]{1,0:T(8,128)(2,1)S(1)} %get-tuple-element.26), channel_id=1, source_target_pairs={{1,0},{2,1},{3,2},{0,3},{5,4},{6,5},{7,6},{4,7},{9,8},{10,9},{11,1... | collective-permute-start | bytes 196616 | tf_op jit(solution)/shard_map/ppermute | solution.py:396
  32.2 10.9 %collective-permute-start.8 = (bf16[64,512]{1,0:T(8,128)(2,1)S(1)}, bf16[64,512]{1,0:T(8,128)(2,1)S(1)}, u32[]{:S(2)}, u32[]{:S(2)}) collective-permute-start(bf16[64,512]{1,0:T(8,128)(2,1)S(1)} %get-tuple-element.27), channel_id=1, source_target_pairs={{12,0},{13,1},{14,2},{15,3},{0,4},{1,5},{2,6},{3,7},{4,8},{5,9},{6... | collective-permute-start | bytes 196616 | tf_op jit(solution)/shard_map/ppermute | solution.py:396
  32.8 4.6 %collective-permute-start.6 = (bf16[64,512]{1,0:T(8,128)(2,1)S(1)}, bf16[64,512]{1,0:T(8,128)(2,1)S(1)}, u32[]{:S(2)}, u32[]{:S(2)}) collective-permute-start(bf16[64,512]{1,0:T(8,128)(2,1)S(1)} %get-tuple-element.27), channel_id=1, source_target_pairs={{4,0},{5,1},{6,2},{7,3},{8,4},{9,5},{10,6},{11,7},{12,8},{13,9},{1... | collective-permute-start | bytes 196616 | tf_op jit(solution)/shard_map/ppermute | solution.py:396
  37.3 5.8 %collective-permute-start.7 = (bf16[64,512]{1,0:T(8,128)(2,1)S(1)}, bf16[64,512]{1,0:T(8,128)(2,1)S(1)}, u32[]{:S(2)}, u32[]{:S(2)}) collective-permute-start(bf16[64,512]{1,0:T(8,128)(2,1)S(1)} %get-tuple-element.27), channel_id=1, source_target_pairs={{8,0},{9,1},{10,2},{11,3},{12,4},{13,5},{14,6},{15,7},{0,8},{1,9},... | collective-permute-start | bytes 196616 | tf_op jit(solution)/shard_map/ppermute | solution.py:396
  43.1 19.6 %copy-start.6 = (bf16[256,512]{1,0:T(8,128)(2,1)}, bf16[256,512]{1,0:T(8,128)(2,1)S(1)}, u32[]{:S(2)}) copy-start(bf16[256,512]{1,0:T(8,128)(2,1)S(1)} %constant_dynamic-update-slice_fusion.4.refs_4_) | copy-start | bytes 786436
  43.1 12.2 %collective-permute-start.11 = (bf16[256,512]{1,0:T(8,128)(2,1)S(1)}, bf16[256,512]{1,0:T(8,128)(2,1)S(1)}, u32[]{:S(2)}, u32[]{:S(2)}) collective-permute-start(bf16[256,512]{1,0:T(8,128)(2,1)S(1)} %constant_dynamic-update-slice_fusion.4.refs_4_), channel_id=1, source_target_pairs={{3,0},{0,1},{1,2},{2,3},{7,4},{4,5},{5,6},{6,7},{11,8},{8,9},{9,10... | collective-permute-start | bytes 786440 | tf_op jit(solution)/shard_map/ppermute | solution.py:396
  43.8 15.0 %collective-permute-start.10 = (bf16[256,512]{1,0:T(8,128)(2,1)S(1)}, bf16[256,512]{1,0:T(8,128)(2,1)S(1)}, u32[]{:S(2)}, u32[]{:S(2)}) collective-permute-start(bf16[256,512]{1,0:T(8,128)(2,1)S(1)} %constant_dynamic-update-slice_fusion.4.refs_4_), channel_id=1, source_target_pairs={{2,0},{3,1},{0,2},{1,3},{6,4},{7,5},{4,6},{5,7},{10,8},{11,9},{8,1... | collective-permute-start | bytes 786440 | tf_op jit(solution)/shard_map/ppermute | solution.py:396
  46.0 12.8 %collective-permute-start.9 = (bf16[256,512]{1,0:T(8,128)(2,1)S(1)}, bf16[256,512]{1,0:T(8,128)(2,1)S(1)}, u32[]{:S(2)}, u32[]{:S(2)}) collective-permute-start(bf16[256,512]{1,0:T(8,128)(2,1)S(1)} %constant_dynamic-update-slice_fusion.4.refs_4_), channel_id=1, source_target_pairs={{1,0},{2,1},{3,2},{0,3},{5,4},{6,5},{7,6},{4,7},{9,8},{10,9},{11,1... | collective-permute-start | bytes 786440 | tf_op jit(solution)/shard_map/ppermute | solution.py:396
  48.6 14.1 %copy-start.5 = (bf16[256,512]{1,0:T(8,128)(2,1)}, bf16[256,512]{1,0:T(8,128)(2,1)S(1)}, u32[]{:S(2)}) copy-start(bf16[256,512]{1,0:T(8,128)(2,1)S(1)} %constant_dynamic-update-slice_fusion.refs_0_) | copy-start | bytes 786436
  48.6 10.3 %collective-permute-start.5 = (bf16[256,512]{1,0:T(8,128)(2,1)S(1)}, bf16[256,512]{1,0:T(8,128)(2,1)S(1)}, u32[]{:S(2)}, u32[]{:S(2)}) collective-permute-start(bf16[256,512]{1,0:T(8,128)(2,1)S(1)} %constant_dynamic-update-slice_fusion.refs_0_), channel_id=1, source_target_pairs={{12,0},{13,1},{14,2},{15,3},{0,4},{1,5},{2,6},{3,7},{4,8},{5,9},{6... | collective-permute-start | bytes 786440 | tf_op jit(solution)/shard_map/ppermute | solution.py:396
  49.6 12.1 %collective-permute-start.4 = (bf16[256,512]{1,0:T(8,128)(2,1)S(1)}, bf16[256,512]{1,0:T(8,128)(2,1)S(1)}, u32[]{:S(2)}, u32[]{:S(2)}) collective-permute-start(bf16[256,512]{1,0:T(8,128)(2,1)S(1)} %constant_dynamic-update-slice_fusion.refs_0_), channel_id=1, source_target_pairs={{8,0},{9,1},{10,2},{11,3},{12,4},{13,5},{14,6},{15,7},{0,8},{1,9},... | collective-permute-start | bytes 786440 | tf_op jit(solution)/shard_map/ppermute | solution.py:396
  55.3 7.4 %copy-start.12 = (bf16[256,512]{1,0:T(8,128)(2,1)}, bf16[256,512]{1,0:T(8,128)(2,1)S(1)}, u32[]{:S(2)}) copy-start(bf16[256,512]{1,0:T(8,128)(2,1)S(1)} %collective-permute-done.11.refs_7_) | copy-start | bytes 786436
  55.3 7.4 %collective-permute-start.3 = (bf16[256,512]{1,0:T(8,128)(2,1)S(1)}, bf16[256,512]{1,0:T(8,128)(2,1)}, u32[]{:S(2)}, u32[]{:S(2)}) collective-permute-start(bf16[256,512]{1,0:T(8,128)(2,1)S(1)} %constant_dynamic-update-slice_fusion.refs_0_), channel_id=1, source_target_pairs={{4,0},{5,1},{6,2},{7,3},{8,4},{9,5},{10,6},{11,7},{12,8},{13,9},{1... | collective-permute-start | bytes 786440 | tf_op jit(solution)/shard_map/ppermute | solution.py:396
  58.8 3.9 %copy-start.13 = (bf16[256,512]{1,0:T(8,128)(2,1)}, bf16[256,512]{1,0:T(8,128)(2,1)S(1)}, u32[]{:S(2)}) copy-start(bf16[256,512]{1,0:T(8,128)(2,1)S(1)} %collective-permute-done.10.refs_6_) | copy-start | bytes 786436
  58.8 2.9 %copy-start.14 = (bf16[256,512]{1,0:T(8,128)(2,1)}, bf16[256,512]{1,0:T(8,128)(2,1)S(1)}, u32[]{:S(2)}) copy-start(bf16[256,512]{1,0:T(8,128)(2,1)S(1)} %collective-permute-done.9.refs_5_) | copy-start | bytes 786436
  58.9 2.8 %copy-start.15 = (bf16[256,512]{1,0:T(8,128)(2,1)}, bf16[256,512]{1,0:T(8,128)(2,1)S(1)}, u32[]{:S(2)}) copy-start(bf16[256,512]{1,0:T(8,128)(2,1)S(1)} %collective-permute-done.5.refs_3_) | copy-start | bytes 786436
  61.7 0.7 copy-start.16
  62.7 1.4 copy-start.1
  81.7 15.5 %all-to-all-start.2 = ((bf16[16,24,512]{2,1,0:T(8,128)(2,1)}), bf16[16,24,512]{2,1,0:T(8,128)(2,1)S(1)}, u32[]{:S(2)}, u32[]{:S(2)}) async-start(bf16[16,24,512]{2,1,0:T(8,128)(2,1)} %bitcast.30), calls=%async_computation.2 | async-start | bytes 786432 | tf_op jit(solution)/shard_map/all_to_all | solution.py:414
  97.5 38.5 %all-to-all-start.3 = ((bf16[8,256,512]{2,1,0:T(8,128)(2,1)}), bf16[8,256,512]{2,1,0:T(8,128)(2,1)S(1)}, u32[]{:S(2)}, u32[]{:S(2)}) async-start(bf16[8,256,512]{2,1,0:T(8,128)(2,1)} %bitcast.24), calls=%async_computation.3 | async-start | bytes 4194304 | tf_op jit(solution)/shard_map/all_to_all | solution.py:418
  102.0 19.8 %collective-permute-start.14 = (bf16[64,512]{1,0:T(8,128)(2,1)S(1)}, bf16[64,512]{1,0:T(8,128)(2,1)S(1)}, u32[]{:S(2)}, u32[]{:S(2)}) collective-permute-start(bf16[64,512]{1,0:T(8,128)(2,1)S(1)} %get-tuple-element.35), channel_id=1, source_target_pairs={{3,0},{0,1},{1,2},{2,3},{7,4},{4,5},{5,6},{6,7},{11,8},{8,9},{9,10... | collective-permute-start | bytes 196616 | tf_op jit(solution)/shard_map/ppermute | solution.py:396
  102.5 19.3 %collective-permute-start.13 = (bf16[64,512]{1,0:T(8,128)(2,1)S(1)}, bf16[64,512]{1,0:T(8,128)(2,1)S(1)}, u32[]{:S(2)}, u32[]{:S(2)}) collective-permute-start(bf16[64,512]{1,0:T(8,128)(2,1)S(1)} %get-tuple-element.35), channel_id=1, source_target_pairs={{2,0},{3,1},{0,2},{1,3},{6,4},{7,5},{4,6},{5,7},{10,8},{11,9},{8,1... | collective-permute-start | bytes 196616 | tf_op jit(solution)/shard_map/ppermute | solution.py:396
  104.0 15.3 %collective-permute-start.12 = (bf16[64,512]{1,0:T(8,128)(2,1)S(1)}, bf16[64,512]{1,0:T(8,128)(2,1)S(1)}, u32[]{:S(2)}, u32[]{:S(2)}) collective-permute-start(bf16[64,512]{1,0:T(8,128)(2,1)S(1)} %get-tuple-element.35), channel_id=1, source_target_pairs={{1,0},{2,1},{3,2},{0,3},{5,4},{6,5},{7,6},{4,7},{9,8},{10,9},{11,1... | collective-permute-start | bytes 196616 | tf_op jit(solution)/shard_map/ppermute | solution.py:396
  105.5 10.9 %collective-permute-start.20 = (bf16[64,512]{1,0:T(8,128)(2,1)S(1)}, bf16[64,512]{1,0:T(8,128)(2,1)S(1)}, u32[]{:S(2)}, u32[]{:S(2)}) collective-permute-start(bf16[64,512]{1,0:T(8,128)(2,1)S(1)} %get-tuple-element.36), channel_id=1, source_target_pairs={{12,0},{13,1},{14,2},{15,3},{0,4},{1,5},{2,6},{3,7},{4,8},{5,9},{6... | collective-permute-start | bytes 196616 | tf_op jit(solution)/shard_map/ppermute | solution.py:396
  106.0 4.6 %collective-permute-start.18 = (bf16[64,512]{1,0:T(8,128)(2,1)S(1)}, bf16[64,512]{1,0:T(8,128)(2,1)S(1)}, u32[]{:S(2)}, u32[]{:S(2)}) collective-permute-start(bf16[64,512]{1,0:T(8,128)(2,1)S(1)} %get-tuple-element.36), channel_id=1, source_target_pairs={{4,0},{5,1},{6,2},{7,3},{8,4},{9,5},{10,6},{11,7},{12,8},{13,9},{1... | collective-permute-start | bytes 196616 | tf_op jit(solution)/shard_map/ppermute | solution.py:396
  110.6 5.8 %collective-permute-start.19 = (bf16[64,512]{1,0:T(8,128)(2,1)S(1)}, bf16[64,512]{1,0:T(8,128)(2,1)S(1)}, u32[]{:S(2)}, u32[]{:S(2)}) collective-permute-start(bf16[64,512]{1,0:T(8,128)(2,1)S(1)} %get-tuple-element.36), channel_id=1, source_target_pairs={{8,0},{9,1},{10,2},{11,3},{12,4},{13,5},{14,6},{15,7},{0,8},{1,9},... | collective-permute-start | bytes 196616 | tf_op jit(solution)/shard_map/ppermute | solution.py:396
  116.4 19.6 %copy-start.4 = (bf16[256,512]{1,0:T(8,128)(2,1)}, bf16[256,512]{1,0:T(8,128)(2,1)S(1)}, u32[]{:S(2)}) copy-start(bf16[256,512]{1,0:T(8,128)(2,1)S(1)} %constant_dynamic-update-slice_fusion.12.refs_4_) | copy-start | bytes 786436
  116.4 12.2 %collective-permute-start.23 = (bf16[256,512]{1,0:T(8,128)(2,1)S(1)}, bf16[256,512]{1,0:T(8,128)(2,1)S(1)}, u32[]{:S(2)}, u32[]{:S(2)}) collective-permute-start(bf16[256,512]{1,0:T(8,128)(2,1)S(1)} %constant_dynamic-update-slice_fusion.12.refs_4_), channel_id=1, source_target_pairs={{3,0},{0,1},{1,2},{2,3},{7,4},{4,5},{5,6},{6,7},{11,8},{8,9},{9,10... | collective-permute-start | bytes 786440 | tf_op jit(solution)/shard_map/ppermute | solution.py:396
  117.1 15.0 %collective-permute-start.22 = (bf16[256,512]{1,0:T(8,128)(2,1)S(1)}, bf16[256,512]{1,0:T(8,128)(2,1)S(1)}, u32[]{:S(2)}, u32[]{:S(2)}) collective-permute-start(bf16[256,512]{1,0:T(8,128)(2,1)S(1)} %constant_dynamic-update-slice_fusion.12.refs_4_), channel_id=1, source_target_pairs={{2,0},{3,1},{0,2},{1,3},{6,4},{7,5},{4,6},{5,7},{10,8},{11,9},{8,1... | collective-permute-start | bytes 786440 | tf_op jit(solution)/shard_map/ppermute | solution.py:396
  119.3 12.8 %collective-permute-start.21 = (bf16[256,512]{1,0:T(8,128)(2,1)S(1)}, bf16[256,512]{1,0:T(8,128)(2,1)S(1)}, u32[]{:S(2)}, u32[]{:S(2)}) collective-permute-start(bf16[256,512]{1,0:T(8,128)(2,1)S(1)} %constant_dynamic-update-slice_fusion.12.refs_4_), channel_id=1, source_target_pairs={{1,0},{2,1},{3,2},{0,3},{5,4},{6,5},{7,6},{4,7},{9,8},{10,9},{11,1... | collective-permute-start | bytes 786440 | tf_op jit(solution)/shard_map/ppermute | solution.py:396
  121.9 14.1 %copy-start.3 = (bf16[256,512]{1,0:T(8,128)(2,1)}, bf16[256,512]{1,0:T(8,128)(2,1)S(1)}, u32[]{:S(2)}) copy-start(bf16[256,512]{1,0:T(8,128)(2,1)S(1)} %constant_dynamic-update-slice_fusion.8.refs_0_) | copy-start | bytes 786436
  121.9 10.3 %collective-permute-start.17 = (bf16[256,512]{1,0:T(8,128)(2,1)S(1)}, bf16[256,512]{1,0:T(8,128)(2,1)S(1)}, u32[]{:S(2)}, u32[]{:S(2)}) collective-permute-start(bf16[256,512]{1,0:T(8,128)(2,1)S(1)} %constant_dynamic-update-slice_fusion.8.refs_0_), channel_id=1, source_target_pairs={{12,0},{13,1},{14,2},{15,3},{0,4},{1,5},{2,6},{3,7},{4,8},{5,9},{6... | collective-permute-start | bytes 786440 | tf_op jit(solution)/shard_map/ppermute | solution.py:396
  122.8 12.1 %collective-permute-start.16 = (bf16[256,512]{1,0:T(8,128)(2,1)S(1)}, bf16[256,512]{1,0:T(8,128)(2,1)S(1)}, u32[]{:S(2)}, u32[]{:S(2)}) collective-permute-start(bf16[256,512]{1,0:T(8,128)(2,1)S(1)} %constant_dynamic-update-slice_fusion.8.refs_0_), channel_id=1, source_target_pairs={{8,0},{9,1},{10,2},{11,3},{12,4},{13,5},{14,6},{15,7},{0,8},{1,9},... | collective-permute-start | bytes 786440 | tf_op jit(solution)/shard_map/ppermute | solution.py:396
  128.6 7.4 %copy-start.7 = (bf16[256,512]{1,0:T(8,128)(2,1)}, bf16[256,512]{1,0:T(8,128)(2,1)S(1)}, u32[]{:S(2)}) copy-start(bf16[256,512]{1,0:T(8,128)(2,1)S(1)} %collective-permute-done.23.refs_7_) | copy-start | bytes 786436
  128.6 7.4 %collective-permute-start.15 = (bf16[256,512]{1,0:T(8,128)(2,1)S(1)}, bf16[256,512]{1,0:T(8,128)(2,1)}, u32[]{:S(2)}, u32[]{:S(2)}) collective-permute-start(bf16[256,512]{1,0:T(8,128)(2,1)S(1)} %constant_dynamic-update-slice_fusion.8.refs_0_), channel_id=1, source_target_pairs={{4,0},{5,1},{6,2},{7,3},{8,4},{9,5},{10,6},{11,7},{12,8},{13,9},{1... | collective-permute-start | bytes 786440 | tf_op jit(solution)/shard_map/ppermute | solution.py:396
  132.1 3.9 %copy-start.8 = (bf16[256,512]{1,0:T(8,128)(2,1)}, bf16[256,512]{1,0:T(8,128)(2,1)S(1)}, u32[]{:S(2)}) copy-start(bf16[256,512]{1,0:T(8,128)(2,1)S(1)} %collective-permute-done.22.refs_6_) | copy-start | bytes 786436
  132.1 3.9 %copy-start.9 = (bf16[256,512]{1,0:T(8,128)(2,1)}, bf16[256,512]{1,0:T(8,128)(2,1)S(1)}, u32[]{:S(2)}) copy-start(bf16[256,512]{1,0:T(8,128)(2,1)S(1)} %collective-permute-done.21.refs_5_) | copy-start | bytes 786436
  132.1 2.8 %copy-start.10 = (bf16[256,512]{1,0:T(8,128)(2,1)}, bf16[256,512]{1,0:T(8,128)(2,1)S(1)}, u32[]{:S(2)}) copy-start(bf16[256,512]{1,0:T(8,128)(2,1)S(1)} %collective-permute-done.17.refs_3_) | copy-start | bytes 786436
  135.0 0.7 copy-start.11
  136.0 1.4 copy-start.2
